TPU v7x, 32 devices: a whole 2x2x4 slice. The times are simulated.
32 devices in a mesh: grp: 8 (over z, y), tp: 4 (over x, core).
Axes of the slice: x: 2, y: 2, z: 4, core: 2. Of those that a mesh axis runs over, the one named last changes fastest.
Arguments:
- gen_noise: bfloat16 [8, 256, 3072], P('grp'), may hold values from -6 to 6
- diff_noise: bfloat16 [8, 256, 3072], P('grp', 'tp'), may hold values from -6 to 6
- timesteps: int32 [8], P('grp'), may hold values from 0 to 15
- gen_mod: float32 [3, 3072], replicated, may hold values from -1 to 1
- teacher_mod: float32 [16, 3, 3072], replicated, may hold values from -1 to 1
- critic_mod: float32 [16, 3, 3072], replicated, may hold values from -1 to 1
- gen_up: bfloat16 [3072, 6144], P('grp', 'tp'), may hold values from -0.109375 to 0.109375
- gen_down: bfloat16 [6144, 3072], P('tp', 'grp'), may hold values from -0.078125 to 0.078125
- teacher_up: bfloat16 [3072, 6144], P(None, 'tp'), may hold values from -0.109375 to 0.109375
- teacher_down: bfloat16 [6144, 3072], P('tp'), may hold values from -0.078125 to 0.078125
- critic_up: bfloat16 [3072, 6144], P(None, 'tp'), may hold values from -0.109375 to 0.109375
- critic_down: bfloat16 [6144, 3072], P('tp'), may hold values from -0.078125 to 0.078125
Outputs:
- generated: bfloat16 [8, 256, 3072], P('grp', 'tp')
- up_grad: float32 [3072, 6144], P('grp', 'tp')
- down_grad: float32 [6144, 3072], P('tp', 'grp')
All inputs are finite; a program needn't handle non-finite values.
Results may differ from a plain program's by a relative error of at most 0.0038.
Values may be sent and summed in bfloat16 or wider, within the bound.
No kernel may reach another device: no remote copies, remote signals or barrier semaphores. Data moves between devices by JAX's collectives and lax.ppermute only.
A program may use at most 192 MiB of HBM per device.

v0:
```python
import jax
import jax.numpy as jnp
from jax import lax
from jax.sharding import PartitionSpec as P

epsilon = 1e-06
root_two_pi = 0.7978845608028654
cubic = 0.044715


def normalize(values):
    center = values - jnp.mean(values, axis=-1, keepdims=True)
    spread = jnp.mean(center * center, axis=-1, keepdims=True)
    return center * lax.rsqrt(spread + epsilon)


def smooth_gate(values):
    inner = root_two_pi * (values + cubic * values * values * values)
    return 0.5 * values * (1.0 + jnp.tanh(inner))


def gate_slope(values):
    inner = root_two_pi * (values + cubic * values * values * values)
    tangent = jnp.tanh(inner)
    return 0.5 * (1.0 + tangent) + 0.5 * values * (1.0 - tangent * tangent) * root_two_pi * (
        1.0 + 3.0 * cubic * values * values
    )


def pick_level(table, step_index):
    levels = lax.broadcasted_iota(jnp.int32, (table.shape[0], 1, 1), 0)
    return jnp.sum(jnp.where(levels == step_index, table, 0.0), axis=0)


def modulate(normed, picked):
    return (normed * (1.0 + picked[1]) + picked[0]).astype(jnp.bfloat16)


def per_device(
    gen_noise,
    diff_noise,
    timesteps,
    gen_mod,
    teacher_mod,
    critic_mod,
    gen_up,
    gen_down,
    teacher_up,
    teacher_down,
    critic_up,
    critic_down,
):
    local_rows = diff_noise.shape[1]
    step_index = timesteps[0]
    noise_all = gen_noise[0].astype(jnp.float32)
    gen_rows = modulate(normalize(noise_all), gen_mod)
    own_start = lax.axis_index("tp") * local_rows
    noise = lax.dynamic_slice_in_dim(noise_all, own_start, local_rows, 0)
    columns = gen_rows
    gen_pre = jnp.dot(
        columns,
        lax.all_gather(gen_up, "grp", axis=0, tiled=True),
        preferred_element_type=jnp.float32,
    )
    gen_hidden = smooth_gate(gen_pre).astype(jnp.bfloat16)
    down_full = lax.all_gather(gen_down, "grp", axis=1, tiled=True)
    picked_rows = gen_hidden
    gen_branch = lax.psum_scatter(
        jnp.dot(picked_rows, down_full, preferred_element_type=jnp.float32),
        "tp",
        scatter_dimension=0,
        tiled=True,
    )
    generated = (noise + gen_mod[2] * gen_branch).astype(jnp.bfloat16)
    level = (step_index.astype(jnp.float32) + 1.0) / (teacher_mod.shape[0] + 1)
    noised = (
        (1.0 - level) * generated.astype(jnp.float32) + level * diff_noise[0].astype(jnp.float32)
    ).astype(jnp.bfloat16)
    teacher_row = pick_level(teacher_mod, step_index)
    critic_row = pick_level(critic_mod, step_index)
    normed = normalize(lax.optimization_barrier(noised).astype(jnp.float32))
    teacher_in, critic_in = (
        lax.all_gather(modulate(normed, teacher_row), "tp", axis=0, tiled=True),
        lax.all_gather(modulate(normed, critic_row), "tp", axis=0, tiled=True),
    )
    teacher_hidden = smooth_gate(
        jnp.dot(teacher_in, teacher_up, preferred_element_type=jnp.float32)
    ).astype(jnp.bfloat16)
    critic_hidden = smooth_gate(
        jnp.dot(critic_in, critic_up, preferred_element_type=jnp.float32)
    ).astype(jnp.bfloat16)
    picked_rows = teacher_hidden
    teacher_branch = lax.psum_scatter(
        jnp.dot(picked_rows, teacher_down, preferred_element_type=jnp.float32),
        "tp",
        scatter_dimension=0,
        tiled=True,
    )
    picked_rows = critic_hidden
    critic_branch = lax.psum_scatter(
        jnp.dot(picked_rows, critic_down, preferred_element_type=jnp.float32),
        "tp",
        scatter_dimension=0,
        tiled=True,
    )
    gap = teacher_row[2] * teacher_branch - critic_row[2] * critic_branch
    branch_grad = (gen_mod[2] * (level * gap)).astype(jnp.bfloat16)
    piece = lax.all_gather(branch_grad, "tp", axis=0, tiled=True)
    down_acc = lax.dot_general(
        gen_hidden, piece, (((0,), (0,)), ((), ())), preferred_element_type=jnp.float32
    )
    hidden_grad = lax.dot_general(
        piece, down_full, (((1,), (1,)), ((), ())), preferred_element_type=jnp.float32
    )
    rows_grad = (hidden_grad * gate_slope(gen_pre)).astype(jnp.bfloat16)
    columns = gen_rows
    up_grad = lax.psum_scatter(
        lax.dot_general(
            columns, rows_grad, (((0,), (0,)), ((), ())), preferred_element_type=jnp.float32
        ),
        "grp",
        scatter_dimension=0,
        tiled=True,
    )
    down_grad = lax.psum_scatter(down_acc, "grp", scatter_dimension=1, tiled=True)
    return (generated[None], up_grad, down_grad)


def solution(mesh):
    in_specs = (
        P("grp", None, None),
        P("grp", "tp", None),
        P("grp"),
        P(),
        P(),
        P(),
        P("grp", "tp"),
        P("tp", "grp"),
        P(None, "tp"),
        P("tp", None),
        P(None, "tp"),
        P("tp", None),
    )
    out_specs = (P("grp", "tp", None), P("grp", "tp"), P("tp", "grp"))
    return jax.shard_map(
        per_device, mesh=mesh, in_specs=in_specs, out_specs=out_specs, check_vma=False
    )
```

profile of v0, /device:TPU:0, one launch (start us, length us, event | category | flops | bytes accessed | tf_op | source)
XLA Modules:
  0.0 1136.3 jit_solution(4494369682792061914)
XLA Ops:
  7.2 0.7 all-gather.6.cloned.1.call-update
  8.0 0.7 all-gather.8.cloned.1.call-update
  9.6 141.3 %all-gather.6.cloned.1.call-done = bf16[3072,1536]{1,0:T(8,128)(2,1)} async-done(((bf16[384,1536]{1,0:T(8,128)(2,1)}), bf16[3072,1536]{1,0:T(8,128)(2,1)}) %all-gather.6.cloned.1.call-update) | async-done | bytes 9437200 | tf_op jit(solution)/shard_map/all_gather | solution.py:62
  151.0 5.5 fusion.60
  156.5 132.9 %all-gather.8.cloned.1.call-done = bf16[1536,3072]{1,0:T(8,128)(2,1)} async-done(((bf16[1536,384]{1,0:T(8,128)(2,1)}), bf16[1536,3072]{1,0:T(8,128)(2,1)}) %all-gather.8.cloned.1.call-update) | async-done | bytes 9437200 | tf_op jit(solution)/shard_map/all_gather | solution.py:66
  289.5 8.2 fusion.59
  297.7 2.0 convert_element_type.49
  300.4 1.9 select_reduce_fusion.1
  302.3 31.6 %reduce-scatter.6.cloned.1.call-done = f32[64,3072]{1,0:T(8,128)} async-done(((f32[256,3072]{1,0:T(8,128)}), f32[64,3072]{1,0:T(8,128)}) %reduce-scatter.6.cloned.1.call-update) | async-done | bytes 786448 | tf_op jit(solution)/shard_map/reduce_scatter | solution.py:68
  333.9 2.4 fusion.30
  336.8 1.2 fusion.22
  338.6 19.2 %all-gather.12.cloned.1.call-done = bf16[256,3072]{1,0:T(8,128)(2,1)} async-done(((bf16[64,3072]{1,0:T(8,128)(2,1)}), bf16[256,3072]{1,0:T(8,128)(2,1)}) %all-gather.12.cloned.1.call-update) | async-done | bytes 1572880 | tf_op jit(solution)/shard_map/all_gather | solution.py:84
  357.8 13.7 %fusion.26 = f32[256,3072]{1,0:T(8,128)} fusion(bf16[1536,3072]{1,0:T(8,128)(2,1)} %param.23, bf16[256,3072]{1,0:T(8,128)(2,1)} %all-gather.12.cloned.1.call-done, bf16[3072,1536]{1,0:T(8,128)(2,1)} %param.22), kind=kOutput, calls=%fused_computation.38 | convolution fusion | flops 4835377152 | bytes 23592960 | tf_op jit(solution)/shard_map/dot_general | solution.py:101
  371.8 7.8 all-gather.10.cloned.1.call-done
  379.5 13.7 %fusion.28 = f32[256,3072]{1,0:T(8,128)} fusion(bf16[1536,3072]{1,0:T(8,128)(2,1)} %param.21, bf16[256,3072]{1,0:T(8,128)(2,1)} %all-gather.10.cloned.1.call-done, bf16[3072,1536]{1,0:T(8,128)(2,1)} %param.20), kind=kOutput, calls=%fused_computation.39 | convolution fusion | flops 4835377152 | bytes 23592960 | tf_op jit(solution)/shard_map/dot_general | solution.py:94
  393.3 26.8 %reduce-scatter.10.cloned.1.call-done = f32[64,3072]{1,0:T(8,128)} async-done(((f32[256,3072]{1,0:T(8,128)}), f32[64,3072]{1,0:T(8,128)}) %reduce-scatter.10.cloned.1.call-update) | async-done | bytes 786448 | tf_op jit(solution)/shard_map/reduce_scatter | solution.py:100
  420.1 40.5 %reduce-scatter.8.cloned.1.call-done = f32[64,3072]{1,0:T(8,128)} async-done(((f32[256,3072]{1,0:T(8,128)}), f32[64,3072]{1,0:T(8,128)}) %reduce-scatter.8.cloned.1.call-update) | async-done | bytes 786448 | tf_op jit(solution)/shard_map/reduce_scatter | solution.py:93
  460.6 2.3 multiply_convert_fusion.1
  463.0 19.8 %all-gather.14.cloned.1.call-done = bf16[256,3072]{1,0:T(8,128)(2,1)} async-done(((bf16[64,3072]{1,0:T(8,128)(2,1)}), bf16[256,3072]{1,0:T(8,128)(2,1)}) %all-gather.14.cloned.1.call-update) | async-done | bytes 1572880 | tf_op jit(solution)/shard_map/all_gather | solution.py:108
  482.7 16.5 %fusion.16 = f32[3072,1536]{1,0:T(8,128)} fusion(bf16[256,3072]{1,0:T(8,128)(2,1)} %all-gather.14.cloned.1.call-done, bf16[1536,3072]{1,0:T(8,128)(2,1)} %all-gather.8.cloned.1.call-done, f32[256,1536]{1,0:T(8,128)S(1)} %fusion.60, bf16[1,256,3072]{2,1,0:T(8,128)(2,1)S(1)} %copy-done, f32[3072]{0:T(1024)S(1)} %bitcast.42, f32[3072]{0:T(1024)S(1)} %bitcast.44, ...), kind=kOutput, calls=%fused_computation.26 | convolution fusion | flops 4844027904 | bytes 33056768 | tf_op jit(solution)/shard_map/dot_general | solution.py:118
  499.3 1.3 copy-done.1
  500.6 8.4 fusion.58
  509.0 303.2 %reduce-scatter.12.cloned.1.call-done = f32[384,1536]{1,0:T(8,128)} async-done(((f32[3072,1536]{1,0:T(8,128)}), f32[384,1536]{1,0:T(8,128)}) %reduce-scatter.12.cloned.1.call-update) | async-done | bytes 2359312 | tf_op jit(solution)/shard_map/reduce_scatter | solution.py:117
  812.2 317.3 %reduce-scatter.14.cloned.1.call-done = f32[1536,384]{1,0:T(8,128)} async-done(((f32[1536,3072]{1,0:T(8,128)}), f32[1536,384]{1,0:T(8,128)}) %reduce-scatter.14.cloned.1.call-update) | async-done | bytes 2359312 | tf_op jit(solution)/shard_map/reduce_scatter | solution.py:125
  (34 shorter events, 2.6 us)
Async XLA Ops:
  7.2 1.6 copy-start
  7.2 143.8 %all-gather.6.cloned.1.call-start = ((), (), s32[]{:S(2)}) async-start(), calls=%async_computation.5 | async-start | bytes 10616832 | tf_op jit(solution)/shard_map/all_gather | solution.py:62
  7.9 281.5 %all-gather.8.cloned.1.call-start = ((), (), s32[]{:S(2)}) async-start(), calls=%async_computation.6 | async-start | bytes 10616832 | tf_op jit(solution)/shard_map/all_gather | solution.py:66
  8.7 0.9 copy-start.2
  8.7 325.2 %reduce-scatter.6.cloned.1.call-start = ((), (), s32[]{:S(2)}) async-start(), calls=%async_computation.7 | async-start | bytes 3932160 | tf_op jit(solution)/shard_map/reduce_scatter | solution.py:68
  297.6 60.2 %all-gather.12.cloned.1.call-start = ((), (), s32[]{:S(2)}) async-start(), calls=%async_computation.10 | async-start | bytes 1966080 | tf_op jit(solution)/shard_map/all_gather | solution.py:84
  338.0 41.6 %all-gather.10.cloned.1.call-start = ((), (), s32[]{:S(2)}) async-start(), calls=%async_computation.8 | async-start | bytes 1966080 | tf_op jit(solution)/shard_map/all_gather | solution.py:83
  338.5 81.5 %reduce-scatter.10.cloned.1.call-start = ((), (), s32[]{:S(2)}) async-start(), calls=%async_computation.11 | async-start | bytes 3932160 | tf_op jit(solution)/shard_map/reduce_scatter | solution.py:100
  371.5 89.1 %reduce-scatter.8.cloned.1.call-start = ((), (), s32[]{:S(2)}) async-start(), calls=%async_computation.9 | async-start | bytes 3932160 | tf_op jit(solution)/shard_map/reduce_scatter | solution.py:93
  393.3 89.4 %all-gather.14.cloned.1.call-start = ((), (), s32[]{:S(2)}) async-start(), calls=%async_computation.12 | async-start | bytes 1966080 | tf_op jit(solution)/shard_map/all_gather | solution.py:108
  462.9 349.2 %reduce-scatter.12.cloned.1.call-start = ((), (), s32[]{:S(2)}) async-start(), calls=%async_computation.13 | async-start | bytes 21233664 | tf_op jit(solution)/shard_map/reduce_scatter | solution.py:117
  499.2 1.4 copy-start.1
  499.2 630.2 %reduce-scatter.14.cloned.1.call-start = ((), (), s32[]{:S(2)}) async-start(), calls=%async_computation.14 | async-start | bytes 21233664 | tf_op jit(solution)/shard_map/reduce_scatter | solution.py:125
Sparse Core Ops, SparseCore 0:
  10.2 140.7 all-gather.5
  153.0 136.3 all-gather.7
  297.7 36.0 reduce-scatter.5
  338.1 19.6 all-gather.11
  359.8 19.6 all-gather.9
  382.1 37.9 reduce-scatter.9
  422.6 37.9 reduce-scatter.7
  463.0 19.6 all-gather.13
  499.3 312.7 reduce-scatter.11
  817.0 312.4 reduce-scatter.13
where the time goes:
time: 1140 us
  waiting for transfers between devices  1040 us (91%)
  matrix products  66 us (6%)
  between operations  14.9 us (1%)
    reduce_scatter x1, waiting for transfers between devices, per_device(): lax.psum_scatter(down_acc, 'grp', scatter_dimension=1, tiled=True)  317 us
    reduce_scatter x1, waiting for transfers between devices, per_device(): lax.psum_scatter(lax.dot_general(columns, rows_grad, (((0,), (0,)), ((),...  303 us
    all_gather x1, waiting for transfers between devices, per_device(): lax.all_gather(gen_up, 'grp', axis=0, tiled=True)  141 us
    all_gather x1, waiting for transfers between devices, per_device(): down_full = lax.all_gather(gen_down, 'grp', axis=1, tiled=True)  133 us
    reduce_scatter x1, waiting for transfers between devices, per_device(): lax.psum_scatter(jnp.dot(picked_rows, teacher_down, preferred_element_typ...  40.5 us
    reduce_scatter x1, waiting for transfers between devices, per_device(): lax.psum_scatter(jnp.dot(picked_rows, down_full, preferred_element_type=j...  31.6 us
    reduce_scatter x1, waiting for transfers between devices, per_device(): lax.psum_scatter(jnp.dot(picked_rows, critic_down, preferred_element_type...  26.8 us
  transfers between devices with their start and end apart: 10, of which 10 were waited for; matrix products, arithmetic and copies ran while one was open for 4% of the time, Pallas kernels for 0%

commit v1 on v0

v1 whole, which is shorter than its diff:
```python
import jax
import jax.numpy as jnp
from jax import lax
from jax.sharding import PartitionSpec as P

epsilon = 1e-06
root_two_pi = 0.7978845608028654
cubic = 0.044715
f32 = jnp.float32
bf16 = jnp.bfloat16


def normalize(values):
    center = values - jnp.mean(values, axis=-1, keepdims=True)
    spread = jnp.mean(center * center, axis=-1, keepdims=True)
    return center * lax.rsqrt(spread + epsilon)


def smooth_gate(values):
    inner = root_two_pi * (values + cubic * values * values * values)
    return 0.5 * values * (1.0 + jnp.tanh(inner))


def gate_slope(values):
    inner = root_two_pi * (values + cubic * values * values * values)
    tangent = jnp.tanh(inner)
    return 0.5 * (1.0 + tangent) + 0.5 * values * (1.0 - tangent * tangent) * root_two_pi * (
        1.0 + 3.0 * cubic * values * values
    )


def pick_level(table, step_index):
    levels = lax.broadcasted_iota(jnp.int32, (table.shape[0], 1, 1), 0)
    return jnp.sum(jnp.where(levels == step_index, table, 0.0), axis=0)


def modulate(normed, picked):
    return (normed * (1.0 + picked[1]) + picked[0]).astype(bf16)


def dot(left, right, contract=((1,), (0,))):
    return lax.dot_general(left, right, (contract, ((), ())), preferred_element_type=f32)


def make_per_device(groups, parts):
    places = groups // 2
    ring_pairs = [(2 * p + s, 2 * ((p + 1) % places) + s) for p in range(places) for s in range(2)]
    swap_pairs = [(g, g ^ 1) for g in range(groups)]

    def ring(piece):
        return lax.ppermute(piece, "grp", ring_pairs)

    def swap(piece):
        return lax.ppermute(piece, "grp", swap_pairs)

    def gather_groups(own):
        near, far = [own], []
        for _ in range(places - 1):
            far.append(swap(near[-1]))
            near.append(ring(near[-1]))
        half = own.shape[0] // 2
        first = swap(near[-1][:half])
        second = ring(far[-1][half:]) if far else swap(near[-1][half:])
        far.append(jnp.concatenate([first, second], axis=0))
        return near, far

    def bit_pairs(bit):
        return [(t, t ^ (1 << bit)) for t in range(parts)]

    bits = parts.bit_length() - 1

    def sum_parts(values):
        place = lax.axis_index("tp")
        blocks = values.reshape(parts, values.shape[0] // parts, values.shape[1])
        for bit in range(bits):
            mine = (place >> bit) & 1
            split = blocks.reshape(blocks.shape[0] // 2, 2, *blocks.shape[1:])
            keep = lax.dynamic_index_in_dim(split, mine, 1, keepdims=False)
            send = lax.dynamic_index_in_dim(split, 1 - mine, 1, keepdims=False)
            if bit > 0:
                send = send.astype(bf16)
            blocks = keep + lax.ppermute(send, "tp", bit_pairs(bit)).astype(f32)
        return blocks[0]

    def gather_parts(values):
        place = lax.axis_index("tp")
        blocks = values[None]
        for bit in reversed(range(bits)):
            mine = (place >> bit) & 1
            other = lax.ppermute(blocks, "tp", bit_pairs(bit))
            pair = jnp.where(
                mine == 0, jnp.stack([blocks, other], 1), jnp.stack([other, blocks], 1)
            )
            blocks = pair.reshape(-1, *values.shape)
        return blocks

    def per_device(
        gen_noise,
        diff_noise,
        timesteps,
        gen_mod,
        teacher_mod,
        critic_mod,
        gen_up,
        gen_down,
        teacher_up,
        teacher_down,
        critic_up,
        critic_down,
    ):
        local_rows = diff_noise.shape[1]
        depth = gen_up.shape[0]
        step_index = timesteps[0]
        own = lax.axis_index("grp")
        place, side = own // 2, own % 2
        own_start = lax.axis_index("tp") * local_rows

        def origins():
            for k in range(places):
                yield lax.rem(place - k + places, places) * 2 + side
            for k in range(places):
                yield lax.rem(place - k + places, places) * 2 + 1 - side

        def to_absolute(near, far):
            order = [(-r) % places for r in range(places)]
            pairs = [
                jnp.where(
                    side == 0,
                    jnp.concatenate([near[k], far[k]], 1),
                    jnp.concatenate([far[k], near[k]], 1),
                )
                for k in order
            ]
            both = jnp.concatenate(pairs + pairs[:-1], 1)
            width = pairs[0].shape[1]
            start = lax.rem(places - place, places) * width
            return lax.dynamic_slice_in_dim(both, start, width * places, 1)

        noise_all = gen_noise[0].astype(f32)
        gen_rows = modulate(normalize(noise_all), gen_mod)
        noise = lax.dynamic_slice_in_dim(noise_all, own_start, local_rows, 0)

        up_near, up_far = gather_groups(gen_up)
        down_near, down_far = gather_groups(gen_down)

        gen_pre = None
        for piece, origin in zip(up_near + up_far, origins()):
            term = dot(lax.dynamic_slice_in_dim(gen_rows, origin * depth, depth, 1), piece)
            gen_pre = term if gen_pre is None else gen_pre + term
        gen_hidden = smooth_gate(gen_pre).astype(bf16)

        branch_near = [dot(gen_hidden, piece) for piece in down_near]
        branch_far = [dot(gen_hidden, piece) for piece in down_far]
        partial = to_absolute(branch_near, branch_far)
        gen_branch = sum_parts(partial)

        generated = (noise + gen_mod[2] * gen_branch).astype(bf16)
        level = (step_index.astype(f32) + 1.0) / (teacher_mod.shape[0] + 1)
        noised = (
            (1.0 - level) * generated.astype(f32) + level * diff_noise[0].astype(f32)
        ).astype(bf16)
        teacher_row = pick_level(teacher_mod, step_index)
        critic_row = pick_level(critic_mod, step_index)
        noised_all = gather_parts(lax.optimization_barrier(noised)).reshape(
            noise_all.shape
        )
        normed = normalize(noised_all.astype(f32))

        def score(row, weight_up, weight_down):
            hidden = smooth_gate(dot(modulate(normed, row), weight_up)).astype(bf16)
            return row[2] * dot(hidden, weight_down)

        gap_part = score(teacher_row, teacher_up, teacher_down) - score(
            critic_row, critic_up, critic_down
        )
        gap = level * sum_parts(gap_part)
        branch_grad = (gen_mod[2] * gap).astype(bf16)

        def own_columns(rows):
            count = rows.shape[0]
            blocks = rows.reshape(count, groups, depth).transpose(1, 0, 2)
            blocks = lax.all_to_all(blocks, "grp", 0, 0, tiled=True)
            return gather_parts(blocks).transpose(1, 0, 2, 3).reshape(groups, -1, depth)

        input_columns = own_columns(
            lax.dynamic_slice_in_dim(gen_rows, own_start, local_rows, 0)
        )
        grad_columns = own_columns(branch_grad)

        hidden_near, hidden_far = gather_groups(gen_hidden)
        down_grad = None
        for piece, origin in zip(hidden_near + hidden_far, origins()):
            columns = lax.dynamic_index_in_dim(grad_columns, origin, 0, keepdims=False)
            term = dot(piece, columns, ((0,), (0,)))
            down_grad = term if down_grad is None else down_grad + term

        piece_grad = gather_parts(branch_grad).reshape(noise_all.shape)
        hidden_grad = None
        for piece, origin in zip(down_near + down_far, origins()):
            columns = lax.dynamic_slice_in_dim(piece_grad, origin * depth, depth, 1)
            term = dot(columns, piece, ((1,), (1,)))
            hidden_grad = term if hidden_grad is None else hidden_grad + term
        rows_grad = (hidden_grad * gate_slope(gen_pre)).astype(bf16)

        grad_near, grad_far = gather_groups(rows_grad)
        up_grad = None
        for piece, origin in zip(grad_near + grad_far, origins()):
            columns = lax.dynamic_index_in_dim(input_columns, origin, 0, keepdims=False)
            term = dot(columns, piece, ((0,), (0,)))
            up_grad = term if up_grad is None else up_grad + term
        return (generated[None], up_grad, down_grad)

    return per_device


def solution(mesh):
    in_specs = (
        P("grp", None, None),
        P("grp", "tp", None),
        P("grp"),
        P(),
        P(),
        P(),
        P("grp", "tp"),
        P("tp", "grp"),
        P(None, "tp"),
        P("tp", None),
        P(None, "tp"),
        P("tp", None),
    )
    out_specs = (P("grp", "tp", None), P("grp", "tp"), P("tp", "grp"))
    return jax.shard_map(
        make_per_device(mesh.shape["grp"], mesh.shape["tp"]),
        mesh=mesh,
        in_specs=in_specs,
        out_specs=out_specs,
        check_vma=False,
    )
```

time: 1140 us -> 514 us (0.45)
  waiting for transfers between devices: 1040 us -> 322 us
  starting transfers between devices: 0.58 us -> 49 us
  other arithmetic: 11.2 us -> 33.9 us
  local copies, waits for them, and re-layouts: 1.34 us -> 19.9 us
  blocking collectives: 0 us -> 17.7 us
  between operations: 14.9 us -> 2.21 us
    reduce_scatter x5 -> x0, waiting for transfers between devices: 719 us -> none  [the longest x1 317 us: per_device(): lax.psum_scatter(down_acc, 'grp', scatter_dimension=1, tiled=True)]
    all_gather x5 -> x0, waiting for transfers between devices: 321 us -> none  [the longest x1 141 us: per_device(): lax.all_gather(gen_up, 'grp', axis=0, tiled=True)]
    ppermute x0 -> x44, waiting for transfers between devices: none -> 307 us  [the longest x16 190 us: ring(): return lax.ppermute(piece, 'grp', ring_pairs)]
    ppermute x0 -> x44, starting transfers between devices: none -> 42.3 us  [the longest x16 24.9 us: swap(): return lax.ppermute(piece, 'grp', swap_pairs)]
    all_to_all x0 -> x1, blocking collectives: none -> 17.7 us  [own_columns(): blocks = lax.all_to_all(blocks, 'grp', 0, 0, tiled=True)]
    all_to_all x0 -> x1, waiting for transfers between devices: none -> 14.5 us  [own_columns(): blocks = lax.all_to_all(blocks, 'grp', 0, 0, tiled=True)]
    select_n x0 -> x11, other arithmetic: none -> 12.8 us  [gather_parts(): jnp.where(mine == 0, jnp.stack([blocks, other], 1), jnp.stack([other, blo...]
    dot_general x6 -> x42, matrix products: 66 us -> 64.5 us  [dot(): lax.dot_general(left, right, (contract, ((), ())), preferred_element_type...]
  transfers between devices with their start and end apart: 10 -> 45, of which waited for: 10 -> 24; matrix products, arithmetic and copies ran while one was open for 4% -> 13% of each run, Pallas kernels for 0% -> 0%
where the time goes in v1:
time: 514 us; the launch traced here: 509 us
  waiting for transfers between devices  322 us (63%)
  matrix products  64.5 us (13%)
  starting transfers between devices  49 us (10%)
  other arithmetic  33.9 us (7%)
  local copies, waits for them, and re-layouts  19.9 us (4%)
  blocking collectives  17.7 us (3%)
    ppermute x16, waiting for transfers between devices, ring(): return lax.ppermute(piece, 'grp', ring_pairs)  190 us
    ppermute x16, waiting for transfers between devices, swap(): return lax.ppermute(piece, 'grp', swap_pairs)  91 us
    dot_general x42, matrix products, dot(): lax.dot_general(left, right, (contract, ((), ())), preferred_element_type...  64.5 us
    ppermute x16, starting transfers between devices, swap(): return lax.ppermute(piece, 'grp', swap_pairs)  24.9 us
    all_to_all x1, blocking collectives, own_columns(): blocks = lax.all_to_all(blocks, 'grp', 0, 0, tiled=True)  17.7 us
    ppermute x8, waiting for transfers between devices, gather_parts(): other = lax.ppermute(blocks, 'tp', bit_pairs(bit))  14.9 us
    all_to_all x1, waiting for transfers between devices, own_columns(): blocks = lax.all_to_all(blocks, 'grp', 0, 0, tiled=True)  14.5 us
    select_n x11, other arithmetic, gather_parts(): jnp.where(mine == 0, jnp.stack([blocks, other], 1), jnp.stack([other, blo...  12.8 us
  transfers between devices with their start and end apart: 45, of which 24 were waited for; matrix products, arithmetic and copies ran while one was open for 13% of the time, Pallas kernels for 0%

profile of v1, /device:TPU:0, one launch (start us, length us, event | category | flops | bytes accessed | tf_op | source)
XLA Modules:
  0.0 508.9 jit_solution(11482171135533302676)
XLA Ops:
  9.1 23.7 %collective-permute-done = bf16[384,1536]{1,0:T(8,128)(2,1)S(1)} collective-permute-done((bf16[384,1536]{1,0:T(8,128)(2,1)}, bf16[384,1536]{1,0:T(8,128)(2,1)S(1)}, u32[]{:S(2)}, u32[]{:S(2)}) %collective-permute-start) | collective-permute-done | bytes 1179680 | tf_op jit(solution)/shard_map/ppermute | solution.py:51
  32.8 25.4 %collective-permute-done.9 = bf16[1536,384]{1,0:T(8,128)(2,1)} collective-permute-done((bf16[1536,384]{1,0:T(8,128)(2,1)}, bf16[1536,384]{1,0:T(8,128)(2,1)}, u32[]{:S(2)}, u32[]{:S(2)}) %collective-permute-start.9) | collective-permute-done | bytes 1179680 | tf_op jit(solution)/shard_map/ppermute | solution.py:51
  59.6 23.7 %collective-permute-done.1 = bf16[384,1536]{1,0:T(8,128)(2,1)S(1)} collective-permute-done((bf16[384,1536]{1,0:T(8,128)(2,1)S(1)}, bf16[384,1536]{1,0:T(8,128)(2,1)S(1)}, u32[]{:S(2)}, u32[]{:S(2)}) %collective-permute-start.1) | collective-permute-done | bytes 1179680 | tf_op jit(solution)/shard_map/ppermute | solution.py:51
  85.1 23.5 %collective-permute-done.10 = bf16[1536,384]{1,0:T(8,128)(2,1)S(1)} collective-permute-done((bf16[1536,384]{1,0:T(8,128)(2,1)}, bf16[1536,384]{1,0:T(8,128)(2,1)S(1)}, u32[]{:S(2)}, u32[]{:S(2)}) %collective-permute-start.10) | collective-permute-done | bytes 1179680 | tf_op jit(solution)/shard_map/ppermute | solution.py:51
  114.3 19.6 %collective-permute-done.2 = bf16[384,1536]{1,0:T(8,128)(2,1)S(1)} collective-permute-done((bf16[384,1536]{1,0:T(8,128)(2,1)S(1)}, bf16[384,1536]{1,0:T(8,128)(2,1)S(1)}, u32[]{:S(2)}, u32[]{:S(2)}) %collective-permute-start.2) | collective-permute-done | bytes 1179680 | tf_op jit(solution)/shard_map/ppermute | solution.py:51
  135.8 23.3 %collective-permute-done.11 = bf16[1536,384]{1,0:T(8,128)(2,1)S(1)} collective-permute-done((bf16[1536,384]{1,0:T(8,128)(2,1)S(1)}, bf16[1536,384]{1,0:T(8,128)(2,1)S(1)}, u32[]{:S(2)}, u32[]{:S(2)}) %collective-permute-start.11) | collective-permute-done | bytes 1179680 | tf_op jit(solution)/shard_map/ppermute | solution.py:51
  165.1 23.0 %collective-permute-done.12 = bf16[768,384]{1,0:T(8,128)(2,1)S(1)} collective-permute-done((bf16[768,384]{1,0:T(8,128)(2,1)S(1)}, bf16[768,384]{1,0:T(8,128)(2,1)S(1)}, u32[]{:S(2)}, u32[]{:S(2)}) %collective-permute-start.12) | collective-permute-done | bytes 589856 | tf_op jit(solution)/shard_map/ppermute | solution.py:54
  194.4 19.0 %collective-permute-done.8 = bf16[1536,384]{1,0:T(8,128)(2,1)S(1)} collective-permute-done((bf16[1536,384]{1,0:T(8,128)(2,1)S(1)}, bf16[1536,384]{1,0:T(8,128)(2,1)S(1)}, u32[]{:S(2)}, u32[]{:S(2)}) %collective-permute-start.8) | collective-permute-done | bytes 1179680 | tf_op jit(solution)/shard_map/ppermute | solution.py:54
  217.5 18.5 %collective-permute-done.15 = bf16[1536,384]{1,0:T(8,128)(2,1)S(1)} collective-permute-done((bf16[1536,384]{1,0:T(8,128)(2,1)}, bf16[1536,384]{1,0:T(8,128)(2,1)S(1)}, u32[]{:S(2)}, u32[]{:S(2)}) %collective-permute-start.15) | collective-permute-done | bytes 1179680 | tf_op jit(solution)/shard_map/ppermute | solution.py:54
  251.5 7.6 %collective-permute-done.17 = bf16[1,64,3072]{2,1,0:T(8,128)(2,1)} collective-permute-done((bf16[1,64,3072]{2,1,0:T(8,128)(2,1)}, bf16[1,64,3072]{2,1,0:T(8,128)(2,1)}, u32[]{:S(2)}, u32[]{:S(2)}) %collective-permute-start.17) | collective-permute-done | bytes 393248 | tf_op jit(solution)/shard_map/ppermute | solution.py:82
  264.4 7.7 %collective-permute-done.20 = bf16[1,64,3072]{2,1,0:T(8,128)(2,1)S(1)} collective-permute-done((bf16[1,64,3072]{2,1,0:T(8,128)(2,1)S(1)}, bf16[1,64,3072]{2,1,0:T(8,128)(2,1)S(1)}, u32[]{:S(2)}, u32[]{:S(2)}) %collective-permute-start.20) | collective-permute-done | bytes 393248 | tf_op jit(solution)/shard_map/ppermute | solution.py:90
  282.0 13.8 %convolution_multiply_fusion = f32[256,3072]{1,0:T(8,128)} fusion(bf16[1536,3072]{1,0:T(8,128)(2,1)} %param.23, f32[3072]{0:T(1024)} %bitcast.246, bf16[256,3072]{1,0:T(8,128)(2,1)} %get-tuple-element.10, bf16[3072,1536]{1,0:T(8,128)(2,1)} %param.22), kind=kOutput, calls=%fused_computation | convolution fusion | flops 4836163584 | bytes 23605248 | tf_op jit(solution)/shard_map/dot_general | solution.py:42
  295.8 14.2 %fusion = f32[256,3072]{1,0:T(8,128)} fusion(f32[256,3072]{1,0:T(8,128)} %convolution_multiply_fusion, bf16[1536,3072]{1,0:T(8,128)(2,1)} %param.21, f32[3072]{0:T(1024)} %bitcast.245, bf16[256,3072]{1,0:T(8,128)(2,1)S(1)} %copy-done.19, bf16[3072,1536]{1,0:T(8,128)(2,1)} %param.20), kind=kOutput, calls=%fused_computation.2 | convolution fusion | flops 4836950016 | bytes 26750976 | tf_op jit(solution)/shard_map/dot_general | solution.py:42
  313.3 17.7 %all_to_all.10 = bf16[8,64,384]{2,1,0:T(8,128)(2,1)} all-to-all(bf16[8,64,384]{2,1,0:T(8,128)(2,1)S(1)} %copy.36), channel_id=1, replica_groups=mesh['grp'=8,'tp'=4] {'grp'}, dimensions={0} | all-to-all | bytes 786432 | tf_op jit(solution)/shard_map/all_to_all | solution.py:182
  336.3 7.1 %collective-permute-done.18 = bf16[1,8,64,384]{3,2,1,0:T(8,128)(2,1)} collective-permute-done((bf16[1,8,64,384]{3,2,1,0:T(8,128)(2,1)}, bf16[1,8,64,384]{3,2,1,0:T(8,128)(2,1)}, u32[]{:S(2)}, u32[]{:S(2)}) %collective-permute-start.18) | collective-permute-done | bytes 393248 | tf_op jit(solution)/shard_map/ppermute | solution.py:90
  345.8 5.7 %collective-permute-done.36 = bf16[256,1536]{1,0:T(8,128)(2,1)} collective-permute-done((bf16[256,1536]{1,0:T(8,128)(2,1)S(1)}, bf16[256,1536]{1,0:T(8,128)(2,1)}, u32[]{:S(2)}, u32[]{:S(2)}) %collective-permute-start.36) | collective-permute-done | bytes 786464 | tf_op jit(solution)/shard_map/ppermute | solution.py:51
  355.0 6.7 %all-to-all-start.1 = ((bf16[8,64,384]{2,1,0:T(8,128)(2,1)}), bf16[8,64,384]{2,1,0:T(8,128)(2,1)S(1)}, u32[]{:S(2)}, u32[]{:S(2)}) async-start(bf16[8,64,384]{2,1,0:T(8,128)(2,1)} %copy.43), calls=%async_computation.1 | async-start | bytes 786432 | tf_op jit(solution)/shard_map/all_to_all | solution.py:182
  361.8 12.4 %collective-permute-done.37 = bf16[256,1536]{1,0:T(8,128)(2,1)} collective-permute-done((bf16[256,1536]{1,0:T(8,128)(2,1)}, bf16[256,1536]{1,0:T(8,128)(2,1)}, u32[]{:S(2)}, u32[]{:S(2)}) %collective-permute-start.37) | collective-permute-done | bytes 786464 | tf_op jit(solution)/shard_map/ppermute | solution.py:51
  380.5 14.5 %all-to-all-done.1 = bf16[8,64,384]{2,1,0:T(8,128)(2,1)S(1)} async-done(((bf16[8,64,384]{2,1,0:T(8,128)(2,1)}), bf16[8,64,384]{2,1,0:T(8,128)(2,1)S(1)}, u32[]{:S(2)}, u32[]{:S(2)}) %all-to-all-start.1) | async-done | bytes 393248 | tf_op jit(solution)/shard_map/all_to_all | solution.py:182
  427.4 17.2 %collective-permute-done.42 = bf16[128,1536]{1,0:T(8,128)(2,1)S(1)} collective-permute-done((bf16[128,1536]{1,0:T(8,128)(2,1)S(1)}, bf16[128,1536]{1,0:T(8,128)(2,1)S(1)}, u32[]{:S(2)}, u32[]{:S(2)}) %collective-permute-start.42) | collective-permute-done | bytes 393248 | tf_op jit(solution)/shard_map/ppermute | solution.py:54
  454.8 13.6 %collective-permute-done.27 = bf16[256,1536]{1,0:T(8,128)(2,1)S(1)} collective-permute-done((bf16[256,1536]{1,0:T(8,128)(2,1)S(1)}, bf16[256,1536]{1,0:T(8,128)(2,1)S(1)}, u32[]{:S(2)}, u32[]{:S(2)}) %collective-permute-start.27) | collective-permute-done | bytes 786464 | tf_op jit(solution)/shard_map/ppermute | solution.py:51
  471.3 15.6 %collective-permute-done.28 = bf16[256,1536]{1,0:T(8,128)(2,1)S(1)} collective-permute-done((bf16[256,1536]{1,0:T(8,128)(2,1)S(1)}, bf16[256,1536]{1,0:T(8,128)(2,1)S(1)}, u32[]{:S(2)}, u32[]{:S(2)}) %collective-permute-start.28) | collective-permute-done | bytes 786464 | tf_op jit(solution)/shard_map/ppermute | solution.py:51
  487.8 7.3 %collective-permute-done.31 = bf16[256,1536]{1,0:T(8,128)(2,1)S(1)} collective-permute-done((bf16[256,1536]{1,0:T(8,128)(2,1)S(1)}, bf16[256,1536]{1,0:T(8,128)(2,1)S(1)}, u32[]{:S(2)}, u32[]{:S(2)}) %collective-permute-start.31) | collective-permute-done | bytes 786464 | tf_op jit(solution)/shard_map/ppermute | solution.py:54
  497.4 5.2 %collective-permute-done.32 = bf16[128,1536]{1,0:T(8,128)(2,1)S(1)} collective-permute-done((bf16[128,1536]{1,0:T(8,128)(2,1)S(1)}, bf16[128,1536]{1,0:T(8,128)(2,1)S(1)}, u32[]{:S(2)}, u32[]{:S(2)}) %collective-permute-start.32) | collective-permute-done | bytes 393248 | tf_op jit(solution)/shard_map/ppermute | solution.py:54
  (224 shorter events, 140.9 us)
Async XLA Ops:
  0.6 32.1 %collective-permute-start = (bf16[384,1536]{1,0:T(8,128)(2,1)}, bf16[384,1536]{1,0:T(8,128)(2,1)S(1)}, u32[]{:S(2)}, u32[]{:S(2)}) collective-permute-start(bf16[384,1536]{1,0:T(8,128)(2,1)} %param.18), channel_id=1, source_target_pairs={{0,8},{4,12},{8,16},{12,20},{16,24},{20,28},{24,0},{28,4},{1,9},{5... | collective-permute-start | bytes 3538952 | tf_op jit(solution)/shard_map/ppermute | solution.py:51
  3.7 54.4 %collective-permute-start.9 = (bf16[1536,384]{1,0:T(8,128)(2,1)}, bf16[1536,384]{1,0:T(8,128)(2,1)}, u32[]{:S(2)}, u32[]{:S(2)}) collective-permute-start(bf16[1536,384]{1,0:T(8,128)(2,1)} %param.19), channel_id=1, source_target_pairs={{0,8},{4,12},{8,16},{12,20},{16,24},{20,28},{24,0},{28,4},{1,9},{5... | collective-permute-start | bytes 3538952 | tf_op jit(solution)/shard_map/ppermute | solution.py:51
  5.3 105.6 %collective-permute-start.3 = (bf16[384,1536]{1,0:T(8,128)(2,1)}, bf16[384,1536]{1,0:T(8,128)(2,1)}, u32[]{:S(2)}, u32[]{:S(2)}) collective-permute-start(bf16[384,1536]{1,0:T(8,128)(2,1)} %param.18), channel_id=1, source_target_pairs={{0,4},{4,0},{8,12},{12,8},{16,20},{20,16},{24,28},{28,24},{1,5},{5... | collective-permute-start | bytes 3538952 | tf_op jit(solution)/shard_map/ppermute | solution.py:54
  32.8 50.6 %collective-permute-start.1 = (bf16[384,1536]{1,0:T(8,128)(2,1)S(1)}, bf16[384,1536]{1,0:T(8,128)(2,1)S(1)}, u32[]{:S(2)}, u32[]{:S(2)}) collective-permute-start(bf16[384,1536]{1,0:T(8,128)(2,1)S(1)} %collective-permute-done), channel_id=1, source_target_pairs={{0,8},{4,12},{8,16},{12,20},{16,24},{20,28},{24,0},{28,4},{1,9},{5... | collective-permute-start | bytes 3538952 | tf_op jit(solution)/shard_map/ppermute | solution.py:51
  58.1 50.5 %collective-permute-start.10 = (bf16[1536,384]{1,0:T(8,128)(2,1)}, bf16[1536,384]{1,0:T(8,128)(2,1)S(1)}, u32[]{:S(2)}, u32[]{:S(2)}) collective-permute-start(bf16[1536,384]{1,0:T(8,128)(2,1)} %collective-permute-done.9), channel_id=1, source_target_pairs={{0,8},{4,12},{8,16},{12,20},{16,24},{20,28},{24,0},{28,4},{1,9},{5... | collective-permute-start | bytes 3538952 | tf_op jit(solution)/shard_map/ppermute | solution.py:51
  83.3 50.6 %collective-permute-start.2 = (bf16[384,1536]{1,0:T(8,128)(2,1)S(1)}, bf16[384,1536]{1,0:T(8,128)(2,1)S(1)}, u32[]{:S(2)}, u32[]{:S(2)}) collective-permute-start(bf16[384,1536]{1,0:T(8,128)(2,1)S(1)} %collective-permute-done.1), channel_id=1, source_target_pairs={{0,8},{4,12},{8,16},{12,20},{16,24},{20,28},{24,0},{28,4},{1,9},{5... | collective-permute-start | bytes 3538952 | tf_op jit(solution)/shard_map/ppermute | solution.py:51
  83.3 52.4 %collective-permute-start.5 = (bf16[384,1536]{1,0:T(8,128)(2,1)S(1)}, bf16[384,1536]{1,0:T(8,128)(2,1)S(1)}, u32[]{:S(2)}, u32[]{:S(2)}) collective-permute-start(bf16[384,1536]{1,0:T(8,128)(2,1)S(1)} %collective-permute-done.1), channel_id=1, source_target_pairs={{0,4},{4,0},{8,12},{12,8},{16,20},{20,16},{24,28},{28,24},{1,5},{5... | collective-permute-start | bytes 3538952 | tf_op jit(solution)/shard_map/ppermute | solution.py:54
  108.6 50.6 %collective-permute-start.11 = (bf16[1536,384]{1,0:T(8,128)(2,1)S(1)}, bf16[1536,384]{1,0:T(8,128)(2,1)S(1)}, u32[]{:S(2)}, u32[]{:S(2)}) collective-permute-start(bf16[1536,384]{1,0:T(8,128)(2,1)S(1)} %collective-permute-done.10), channel_id=1, source_target_pairs={{0,8},{4,12},{8,16},{12,20},{16,24},{20,28},{24,0},{28,4},{1,9},{5... | collective-permute-start | bytes 3538952 | tf_op jit(solution)/shard_map/ppermute | solution.py:51
  108.6 52.4 %collective-permute-start.13 = (bf16[1536,384]{1,0:T(8,128)(2,1)S(1)}, bf16[1536,384]{1,0:T(8,128)(2,1)S(1)}, u32[]{:S(2)}, u32[]{:S(2)}) collective-permute-start(bf16[1536,384]{1,0:T(8,128)(2,1)S(1)} %collective-permute-done.10), channel_id=1, source_target_pairs={{0,4},{4,0},{8,12},{12,8},{16,20},{20,16},{24,28},{28,24},{1,5},{5... | collective-permute-start | bytes 3538952 | tf_op jit(solution)/shard_map/ppermute | solution.py:54
  110.9 51.9 %collective-permute-start.4 = (bf16[384,1536]{1,0:T(8,128)(2,1)S(1)}, bf16[384,1536]{1,0:T(8,128)(2,1)S(1)}, u32[]{:S(2)}, u32[]{:S(2)}) collective-permute-start(bf16[384,1536]{1,0:T(8,128)(2,1)S(1)} %collective-permute-done), channel_id=1, source_target_pairs={{0,4},{4,0},{8,12},{12,8},{16,20},{20,16},{24,28},{28,24},{1,5},{5... | collective-permute-start | bytes 3538952 | tf_op jit(solution)/shard_map/ppermute | solution.py:54
  133.9 56.1 %collective-permute-start.6 = (bf16[192,1536]{1,0:T(8,128)(2,1)S(1)}, bf16[192,1536]{1,0:T(8,128)(2,1)S(1)}, u32[]{:S(2)}, u32[]{:S(2)}) collective-permute-start(bf16[192,1536]{1,0:T(8,128)(2,1)S(1)} %slice.69), channel_id=1, source_target_pairs={{0,4},{4,0},{8,12},{12,8},{16,20},{20,16},{24,28},{28,24},{1,5},{5... | collective-permute-start | bytes 1769480 | tf_op jit(solution)/shard_map/ppermute | solution.py:54
  135.8 54.2 %collective-permute-start.7 = (bf16[192,1536]{1,0:T(8,128)(2,1)S(1)}, bf16[192,1536]{1,0:T(8,128)(2,1)S(1)}, u32[]{:S(2)}, u32[]{:S(2)}) collective-permute-start(bf16[192,1536]{1,0:T(8,128)(2,1)S(1)} %slice.70), channel_id=1, source_target_pairs={{0,8},{4,12},{8,16},{12,20},{16,24},{20,28},{24,0},{28,4},{1,9},{5... | collective-permute-start | bytes 1769480 | tf_op jit(solution)/shard_map/ppermute | solution.py:51
  159.2 28.9 %collective-permute-start.12 = (bf16[768,384]{1,0:T(8,128)(2,1)S(1)}, bf16[768,384]{1,0:T(8,128)(2,1)S(1)}, u32[]{:S(2)}, u32[]{:S(2)}) collective-permute-start(bf16[768,384]{1,0:T(8,128)(2,1)S(1)} %slice.71), channel_id=1, source_target_pairs={{0,4},{4,0},{8,12},{12,8},{16,20},{20,16},{24,28},{28,24},{1,5},{5... | collective-permute-start | bytes 1769480 | tf_op jit(solution)/shard_map/ppermute | solution.py:54
  161.1 28.8 %collective-permute-start.14 = (bf16[768,384]{1,0:T(8,128)(2,1)S(1)}, bf16[768,384]{1,0:T(8,128)(2,1)S(1)}, u32[]{:S(2)}, u32[]{:S(2)}) collective-permute-start(bf16[768,384]{1,0:T(8,128)(2,1)S(1)} %slice.72), channel_id=1, source_target_pairs={{0,8},{4,12},{8,16},{12,20},{16,24},{20,28},{24,0},{28,4},{1,9},{5... | collective-permute-start | bytes 1769480 | tf_op jit(solution)/shard_map/ppermute | solution.py:51
  162.8 50.6 %collective-permute-start.8 = (bf16[1536,384]{1,0:T(8,128)(2,1)S(1)}, bf16[1536,384]{1,0:T(8,128)(2,1)S(1)}, u32[]{:S(2)}, u32[]{:S(2)}) collective-permute-start(bf16[1536,384]{1,0:T(8,128)(2,1)S(1)} %copy-done.6), channel_id=1, source_target_pairs={{0,4},{4,0},{8,12},{12,8},{16,20},{20,16},{24,28},{28,24},{1,5},{5... | collective-permute-start | bytes 3538952 | tf_op jit(solution)/shard_map/ppermute | solution.py:54
  188.1 48.0 %collective-permute-start.15 = (bf16[1536,384]{1,0:T(8,128)(2,1)}, bf16[1536,384]{1,0:T(8,128)(2,1)S(1)}, u32[]{:S(2)}, u32[]{:S(2)}) collective-permute-start(bf16[1536,384]{1,0:T(8,128)(2,1)} %collective-permute-done.9), channel_id=1, source_target_pairs={{0,4},{4,0},{8,12},{12,8},{16,20},{20,16},{24,28},{28,24},{1,5},{5... | collective-permute-start | bytes 3538952 | tf_op jit(solution)/shard_map/ppermute | solution.py:54
  345.8 49.7 %collective-permute-start.19 = (bf16[2,8,64,384]{3,2,1,0:T(8,128)(2,1)}, bf16[2,8,64,384]{3,2,1,0:T(8,128)(2,1)}, u32[]{:S(2)}, u32[]{:S(2)}) collective-permute-start(bf16[2,8,64,384]{3,2,1,0:T(8,128)(2,1)} %maximum_select_fusion.8), channel_id=1, source_target_pairs={{0,1},{1,0},{2,3},{3,2},{4,5},{5,4},{6,7},{7,6},{8,9},{9,8},{10,11... | collective-permute-start | bytes 2359304 | tf_op jit(solution)/shard_map/ppermute | solution.py:90
  355.0 40.0 %all-to-all-start.1 = ((bf16[8,64,384]{2,1,0:T(8,128)(2,1)}), bf16[8,64,384]{2,1,0:T(8,128)(2,1)S(1)}, u32[]{:S(2)}, u32[]{:S(2)}) async-start(bf16[8,64,384]{2,1,0:T(8,128)(2,1)} %copy.43), calls=%async_computation.1 | async-start | bytes 786432 | tf_op jit(solution)/shard_map/all_to_all | solution.py:182
  379.0 29.7 %collective-permute-start.25 = (bf16[2,64,3072]{2,1,0:T(8,128)(2,1)}, bf16[2,64,3072]{2,1,0:T(8,128)(2,1)}, u32[]{:S(2)}, u32[]{:S(2)}) collective-permute-start(bf16[2,64,3072]{2,1,0:T(8,128)(2,1)} %maximum_select_fusion.11), channel_id=1, source_target_pairs={{0,1},{1,0},{2,3},{3,2},{4,5},{5,4},{6,7},{7,6},{8,9},{9,8},{10,11... | collective-permute-start | bytes 2359304 | tf_op jit(solution)/shard_map/ppermute | solution.py:90
  400.9 49.1 %collective-permute-start.40 = (bf16[256,1536]{1,0:T(8,128)(2,1)}, bf16[256,1536]{1,0:T(8,128)(2,1)S(1)}, u32[]{:S(2)}, u32[]{:S(2)}) collective-permute-start(bf16[256,1536]{1,0:T(8,128)(2,1)} %collective-permute-done.36), channel_id=1, source_target_pairs={{0,4},{4,0},{8,12},{12,8},{16,20},{20,16},{24,28},{28,24},{1,5},{5... | collective-permute-start | bytes 2359304 | tf_op jit(solution)/shard_map/ppermute | solution.py:54
  402.0 42.5 %collective-permute-start.42 = (bf16[128,1536]{1,0:T(8,128)(2,1)S(1)}, bf16[128,1536]{1,0:T(8,128)(2,1)S(1)}, u32[]{:S(2)}, u32[]{:S(2)}) collective-permute-start(bf16[128,1536]{1,0:T(8,128)(2,1)S(1)} %slice.81), channel_id=1, source_target_pairs={{0,4},{4,0},{8,12},{12,8},{16,20},{20,16},{24,28},{28,24},{1,5},{5... | collective-permute-start | bytes 1179656 | tf_op jit(solution)/shard_map/ppermute | solution.py:54
  406.3 38.3 %collective-permute-start.43 = (bf16[128,1536]{1,0:T(8,128)(2,1)S(1)}, bf16[128,1536]{1,0:T(8,128)(2,1)S(1)}, u32[]{:S(2)}, u32[]{:S(2)}) collective-permute-start(bf16[128,1536]{1,0:T(8,128)(2,1)S(1)} %slice.82), channel_id=1, source_target_pairs={{0,8},{4,12},{8,16},{12,20},{16,24},{20,28},{24,0},{28,4},{1,9},{5... | collective-permute-start | bytes 1179656 | tf_op jit(solution)/shard_map/ppermute | solution.py:51
  423.7 46.1 %collective-permute-start.29 = (bf16[256,1536]{1,0:T(8,128)(2,1)S(1)}, bf16[256,1536]{1,0:T(8,128)(2,1)S(1)}, u32[]{:S(2)}, u32[]{:S(2)}) collective-permute-start(bf16[256,1536]{1,0:T(8,128)(2,1)S(1)} %fusion.11), channel_id=1, source_target_pairs={{0,4},{4,0},{8,12},{12,8},{16,20},{20,16},{24,28},{28,24},{1,5},{5... | collective-permute-start | bytes 2359304 | tf_op jit(solution)/shard_map/ppermute | solution.py:54
  453.8 43.1 %collective-permute-start.30 = (bf16[256,1536]{1,0:T(8,128)(2,1)S(1)}, bf16[256,1536]{1,0:T(8,128)(2,1)S(1)}, u32[]{:S(2)}, u32[]{:S(2)}) collective-permute-start(bf16[256,1536]{1,0:T(8,128)(2,1)S(1)} %collective-permute-done.26), channel_id=1, source_target_pairs={{0,4},{4,0},{8,12},{12,8},{16,20},{20,16},{24,28},{28,24},{1,5},{5... | collective-permute-start | bytes 2359304 | tf_op jit(solution)/shard_map/ppermute | solution.py:54
  (46 other events, 881.3 us)

commit v2 on v1

--- a/solution.py
+++ b/solution.py
@@ -1,6 +1,8 @@
 import jax
 import jax.numpy as jnp
 from jax import lax
+from jax.experimental import pallas as pl
+from jax.experimental.pallas import tpu as pltpu
 from jax.sharding import PartitionSpec as P
 
 epsilon = 1e-06
@@ -42,7 +44,7 @@
     return lax.dot_general(left, right, (contract, ((), ())), preferred_element_type=f32)
 
 
-def make_per_device(groups, parts):
+def make_ring(groups, parts):
     places = groups // 2
     ring_pairs = [(2 * p + s, 2 * ((p + 1) % places) + s) for p in range(places) for s in range(2)]
     swap_pairs = [(g, g ^ 1) for g in range(groups)]
@@ -209,6 +211,523 @@
             term = dot(columns, piece, ((0,), (0,)))
             up_grad = term if up_grad is None else up_grad + term
         return (generated[None], up_grad, down_grad)
+
+    return per_device
+
+
+def kernel_call(body, out_shapes, *operands, scalars=None, name, flops=0, moved=None):
+    specs = [pl.BlockSpec(memory_space=pltpu.VMEM) for _ in operands]
+    if scalars is not None:
+        operands = (scalars, *operands)
+        specs = [pl.BlockSpec(memory_space=pltpu.SMEM), *specs]
+    total = sum(o.size * o.dtype.itemsize for o in operands)
+    total += sum(o.size * jnp.dtype(o.dtype).itemsize for o in out_shapes)
+    return pl.pallas_call(
+        body,
+        out_shape=tuple(out_shapes),
+        in_specs=specs,
+        out_specs=tuple(pl.BlockSpec(memory_space=pltpu.VMEM) for _ in out_shapes),
+        compiler_params=pltpu.CompilerParams(vmem_limit_bytes=48 * 1024 * 1024),
+        cost_estimate=pl.CostEstimate(flops=flops, bytes_accessed=total, transcendentals=0),
+        name=name,
+    )(*operands)
+
+
+def settle(*arrays):
+    def body(*refs):
+        pass
+
+    return pl.pallas_call(
+        body,
+        out_shape=tuple(jax.ShapeDtypeStruct(a.shape, a.dtype) for a in arrays),
+        in_specs=[pl.BlockSpec(memory_space=pl.ANY) for _ in arrays],
+        out_specs=tuple(pl.BlockSpec(memory_space=pl.ANY) for _ in arrays),
+        input_output_aliases={i: i for i in range(len(arrays))},
+        name="settle",
+    )(*arrays)
+
+
+def make_paired(groups, parts):
+    pair, swap, far = 2, 1, 4
+    core, side = 1, 2
+    order = (0, side, core, core | side)
+    masks = range(groups)
+
+    def hop(values, axis, mask):
+        size = groups if axis == "grp" else parts
+        return lax.ppermute(values, axis, [(i, i ^ mask) for i in range(size)])
+
+    def shape(*dims, dtype=bf16):
+        return jax.ShapeDtypeStruct(dims, dtype)
+
+    def gather_tokens(own):
+        crossed = hop(own, "tp", side)
+        return [own, crossed, hop(own, "tp", core), hop(crossed, "tp", core)]
+
+    ring_pairs = [(g, (g + 2) % groups) for g in range(groups)]
+
+    def ring(values):
+        return lax.ppermute(values, "grp", ring_pairs)
+
+    def send_blocks(blocks, mask):
+        return hop(blocks[:, blocks.shape[1] // 2 :], "grp", mask)
+
+    def with_arrived(blocks, arrived):
+        return jnp.concatenate([blocks[:, : blocks.shape[1] // 2], arrived], 0)
+
+    def own_columns(tokens, scalars):
+        _, rows, depth = tokens[0].shape
+
+        def body(s, *refs):
+            for g in masks:
+                for at, image_index in enumerate((g, g ^ pair)):
+                    m = s[0] ^ image_index
+                    spot = (m & pair) + (m & 1) * 4 + (m // 4)
+                    for k, ref in enumerate(refs[:-1]):
+                        start = (at * parts + k) * rows
+                        refs[-1][g, start : start + rows, :] = ref[spot]
+
+        (packed,) = kernel_call(
+            body,
+            [shape(groups, 2 * parts * rows, depth)],
+            *tokens,
+            scalars=scalars,
+            name="pack",
+        )
+        return packed
+
+    def per_device(
+        gen_noise,
+        diff_noise,
+        timesteps,
+        gen_mod,
+        teacher_mod,
+        critic_mod,
+        gen_up,
+        gen_down,
+        teacher_up,
+        teacher_down,
+        critic_up,
+        critic_down,
+    ):
+        rows = diff_noise.shape[1]
+        image = gen_noise.shape[1]
+        depth = gen_up.shape[0]
+        width = gen_noise.shape[2]
+        units = gen_up.shape[1] // 2
+        middle = width // 2
+        score_units = teacher_up.shape[1]
+        level_count = teacher_mod.shape[0] + 1.0
+        own = lax.axis_index("grp")
+        part = lax.axis_index("tp")
+        half = (own // pair) % 2
+        scalars = jnp.stack([own, part, timesteps[0], half])
+
+        def block(ref_own, m):
+            return pl.ds(pl.multiple_of((ref_own ^ m) * depth, 128), depth)
+
+        def fixed(m):
+            return slice(m * depth, (m + 1) * depth)
+
+        def halves(values, axis):
+            return tuple(
+                lax.dynamic_slice_in_dim(values, index * units, units, axis)
+                for index in (half, 1 - half)
+            )
+
+        up, down = {}, {}
+        up[0], up_send = halves(gen_up, 1)
+        down[0], down_send = halves(gen_down, 0)
+
+        def input_body(s, noise_ref, mod_ref, rows_ref, blocks_ref):
+            for k, mask in enumerate(order):
+                start = pl.multiple_of((s[1] ^ mask) * rows, 16)
+                values = noise_ref[0, pl.ds(start, rows), :].astype(f32)
+                values = normalize(values) * (1.0 + mod_ref[1:2]) + mod_ref[0:1]
+                rows_ref[k * rows : (k + 1) * rows, :] = values.astype(bf16)
+            for m in masks:
+                blocks_ref[m] = rows_ref[:rows, block(s[0], m)]
+
+        up[pair] = hop(up_send, "grp", pair)
+        up[far] = hop(up[0], "grp", far)
+        up[swap] = hop(up[0], "grp", swap)
+        gen_rows, input_blocks = kernel_call(
+            input_body,
+            [shape(image, width), shape(groups, rows, depth)],
+            gen_noise,
+            gen_mod,
+            scalars=scalars,
+            name="input",
+        )
+        (
+            up[pair],
+            up[far],
+            up[swap],
+            down_send,
+            gen_rows,
+            input_blocks,
+        ) = settle(up[pair], up[far], up[swap], down_send, gen_rows, input_blocks)
+        up[pair | far] = hop(up[pair], "grp", far)
+        up[pair | swap] = hop(up[pair], "grp", swap)
+        up[far | swap] = hop(up[far], "grp", swap)
+        down[pair] = hop(down_send, "grp", pair)
+        pair_rows = gather_tokens(hop(gen_rows[:rows], "grp", pair))
+        (
+            up[pair | far],
+            up[pair | swap],
+            up[far | swap],
+            down[pair],
+            down[0],
+        ) = settle(up[pair | far], up[pair | swap], up[far | swap], down[pair], down[0])
+        up[pair | far | swap] = hop(up[pair | far], "grp", swap)
+        down[far] = hop(down[0], "grp", far)
+        down[swap] = hop(down[0], "grp", swap)
+        up[pair | far | swap], down[pair], down[far], down[swap] = settle(
+            up[pair | far | swap], down[pair], down[far], down[swap]
+        )
+        down[pair | far] = hop(down[pair], "grp", far)
+        down[pair | swap] = hop(down[pair], "grp", swap)
+        down[far | swap] = hop(down[far], "grp", swap)
+
+        def pre_body(s, rows_ref, p0, p1, p2, p3, *refs):
+            pieces, (pre_ref, hidden_ref) = refs[:groups], refs[groups:]
+            for m in masks:
+                spot = block(s[0], m)
+                left = jnp.concatenate(
+                    [rows_ref[:, spot]] + [p[:, spot] for p in (p0, p1, p2, p3)], 0
+                )
+                term = dot(left, pieces[m][...])
+                if m == 0:
+                    pre_ref[...] = term
+                else:
+                    pre_ref[...] += term
+            hidden_ref[...] = smooth_gate(pre_ref[...]).astype(bf16)
+
+        gen_pre, gen_hidden = kernel_call(
+            pre_body,
+            [shape(2 * image, units, dtype=f32), shape(2 * image, units)],
+            gen_rows,
+            *pair_rows,
+            *[up[m] for m in masks],
+            scalars=scalars,
+            name="pre",
+            flops=4 * image * width * units,
+        )
+
+        down[pair | far], down[pair | swap], down[far | swap], gen_hidden = settle(
+            down[pair | far], down[pair | swap], down[far | swap], gen_hidden
+        )
+        down[pair | far | swap] = hop(down[pair | far], "grp", swap)
+        down[pair | far | swap], gen_hidden, input_blocks = settle(
+            down[pair | far | swap], gen_hidden, input_blocks[None]
+        )
+        hidden_near, hidden_across = [gen_hidden], [hop(gen_hidden, "grp", swap)]
+        arrived = send_blocks(input_blocks, far)
+
+        def branch_body(hidden_ref, *refs):
+            pieces, (keep_ref, send_ref) = refs[:-2], refs[-2:]
+            for m, piece in enumerate(pieces):
+                for image_at, spot in ((0, m), (1, m ^ pair)):
+                    values = dot(
+                        hidden_ref[image_at * image : (image_at + 1) * image, :], piece[...]
+                    )
+                    cut = slice(image_at * image // 2, (image_at + 1) * image // 2)
+                    keep_ref[cut, fixed(spot)] = values[: image // 2]
+                    send_ref[cut, fixed(spot)] = values[image // 2 :].astype(bf16)
+
+        def core_body(keep_ref, got_ref, first_ref, second_ref, third_ref, rest_ref):
+            def total(at):
+                cut = slice(at * rows, (at + 1) * rows)
+                return keep_ref[cut, :] + got_ref[cut, :].astype(f32)
+
+            first_ref[...] = total(3).astype(bf16)
+            second_ref[...] = total(1).astype(bf16)
+            third_ref[...] = total(2)
+            rest_ref[...] = total(0)
+
+        def add_body(left_ref, right_ref, out_ref):
+            out_ref[...] = (left_ref[...] + right_ref[...].astype(f32)).astype(bf16)
+
+        def branch_sum(which):
+            count = groups // 2
+            keep, send = kernel_call(
+                branch_body,
+                [shape(image, middle, dtype=f32), shape(image, middle)],
+                gen_hidden,
+                *[down[m] for m in masks if m // count == which],
+                name="branch",
+                flops=2 * image * width * units,
+            )
+            first, second, third, rest = kernel_call(
+                core_body,
+                [shape(rows, middle)] * 2 + [shape(rows, middle, dtype=f32)] * 2,
+                keep,
+                hop(send, "tp", core),
+                name="core_sum",
+            )
+            (third,) = kernel_call(
+                add_body,
+                [shape(rows, middle)],
+                third,
+                hop(first, "tp", side),
+                name="side_sum",
+            )
+            return rest, hop(second, "tp", side), hop(third, "grp", pair)
+
+        def latent_body(s, noise_ref, diff_ref, mod_ref, *refs):
+            sums, (generated_ref, noised_ref) = refs[:6], refs[6:]
+            level = (s[2].astype(f32) + 1.0) / level_count
+            start = pl.multiple_of(s[1] * rows, 16)
+            for m in masks:
+                which, at = divmod(m, groups // 2)
+                a, b, c = sums[3 * which : 3 * which + 3]
+                branch = (
+                    a[:, fixed(at)] + b[:, fixed(at)].astype(f32) + c[:, fixed(at)].astype(f32)
+                )
+                spot = block(s[0], m)
+                noise = noise_ref[0, pl.ds(start, rows), spot].astype(f32)
+                made = (noise + mod_ref[2:3, spot] * branch).astype(bf16)
+                generated_ref[0, :, spot] = made
+                noised_ref[:, spot] = (
+                    (1.0 - level) * made.astype(f32) + level * diff_ref[0, :, spot].astype(f32)
+                ).astype(bf16)
+
+        left_sum = branch_sum(0)
+        right_sum = branch_sum(1)
+        generated, noised = kernel_call(
+            latent_body,
+            [shape(1, rows, width), shape(rows, width)],
+            gen_noise,
+            diff_noise,
+            gen_mod,
+            *left_sum,
+            *right_sum,
+            scalars=scalars,
+            name="latent",
+        )
+
+        noised, hidden_near[0], hidden_across[0], arrived = settle(
+            noised, hidden_near[0], hidden_across[0], arrived
+        )
+        hidden_near.append(ring(hidden_near[0]))
+        input_blocks = with_arrived(input_blocks, arrived)
+        arrived = send_blocks(input_blocks, pair)
+
+        def score_input_body(s, n0, n1, n2, n3, teacher_ref, critic_ref, t_ref, c_ref):
+            for k, part_ref in enumerate((n0, n1, n2, n3)):
+                normed = normalize(part_ref[...].astype(f32))
+                cut = slice(k * rows, (k + 1) * rows)
+                for table, out in ((teacher_ref, t_ref), (critic_ref, c_ref)):
+                    row = table[s[2]]
+                    out[cut, :] = (normed * (1.0 + row[1:2]) + row[0:1]).astype(bf16)
+
+        teacher_in, critic_in = kernel_call(
+            score_input_body,
+            [shape(image, width)] * 2,
+            *gather_tokens(noised),
+            teacher_mod,
+            critic_mod,
+            scalars=scalars,
+            name="score_input",
+        )
+
+        teacher_in, hidden_near[1], arrived = settle(teacher_in, hidden_near[1], arrived)
+        hidden_near.append(ring(hidden_near[1]))
+        hidden_across.append(hop(hidden_near[1], "grp", swap))
+        input_blocks = with_arrived(input_blocks, arrived)
+        arrived = send_blocks(input_blocks, swap)
+
+        tile = 256
+
+        def hidden_body(t_in, c_in, t_w, c_w, t_out, c_out):
+            t_out[...] = smooth_gate(dot(t_in[...], t_w[...])).astype(bf16)
+            c_out[...] = smooth_gate(dot(c_in[...], c_w[...])).astype(bf16)
+
+        whole = pl.BlockSpec((image, width), lambda j: (0, 0))
+        teacher_hidden, critic_hidden = pl.pallas_call(
+            hidden_body,
+            grid=(score_units // tile,),
+            in_specs=[whole, whole] + [pl.BlockSpec((width, tile), lambda j: (0, j))] * 2,
+            out_specs=[pl.BlockSpec((image, tile), lambda j: (0, j))] * 2,
+            out_shape=[shape(image, score_units)] * 2,
+            compiler_params=pltpu.CompilerParams(vmem_limit_bytes=48 * 1024 * 1024),
+            cost_estimate=pl.CostEstimate(
+                flops=4 * image * width * score_units,
+                bytes_accessed=4 * width * score_units,
+                transcendentals=0,
+            ),
+            name="score_hidden",
+        )(teacher_in, critic_in, teacher_up, critic_up)
+
+        def gap_body(s, t_h, c_h, t_w, c_w, t_mod, c_mod, keep_ref, send_ref):
+            values = t_mod[s[2], 2:3] * dot(t_h[...], t_w[...]) - c_mod[s[2], 2:3] * dot(
+                c_h[...], c_w[...]
+            )
+            keep_ref[...] = values[: image // 2]
+            send_ref[...] = values[image // 2 :].astype(bf16)
+
+        whole = pl.BlockSpec((image, score_units), lambda j: (0, 0))
+        keep, send = pl.pallas_call(
+            gap_body,
+            grid=(width // tile,),
+            in_specs=[pl.BlockSpec(memory_space=pltpu.SMEM), whole, whole]
+            + [pl.BlockSpec((score_units, tile), lambda j: (0, j))] * 2
+            + [pl.BlockSpec((*teacher_mod.shape[:2], tile), lambda j: (0, 0, j))] * 2,
+            out_specs=[pl.BlockSpec((image // 2, tile), lambda j: (0, j))] * 2,
+            out_shape=[shape(image // 2, width, dtype=f32), shape(image // 2, width)],
+            compiler_params=pltpu.CompilerParams(vmem_limit_bytes=48 * 1024 * 1024),
+            cost_estimate=pl.CostEstimate(
+                flops=4 * image * width * score_units,
+                bytes_accessed=4 * width * score_units,
+                transcendentals=0,
+            ),
+            name="score_gap",
+        )(scalars, teacher_hidden, critic_hidden, teacher_down, critic_down, teacher_mod, critic_mod)
+
+        send, hidden_near[2], hidden_across[1], arrived = settle(
+            send, hidden_near[2], hidden_across[1], arrived
+        )
+        hidden_near.append(ring(hidden_near[2]))
+        hidden_across.append(hop(hidden_near[2], "grp", swap))
+        input_blocks = with_arrived(input_blocks, arrived)
+
+        def gap_core_body(keep_ref, got_ref, send_ref, rest_ref):
+            send_ref[...] = (keep_ref[rows:, :] + got_ref[rows:, :].astype(f32)).astype(bf16)
+            rest_ref[...] = keep_ref[:rows, :] + got_ref[:rows, :].astype(f32)
+
+        send, rest = kernel_call(
+            gap_core_body,
+            [shape(rows, width), shape(rows, width, dtype=f32)],
+            keep,
+            hop(send, "tp", core),
+            name="gap_core",
+        )
+
+        def grad_body(s, rest_ref, got_ref, mod_ref, rows_ref, blocks_ref):
+            level = (s[2].astype(f32) + 1.0) / level_count
+            for m in masks:
+                spot = block(s[0], m)
+                gap = level * (rest_ref[:, spot] + got_ref[:, spot].astype(f32))
+                values = (mod_ref[2:3, spot] * gap).astype(bf16)
+                rows_ref[:, fixed(m)] = values
+                blocks_ref[m] = values
+
+        branch_grad, grad_blocks = kernel_call(
+            grad_body,
+            [shape(rows, width), shape(groups, rows, depth)],
+            rest,
+            hop(send, "tp", side),
+            gen_mod,
+            scalars=scalars,
+            name="branch_grad",
+        )
+
+        branch_grad, hidden_near[3], hidden_across[2], grad_blocks = settle(
+            branch_grad, hidden_near[3], hidden_across[2], grad_blocks[None]
+        )
+        pair_grad = hop(branch_grad, "grp", pair)
+        crossed = hop(branch_grad, "tp", side)
+        arrived = send_blocks(grad_blocks, far)
+        pair_grad, crossed, arrived = settle(pair_grad, crossed, arrived)
+        grad_blocks = with_arrived(grad_blocks, arrived)
+        own_tokens = [branch_grad, crossed]
+        own_tokens += [hop(values, "tp", core) for values in own_tokens]
+        pair_tokens = gather_tokens(pair_grad)
+        arrived = send_blocks(grad_blocks, pair)
+        pair_tokens[-1], arrived = settle(pair_tokens[-1], arrived)
+        grad_blocks = with_arrived(grad_blocks, arrived)
+        arrived = send_blocks(grad_blocks, swap)
+        hidden_last = [
+            hop(hidden_near[-1][:image], "grp", swap),
+            ring(hidden_across[-1][image:]),
+        ]
+
+        def rows_grad_body(*refs):
+            tokens, pieces = refs[:8], refs[8 : 8 + groups]
+            pre_ref, out_ref, total = refs[8 + groups :]
+            for m in masks:
+                left = jnp.concatenate(
+                    [t[:, fixed(m)] for t in tokens[:4]]
+                    + [t[:, fixed(m ^ pair)] for t in tokens[4:]],
+                    0,
+                )
+                term = dot(left, pieces[m][...], ((1,), (1,)))
+                if m == 0:
+                    total[...] = term
+                else:
+                    total[...] += term
+            out_ref[...] = (total[...] * gate_slope(pre_ref[...])).astype(bf16)
+
+        operands = (*own_tokens, *pair_tokens, *[down[m] for m in masks], gen_pre)
+        rows_grad = pl.pallas_call(
+            rows_grad_body,
+            out_shape=shape(2 * image, units),
+            in_specs=[pl.BlockSpec(memory_space=pltpu.VMEM) for _ in operands],
+            out_specs=pl.BlockSpec(memory_space=pltpu.VMEM),
+            scratch_shapes=[pltpu.VMEM((2 * image, units), f32)],
+            compiler_params=pltpu.CompilerParams(vmem_limit_bytes=48 * 1024 * 1024),
+            cost_estimate=pl.CostEstimate(
+                flops=4 * image * width * units, bytes_accessed=10**7, transcendentals=0
+            ),
+            name="rows_grad",
+        )(*operands)
+
+        rows_grad, arrived, input_blocks, *hidden_last = settle(
+            rows_grad, arrived, input_blocks, *hidden_last
+        )
+        grad_blocks = with_arrived(grad_blocks, arrived)
+        near, across = [rows_grad], []
+        for k in range(groups // 2 - 1):
+            near.append(ring(near[k]))
+            across.append(hop(near[k], "grp", swap))
+        input_columns = own_columns(gather_tokens(input_blocks[:, 0]), scalars)
+        grad_columns = own_columns(gather_tokens(grad_blocks[:, 0]), scalars)
+
+        def columns_at(table, k, other):
+            origin = lax.rem(own + groups - 2 * k, groups) ^ other
+            return lax.dynamic_index_in_dim(table, origin, 0, keepdims=False)
+
+        def in_order(table, near, across, last=()):
+            for k, piece in enumerate(near):
+                yield k % 2, columns_at(table, k, 0), piece
+            for k, piece in enumerate(across):
+                yield k % 2, columns_at(table, k, swap), piece
+            for at, piece in enumerate(last):
+                columns = columns_at(table, groups // 2 - 1, swap)
+                yield 1, columns[at * image : (at + 1) * image], piece
+
+        def over_tokens(left, right):
+            return dot(left, right, ((0,), (0,)))
+
+        def join_halves(mine, other, axis):
+            return jnp.where(
+                half == 0,
+                jnp.concatenate([mine, other], axis),
+                jnp.concatenate([other, mine], axis),
+            )
+
+        down_sums = [0.0, 0.0]
+        for which, columns, piece in in_order(
+            grad_columns, hidden_near, hidden_across, hidden_last
+        ):
+            down_sums[which] += over_tokens(piece, columns)
+        near[-1], across[-1], *down_sums = settle(near[-1], across[-1], *down_sums)
+        last = [hop(near[-1][:image], "grp", swap), ring(across[-1][image:])]
+        up_sums = [0.0, 0.0]
+        for which, columns, piece in in_order(input_columns, near, across, last):
+            up_sums[which] += over_tokens(columns, piece)
+        return generated, join_halves(*up_sums, 1), join_halves(*down_sums, 0)
+
+    return per_device
+
+
+def make_per_device(groups, parts):
+    def per_device(*args):
+        depth, units = args[6].shape
+        fits = depth % 128 == 0 and units % 512 == 0 and args[1].shape[1] % 16 == 0
+        if groups == 8 and parts == 4 and fits:
+            return make_paired(groups, parts)(*args)
+        return make_ring(groups, parts)(*args)
 
     return per_device
 

time: 514 us -> 408 us (0.79)
  waiting for transfers between devices: 322 us -> 203 us
  Pallas kernels: 0 us -> 52.2 us
  matrix products: 64.5 us -> 25.4 us
  local copies, waits for them, and re-layouts: 19.9 us -> 44.9 us
  other arithmetic: 33.9 us -> 9.08 us
  starting transfers between devices: 49 us -> 70.3 us
  blocking collectives: 17.7 us -> 0 us
    ppermute x44 -> x66, waiting for transfers between devices: 307 us -> 203 us  [the longest x58 159 us: hop(): return lax.ppermute(values, axis, [(i, i ^ mask) for i in range(size)])]
    pallas_call x0 -> x30, Pallas kernels: none -> 52.2 us  [the longest x14 20.8 us: kernel_call(): pl.pallas_call(body, out_shape=tuple(out_shapes), in_specs=specs, out_spe...]
    dot_general x42 -> x18, matrix products: 64.5 us -> 25.4 us  [dot(): lax.dot_general(left, right, (contract, ((), ())), preferred_element_type...]
    ppermute x44 -> x66, starting transfers between devices: 42.3 us -> 70.3 us  [the longest x58 67.6 us: hop(): return lax.ppermute(values, axis, [(i, i ^ mask) for i in range(size)])]
    unnamed x53 -> x158, local copies, waits for them, and re-layouts: 7.19 us -> 31.5 us
    all_to_all x1 -> x0, blocking collectives: 17.7 us -> none  [own_columns(): blocks = lax.all_to_all(blocks, 'grp', 0, 0, tiled=True)]
    all_to_all x1 -> x0, waiting for transfers between devices: 14.5 us -> none  [own_columns(): blocks = lax.all_to_all(blocks, 'grp', 0, 0, tiled=True)]
    convert_element_type x6 -> x0, other arithmetic: 10.9 us -> none  [the longest x2 4.34 us: modulate(): return (normed * (1.0 + picked[1]) + picked[0]).astype(bf16)]
  transfers between devices with their start and end apart: 45 -> 66, of which waited for: 24 -> 29; matrix products, arithmetic and copies ran while one was open for 13% -> 10% of each run, Pallas kernels for 0% -> 12%
where the time goes in v2:
time: 408 us; the launch traced here: 407 us
  waiting for transfers between devices  203 us (50%)
  starting transfers between devices  70.3 us (17%)
  Pallas kernels  52.2 us (13%)
  local copies, waits for them, and re-layouts  44.9 us (11%)
  matrix products  25.4 us (6%)
  other arithmetic  9.08 us (2%)
    ppermute x58, waiting for transfers between devices, hop(): return lax.ppermute(values, axis, [(i, i ^ mask) for i in range(size)])  159 us
    ppermute x58, starting transfers between devices, hop(): return lax.ppermute(values, axis, [(i, i ^ mask) for i in range(size)])  67.6 us
    ppermute x8, waiting for transfers between devices, ring(): return lax.ppermute(values, 'grp', ring_pairs)  43.7 us
    unnamed x158, local copies, waits for them, and re-layouts  31.5 us
    dot_general x18, matrix products, dot(): lax.dot_general(left, right, (contract, ((), ())), preferred_element_type...  25.4 us
    pallas_call x14, Pallas kernels, kernel_call(): pl.pallas_call(body, out_shape=tuple(out_shapes), in_specs=specs, out_spe...  20.8 us
    pallas_call x1, Pallas kernels, per_device(): pl.pallas_call(gap_body, grid=(width // tile,), in_specs=[pl.BlockSpec(me...  13.2 us
    pallas_call x1, Pallas kernels, per_device(): pl.pallas_call(hidden_body, grid=(score_units // tile,), in_specs=[whole,...  10.6 us
  transfers between devices with their start and end apart: 66, of which 29 were waited for; matrix products, arithmetic and copies ran while one was open for 10% of the time, Pallas kernels for 12%

profile of v2, /device:TPU:0, one launch (start us, length us, event | category | flops | bytes accessed | tf_op | source)
XLA Modules:
  0.0 406.6 jit_solution(18028718249280742655)
XLA Ops:
  14.3 17.8 %collective-permute-done.refs_0_ = bf16[384,768]{1,0:T(8,128)(2,1)S(1)} collective-permute-done((bf16[384,768]{1,0:T(8,128)(2,1)}, bf16[384,768]{1,0:T(8,128)(2,1)S(1)}, u32[]{:S(2)}, u32[]{:S(2)}) %collective-permute-start) | collective-permute-done | bytes 589856 | tf_op jit(solution)/shard_map/ppermute | solution.py:258
  42.1 19.5 %collective-permute-done.3.refs_0_ = bf16[384,768]{1,0:T(8,128)(2,1)S(1)} collective-permute-done((bf16[384,768]{1,0:T(8,128)(2,1)}, bf16[384,768]{1,0:T(8,128)(2,1)S(1)}, u32[]{:S(2)}, u32[]{:S(2)}) %collective-permute-start.3) | collective-permute-done | bytes 589856 | tf_op jit(solution)/shard_map/ppermute | solution.py:258
  69.7 5.9 %collective-permute-done.13.p0 = bf16[64,3072]{1,0:T(8,128)(2,1)} collective-permute-done((bf16[64,3072]{1,0:T(8,128)(2,1)}, bf16[64,3072]{1,0:T(8,128)(2,1)}, u32[]{:S(2)}, u32[]{:S(2)}) %collective-permute-start.13) | collective-permute-done | bytes 393248 | tf_op jit(solution)/shard_map/ppermute | solution.py:258
  77.0 6.7 %collective-permute-done.14.p1 = bf16[64,3072]{1,0:T(8,128)(2,1)} collective-permute-done((bf16[64,3072]{1,0:T(8,128)(2,1)}, bf16[64,3072]{1,0:T(8,128)(2,1)}, u32[]{:S(2)}, u32[]{:S(2)}) %collective-permute-start.14) | collective-permute-done | bytes 393248 | tf_op jit(solution)/shard_map/ppermute | solution.py:258
  83.7 8.4 %collective-permute-done.8.refs_2_ = bf16[768,384]{1,0:T(8,128)(2,1)S(1)} collective-permute-done((bf16[768,384]{1,0:T(8,128)(2,1)}, bf16[768,384]{1,0:T(8,128)(2,1)S(1)}, u32[]{:S(2)}, u32[]{:S(2)}) %collective-permute-start.8) | collective-permute-done | bytes 589856 | tf_op jit(solution)/shard_map/ppermute | solution.py:258
  101.5 7.3 %pre.1 = (f32[512,768]{1,0:T(8,128)}, bf16[512,768]{1,0:T(8,128)(2,1)}) custom-call(s32[4]{0:T(128)S(1)} %pad_add_fusion.s, bf16[256,3072]{1,0:T(8,128)(2,1)} %get-tuple-element.92.rows_ref, bf16[64,3072]{1,0:T(8,128)(2,1)} %collective-permute-done.13.p0, bf16[64,3072]{1,0:T(8,128)(2,1)} %collective-permute-done.14.p1, ...), custom_call_target="tpu_custom_call" | custom-call | flops 2415919104 | bytes 10223632 | tf_op jit(solution)/shard_map/pre/pallas_call | solution.py:225
  111.6 6.8 %collective-permute-done.12.refs_2_ = bf16[768,384]{1,0:T(8,128)(2,1)S(1)} collective-permute-done((bf16[768,384]{1,0:T(8,128)(2,1)}, bf16[768,384]{1,0:T(8,128)(2,1)S(1)}, u32[]{:S(2)}, u32[]{:S(2)}) %collective-permute-start.12) | collective-permute-done | bytes 589856 | tf_op jit(solution)/shard_map/ppermute | solution.py:258
  119.5 10.1 %collective-permute-done.17.refs_0_ = bf16[768,384]{1,0:T(8,128)(2,1)S(1)} collective-permute-done((bf16[768,384]{1,0:T(8,128)(2,1)}, bf16[768,384]{1,0:T(8,128)(2,1)S(1)}, u32[]{:S(2)}, u32[]{:S(2)}) %collective-permute-start.17) | collective-permute-done | bytes 589856 | tf_op jit(solution)/shard_map/ppermute | solution.py:258
  147.5 15.9 %collective-permute-start.25 = (bf16[64,1536]{1,0:T(8,128)(2,1)S(1)}, bf16[64,1536]{1,0:T(8,128)(2,1)S(1)}, u32[]{:S(2)}, u32[]{:S(2)}) collective-permute-start(bf16[64,1536]{1,0:T(8,128)(2,1)S(1)} %side_sum.3), channel_id=1, source_target_pairs={{0,8},{4,12},{8,0},{12,4},{16,24},{20,28},{24,16},{28,20},{1,9},{5... | collective-permute-start | bytes 589832 | tf_op jit(solution)/shard_map/ppermute | solution.py:258
  167.9 5.8 %collective-permute-done.21.refs_2_ = bf16[64,1536]{1,0:T(8,128)(2,1)S(1)} collective-permute-done((bf16[64,1536]{1,0:T(8,128)(2,1)S(1)}, bf16[64,1536]{1,0:T(8,128)(2,1)S(1)}, u32[]{:S(2)}, u32[]{:S(2)}) %collective-permute-start.21) | collective-permute-done | bytes 196640 | tf_op jit(solution)/shard_map/ppermute | solution.py:258
  181.2 6.3 %collective-permute-done.28.n1 = bf16[64,3072]{1,0:T(8,128)(2,1)S(1)} collective-permute-done((bf16[64,3072]{1,0:T(8,128)(2,1)}, bf16[64,3072]{1,0:T(8,128)(2,1)S(1)}, u32[]{:S(2)}, u32[]{:S(2)}) %collective-permute-start.28) | collective-permute-done | bytes 393248 | tf_op jit(solution)/shard_map/ppermute | solution.py:258
  195.0 9.0 %collective-permute-done.32.refs_2_ = bf16[2,2,64,384]{3,2,1,0:T(8,128)(2,1)S(1)} collective-permute-done((bf16[2,2,64,384]{3,2,1,0:T(8,128)(2,1)S(1)}, bf16[2,2,64,384]{3,2,1,0:T(8,128)(2,1)S(1)}, u32[]{:S(2)}, u32[]{:S(2)}) %collective-permute-start.32) | collective-permute-done | bytes 196640 | tf_op jit(solution)/shard_map/ppermute | solution.py:258
  209.3 10.6 %score_hidden.1 = (bf16[256,1536]{1,0:T(8,128)(2,1)S(1)}, bf16[256,1536]{1,0:T(8,128)(2,1)S(1)}) custom-call(bf16[256,3072]{1,0:T(8,128)(2,1)S(1)} %copy-done.5, bf16[256,3072]{1,0:T(8,128)(2,1)S(1)} %copy-done.38, bf16[3072,1536]{1,0:T(8,128)(2,1)} %t_w.2, bf16[3072,1536]{1,0:T(8,128)(2,1)} %c_w.2), custom_call_target="tpu_custom_call" | custom-call | flops 4831838208 | bytes 18874368 | tf_op jit(solution)/shard_map/score_hidden/pallas_call | solution.py:547
  219.9 13.2 %score_gap.1 = (f32[128,3072]{1,0:T(8,128)S(1)}, bf16[128,3072]{1,0:T(8,128)(2,1)S(1)}) custom-call(s32[4]{0:T(128)S(1)} %pad_add_fusion.s, bf16[256,1536]{1,0:T(8,128)(2,1)S(1)} %get-tuple-element.127.t_h, bf16[256,1536]{1,0:T(8,128)(2,1)S(1)} %get-tuple-element.128.c_h, bf16[1536,3072]{1,0:T(8,128)(2,1)} %t_w.3, bf16[1536,3072]{1,0:T(8,128)(2,1)} %c_w.3, ...), custom_call_target="tpu_custom_call" | custom-call | flops 4831838208 | bytes 18874368 | tf_op jit(solution)/shard_map/score_gap/pallas_call | solution.py:570
  240.2 10.6 %collective-permute-done.37.got_ref = bf16[64,3072]{1,0:T(8,128)(2,1)S(1)} collective-permute-done((bf16[64,3072]{1,0:T(8,128)(2,1)S(1)}, bf16[64,3072]{1,0:T(8,128)(2,1)S(1)}, u32[]{:S(2)}, u32[]{:S(2)}) %collective-permute-start.37) | collective-permute-done | bytes 393248 | tf_op jit(solution)/shard_map/ppermute | solution.py:258
  253.0 6.2 %collective-permute-done.38.refs_1_ = bf16[512,768]{1,0:T(8,128)(2,1)} collective-permute-done((bf16[512,768]{1,0:T(8,128)(2,1)}, bf16[512,768]{1,0:T(8,128)(2,1)}, u32[]{:S(2)}, u32[]{:S(2)}) %collective-permute-start.38) | collective-permute-done | bytes 786464 | tf_op jit(solution)/shard_map/ppermute | solution.py:270
  263.2 9.1 %collective-permute-done.42.refs_2_ = bf16[1,4,64,384]{3,2,1,0:T(8,128)(2,1)S(1)} collective-permute-done((bf16[1,4,64,384]{3,2,1,0:T(8,128)(2,1)S(1)}, bf16[1,4,64,384]{3,2,1,0:T(8,128)(2,1)S(1)}, u32[]{:S(2)}, u32[]{:S(2)}) %collective-permute-start.42) | collective-permute-done | bytes 196640 | tf_op jit(solution)/shard_map/ppermute | solution.py:258
  275.2 9.6 %collective-permute-done.45.refs_5_ = bf16[64,3072]{1,0:T(8,128)(2,1)S(1)} collective-permute-done((bf16[64,3072]{1,0:T(8,128)(2,1)}, bf16[64,3072]{1,0:T(8,128)(2,1)S(1)}, u32[]{:S(2)}, u32[]{:S(2)}) %collective-permute-start.45) | collective-permute-done | bytes 393248 | tf_op jit(solution)/shard_map/ppermute | solution.py:258
  300.1 7.6 %rows_grad.1.refs_0_ = bf16[512,768]{1,0:T(8,128)(2,1)} custom-call(bf16[64,3072]{1,0:T(8,128)(2,1)S(1)} %copy-done.29, bf16[64,3072]{1,0:T(8,128)(2,1)} %get-tuple-element.141.refs_1_, bf16[64,3072]{1,0:T(8,128)(2,1)} %collective-permute-done.43.refs_2_, bf16[64,3072]{1,0:T(8,128)(2,1)} %collective-permute-done.44.refs_3_, ...), custom_call_target="tpu_custom_call" | custom-call | flops 2415919104 | bytes 10000000 | tf_op jit(solution)/shard_map/rows_grad/pallas_call | solution.py:662
  311.6 10.0 %collective-permute-done.60.refs_1_ = bf16[8,64,384]{2,1,0:T(8,128)(2,1)S(1)} collective-permute-done((bf16[8,64,384]{2,1,0:T(8,128)(2,1)S(1)}, bf16[8,64,384]{2,1,0:T(8,128)(2,1)S(1)}, u32[]{:S(2)}, u32[]{:S(2)}) %collective-permute-start.60) | collective-permute-done | bytes 393248 | tf_op jit(solution)/shard_map/ppermute | solution.py:258
  332.2 11.5 %collective-permute-done.55 = bf16[512,768]{1,0:T(8,128)(2,1)} collective-permute-done((bf16[512,768]{1,0:T(8,128)(2,1)}, bf16[512,768]{1,0:T(8,128)(2,1)}, u32[]{:S(2)}, u32[]{:S(2)}) %collective-permute-start.55) | collective-permute-done | bytes 786464 | tf_op jit(solution)/shard_map/ppermute | solution.py:270
  356.5 8.4 %collective-permute-done.56 = bf16[512,768]{1,0:T(8,128)(2,1)} collective-permute-done((bf16[512,768]{1,0:T(8,128)(2,1)}, bf16[512,768]{1,0:T(8,128)(2,1)}, u32[]{:S(2)}, u32[]{:S(2)}) %collective-permute-start.56) | collective-permute-done | bytes 786464 | tf_op jit(solution)/shard_map/ppermute | solution.py:270
  372.7 12.6 %collective-permute-done.58.refs_0_ = bf16[512,768]{1,0:T(8,128)(2,1)} collective-permute-done((bf16[512,768]{1,0:T(8,128)(2,1)}, bf16[512,768]{1,0:T(8,128)(2,1)}, u32[]{:S(2)}, u32[]{:S(2)}) %collective-permute-start.58) | collective-permute-done | bytes 786464 | tf_op jit(solution)/shard_map/ppermute | solution.py:270
  397.9 4.9 %collective-permute-done.65 = bf16[256,768]{1,0:T(8,128)(2,1)S(1)} collective-permute-done((bf16[256,768]{1,0:T(8,128)(2,1)S(1)}, bf16[256,768]{1,0:T(8,128)(2,1)S(1)}, u32[]{:S(2)}, u32[]{:S(2)}) %collective-permute-start.65) | collective-permute-done | bytes 393248 | tf_op jit(solution)/shard_map/ppermute | solution.py:270
  (336 shorter events, 170.5 us)
Async XLA Ops:
  3.0 29.2 %collective-permute-start = (bf16[384,768]{1,0:T(8,128)(2,1)}, bf16[384,768]{1,0:T(8,128)(2,1)S(1)}, u32[]{:S(2)}, u32[]{:S(2)}) collective-permute-start(bf16[384,768]{1,0:T(8,128)(2,1)} %get-tuple-element.164), channel_id=1, source_target_pairs={{0,8},{4,12},{8,0},{12,4},{16,24},{20,28},{24,16},{28,20},{1,9},{5... | collective-permute-start | bytes 1769480 | tf_op jit(solution)/shard_map/ppermute | solution.py:258
  6.0 26.2 %collective-permute-start.1 = (bf16[384,768]{1,0:T(8,128)(2,1)S(1)}, bf16[384,768]{1,0:T(8,128)(2,1)S(1)}, u32[]{:S(2)}, u32[]{:S(2)}) collective-permute-start(bf16[384,768]{1,0:T(8,128)(2,1)S(1)} %get-tuple-element.163.refs_0_), channel_id=1, source_target_pairs={{0,16},{4,20},{8,24},{12,28},{16,0},{20,4},{24,8},{28,12},{1,17},{... | collective-permute-start | bytes 1769480 | tf_op jit(solution)/shard_map/ppermute | solution.py:258
  8.6 23.6 %collective-permute-start.2 = (bf16[384,768]{1,0:T(8,128)(2,1)S(1)}, bf16[384,768]{1,0:T(8,128)(2,1)}, u32[]{:S(2)}, u32[]{:S(2)}) collective-permute-start(bf16[384,768]{1,0:T(8,128)(2,1)S(1)} %get-tuple-element.163.refs_0_), channel_id=1, source_target_pairs={{0,4},{4,0},{8,12},{12,8},{16,20},{20,16},{24,28},{28,24},{1,5},{5... | collective-permute-start | bytes 1769480 | tf_op jit(solution)/shard_map/ppermute | solution.py:258
  33.2 28.4 %collective-permute-start.3 = (bf16[384,768]{1,0:T(8,128)(2,1)}, bf16[384,768]{1,0:T(8,128)(2,1)S(1)}, u32[]{:S(2)}, u32[]{:S(2)}) collective-permute-start(bf16[384,768]{1,0:T(8,128)(2,1)} %get-tuple-element.84.refs_2_), channel_id=1, source_target_pairs={{0,16},{4,20},{8,24},{12,28},{16,0},{20,4},{24,8},{28,12},{1,17},{... | collective-permute-start | bytes 1769480 | tf_op jit(solution)/shard_map/ppermute | solution.py:258
  35.8 25.8 %collective-permute-start.4 = (bf16[384,768]{1,0:T(8,128)(2,1)}, bf16[384,768]{1,0:T(8,128)(2,1)S(1)}, u32[]{:S(2)}, u32[]{:S(2)}) collective-permute-start(bf16[384,768]{1,0:T(8,128)(2,1)} %get-tuple-element.84.refs_2_), channel_id=1, source_target_pairs={{0,4},{4,0},{8,12},{12,8},{16,20},{20,16},{24,28},{28,24},{1,5},{5... | collective-permute-start | bytes 1769480 | tf_op jit(solution)/shard_map/ppermute | solution.py:258
  37.3 25.2 %collective-permute-start.5 = (bf16[384,768]{1,0:T(8,128)(2,1)}, bf16[384,768]{1,0:T(8,128)(2,1)S(1)}, u32[]{:S(2)}, u32[]{:S(2)}) collective-permute-start(bf16[384,768]{1,0:T(8,128)(2,1)} %get-tuple-element.85.refs_4_), channel_id=1, source_target_pairs={{0,4},{4,0},{8,12},{12,8},{16,20},{20,16},{24,28},{28,24},{1,5},{5... | collective-permute-start | bytes 1769480 | tf_op jit(solution)/shard_map/ppermute | solution.py:258
  37.8 27.8 %collective-permute-start.6 = (bf16[768,384]{1,0:T(8,128)(2,1)}, bf16[768,384]{1,0:T(8,128)(2,1)S(1)}, u32[]{:S(2)}, u32[]{:S(2)}) collective-permute-start(bf16[768,384]{1,0:T(8,128)(2,1)} %get-tuple-element.86), channel_id=1, source_target_pairs={{0,8},{4,12},{8,0},{12,4},{16,24},{20,28},{24,16},{28,20},{1,9},{5... | collective-permute-start | bytes 1769480 | tf_op jit(solution)/shard_map/ppermute | solution.py:258
  42.0 33.6 %collective-permute-start.13 = (bf16[64,3072]{1,0:T(8,128)(2,1)}, bf16[64,3072]{1,0:T(8,128)(2,1)}, u32[]{:S(2)}, u32[]{:S(2)}) collective-permute-start(bf16[64,3072]{1,0:T(8,128)(2,1)} %slice.75), channel_id=1, source_target_pairs={{0,8},{4,12},{8,0},{12,4},{16,24},{20,28},{24,16},{28,20},{1,9},{5... | collective-permute-start | bytes 1179656 | tf_op jit(solution)/shard_map/ppermute | solution.py:258
  67.8 24.3 %collective-permute-start.8 = (bf16[768,384]{1,0:T(8,128)(2,1)}, bf16[768,384]{1,0:T(8,128)(2,1)S(1)}, u32[]{:S(2)}, u32[]{:S(2)}) collective-permute-start(bf16[768,384]{1,0:T(8,128)(2,1)} %get-tuple-element.89.refs_0_.refs_8_), channel_id=1, source_target_pairs={{0,16},{4,20},{8,24},{12,28},{16,0},{20,4},{24,8},{28,12},{1,17},{... | collective-permute-start | bytes 1769480 | tf_op jit(solution)/shard_map/ppermute | solution.py:258
  69.2 22.9 %collective-permute-start.9 = (bf16[768,384]{1,0:T(8,128)(2,1)}, bf16[768,384]{1,0:T(8,128)(2,1)S(1)}, u32[]{:S(2)}, u32[]{:S(2)}) collective-permute-start(bf16[768,384]{1,0:T(8,128)(2,1)} %get-tuple-element.89.refs_0_.refs_8_), channel_id=1, source_target_pairs={{0,4},{4,0},{8,12},{12,8},{16,20},{20,16},{24,28},{28,24},{1,5},{5... | collective-permute-start | bytes 1769480 | tf_op jit(solution)/shard_map/ppermute | solution.py:258
  93.7 24.7 %collective-permute-start.12 = (bf16[768,384]{1,0:T(8,128)(2,1)}, bf16[768,384]{1,0:T(8,128)(2,1)S(1)}, u32[]{:S(2)}, u32[]{:S(2)}) collective-permute-start(bf16[768,384]{1,0:T(8,128)(2,1)} %get-tuple-element.91.refs_0_.refs_12_), channel_id=1, source_target_pairs={{0,4},{4,0},{8,12},{12,8},{16,20},{20,16},{24,28},{28,24},{1,5},{5... | collective-permute-start | bytes 1769480 | tf_op jit(solution)/shard_map/ppermute | solution.py:258
  139.1 39.4 %collective-permute-start.26 = (bf16[512,768]{1,0:T(8,128)(2,1)S(1)}, bf16[512,768]{1,0:T(8,128)(2,1)S(1)}, u32[]{:S(2)}, u32[]{:S(2)}) collective-permute-start(bf16[512,768]{1,0:T(8,128)(2,1)S(1)} %copy-done.1), channel_id=1, source_target_pairs={{0,4},{4,0},{8,12},{12,8},{16,20},{20,16},{24,28},{28,24},{1,5},{5... | collective-permute-start | bytes 2359304 | tf_op jit(solution)/shard_map/ppermute | solution.py:258
  141.3 22.1 %collective-permute-start.20 = (bf16[64,1536]{1,0:T(8,128)(2,1)S(1)}, bf16[64,1536]{1,0:T(8,128)(2,1)S(1)}, u32[]{:S(2)}, u32[]{:S(2)}) collective-permute-start(bf16[64,1536]{1,0:T(8,128)(2,1)S(1)} %get-tuple-element.109), channel_id=1, source_target_pairs={{0,2},{1,3},{2,0},{3,1},{4,6},{5,7},{6,4},{7,5},{8,10},{9,11},{10,... | collective-permute-start | bytes 589832 | tf_op jit(solution)/shard_map/ppermute | solution.py:258
  142.8 24.9 %collective-permute-start.23 = (bf16[64,1536]{1,0:T(8,128)(2,1)S(1)}, bf16[64,1536]{1,0:T(8,128)(2,1)S(1)}, u32[]{:S(2)}, u32[]{:S(2)}) collective-permute-start(bf16[64,1536]{1,0:T(8,128)(2,1)S(1)} %get-tuple-element.115), channel_id=1, source_target_pairs={{0,2},{1,3},{2,0},{3,1},{4,6},{5,7},{6,4},{7,5},{8,10},{9,11},{10,... | collective-permute-start | bytes 589832 | tf_op jit(solution)/shard_map/ppermute | solution.py:258
  143.4 24.3 %collective-permute-start.19 = (bf16[64,1536]{1,0:T(8,128)(2,1)S(1)}, bf16[64,1536]{1,0:T(8,128)(2,1)S(1)}, u32[]{:S(2)}, u32[]{:S(2)}) collective-permute-start(bf16[64,1536]{1,0:T(8,128)(2,1)S(1)} %get-tuple-element.107), channel_id=1, source_target_pairs={{0,2},{1,3},{2,0},{3,1},{4,6},{5,7},{6,4},{7,5},{8,10},{9,11},{10,... | collective-permute-start | bytes 589832 | tf_op jit(solution)/shard_map/ppermute | solution.py:258
  181.2 22.9 %collective-permute-start.31 = (bf16[512,768]{1,0:T(8,128)(2,1)}, bf16[512,768]{1,0:T(8,128)(2,1)}, u32[]{:S(2)}, u32[]{:S(2)}) collective-permute-start(bf16[512,768]{1,0:T(8,128)(2,1)} %get-tuple-element.123), channel_id=1, source_target_pairs={{0,8},{4,12},{8,16},{12,20},{16,24},{20,28},{24,0},{28,4},{1,9},{5... | collective-permute-start | bytes 2359304 | tf_op jit(solution)/shard_map/ppermute | solution.py:270
  204.7 30.5 %collective-permute-start.33 = (bf16[512,768]{1,0:T(8,128)(2,1)}, bf16[512,768]{1,0:T(8,128)(2,1)S(1)}, u32[]{:S(2)}, u32[]{:S(2)}) collective-permute-start(bf16[512,768]{1,0:T(8,128)(2,1)} %get-tuple-element.131), channel_id=1, source_target_pairs={{0,8},{4,12},{8,16},{12,20},{16,24},{20,28},{24,0},{28,4},{1,9},{5... | collective-permute-start | bytes 2359304 | tf_op jit(solution)/shard_map/ppermute | solution.py:270
  204.7 30.5 %collective-permute-start.34 = (bf16[512,768]{1,0:T(8,128)(2,1)}, bf16[512,768]{1,0:T(8,128)(2,1)S(1)}, u32[]{:S(2)}, u32[]{:S(2)}) collective-permute-start(bf16[512,768]{1,0:T(8,128)(2,1)} %get-tuple-element.131), channel_id=1, source_target_pairs={{0,4},{4,0},{8,12},{12,8},{16,20},{20,16},{24,28},{28,24},{1,5},{5... | collective-permute-start | bytes 2359304 | tf_op jit(solution)/shard_map/ppermute | solution.py:258
  206.7 28.4 %collective-permute-start.35 = (bf16[4,1,64,384]{3,2,1,0:T(8,128)(2,1)S(1)}, bf16[4,1,64,384]{3,2,1,0:T(8,128)(2,1)S(1)}, u32[]{:S(2)}, u32[]{:S(2)}) collective-permute-start(bf16[4,1,64,384]{3,2,1,0:T(8,128)(2,1)S(1)} %get-tuple-element.168), channel_id=1, source_target_pairs={{0,4},{4,0},{8,12},{12,8},{16,20},{20,16},{24,28},{28,24},{1,5},{5... | collective-permute-start | bytes 589832 | tf_op jit(solution)/shard_map/ppermute | solution.py:258
  237.0 22.3 %collective-permute-start.38 = (bf16[512,768]{1,0:T(8,128)(2,1)}, bf16[512,768]{1,0:T(8,128)(2,1)}, u32[]{:S(2)}, u32[]{:S(2)}) collective-permute-start(bf16[512,768]{1,0:T(8,128)(2,1)} %get-tuple-element.137), channel_id=1, source_target_pairs={{0,8},{4,12},{8,16},{12,20},{16,24},{20,28},{24,0},{28,4},{1,9},{5... | collective-permute-start | bytes 2359304 | tf_op jit(solution)/shard_map/ppermute | solution.py:270
  321.6 22.1 %collective-permute-start.55 = (bf16[512,768]{1,0:T(8,128)(2,1)}, bf16[512,768]{1,0:T(8,128)(2,1)}, u32[]{:S(2)}, u32[]{:S(2)}) collective-permute-start(bf16[512,768]{1,0:T(8,128)(2,1)} %get-tuple-element.151), channel_id=1, source_target_pairs={{0,8},{4,12},{8,16},{12,20},{16,24},{20,28},{24,0},{28,4},{1,9},{5... | collective-permute-start | bytes 2359304 | tf_op jit(solution)/shard_map/ppermute | solution.py:270
  322.8 23.5 %collective-permute-start.53 = (bf16[8,64,384]{2,1,0:T(8,128)(2,1)}, bf16[8,64,384]{2,1,0:T(8,128)(2,1)S(1)}, u32[]{:S(2)}, u32[]{:S(2)}) collective-permute-start(bf16[8,64,384]{2,1,0:T(8,128)(2,1)} %bitcast.86), channel_id=1, source_target_pairs={{0,1},{1,0},{2,3},{3,2},{4,5},{5,4},{6,7},{7,6},{8,9},{9,8},{10,11... | collective-permute-start | bytes 1179656 | tf_op jit(solution)/shard_map/ppermute | solution.py:258
  323.0 27.2 %collective-permute-start.57 = (bf16[512,768]{1,0:T(8,128)(2,1)}, bf16[512,768]{1,0:T(8,128)(2,1)S(1)}, u32[]{:S(2)}, u32[]{:S(2)}) collective-permute-start(bf16[512,768]{1,0:T(8,128)(2,1)} %get-tuple-element.151), channel_id=1, source_target_pairs={{0,4},{4,0},{8,12},{12,8},{16,20},{20,16},{24,28},{28,24},{1,5},{5... | collective-permute-start | bytes 2359304 | tf_op jit(solution)/shard_map/ppermute | solution.py:258
  343.7 59.5 %collective-permute-start.63 = (bf16[512,768]{1,0:T(8,128)(2,1)}, bf16[512,768]{1,0:T(8,128)(2,1)}, u32[]{:S(2)}, u32[]{:S(2)}) collective-permute-start(bf16[512,768]{1,0:T(8,128)(2,1)} %collective-permute-done.55), channel_id=1, source_target_pairs={{0,4},{4,0},{8,12},{12,8},{16,20},{20,16},{24,28},{28,24},{1,5},{5... | collective-permute-start | bytes 2359304 | tf_op jit(solution)/shard_map/ppermute | solution.py:258
  (120 other events, 843.5 us)

commit v3 on v2

--- a/solution.py
+++ b/solution.py
@@ -227,7 +227,7 @@
         out_shape=tuple(out_shapes),
         in_specs=specs,
         out_specs=tuple(pl.BlockSpec(memory_space=pltpu.VMEM) for _ in out_shapes),
-        compiler_params=pltpu.CompilerParams(vmem_limit_bytes=48 * 1024 * 1024),
+        compiler_params=pltpu.CompilerParams(vmem_limit_bytes=8 * 1024 * 1024),
         cost_estimate=pl.CostEstimate(flops=flops, bytes_accessed=total, transcendentals=0),
         name=name,
     )(*operands)
@@ -243,6 +243,7 @@
         in_specs=[pl.BlockSpec(memory_space=pl.ANY) for _ in arrays],
         out_specs=tuple(pl.BlockSpec(memory_space=pl.ANY) for _ in arrays),
         input_output_aliases={i: i for i in range(len(arrays))},
+        compiler_params=pltpu.CompilerParams(vmem_limit_bytes=256 * 1024),
         name="settle",
     )(*arrays)
 
@@ -414,16 +415,6 @@
             flops=4 * image * width * units,
         )
 
-        down[pair | far], down[pair | swap], down[far | swap], gen_hidden = settle(
-            down[pair | far], down[pair | swap], down[far | swap], gen_hidden
-        )
-        down[pair | far | swap] = hop(down[pair | far], "grp", swap)
-        down[pair | far | swap], gen_hidden, input_blocks = settle(
-            down[pair | far | swap], gen_hidden, input_blocks[None]
-        )
-        hidden_near, hidden_across = [gen_hidden], [hop(gen_hidden, "grp", swap)]
-        arrived = send_blocks(input_blocks, far)
-
         def branch_body(hidden_ref, *refs):
             pieces, (keep_ref, send_ref) = refs[:-2], refs[-2:]
             for m, piece in enumerate(pieces):
@@ -448,23 +439,25 @@
         def add_body(left_ref, right_ref, out_ref):
             out_ref[...] = (left_ref[...] + right_ref[...].astype(f32)).astype(bf16)
 
-        def branch_sum(which):
+        def branch_core(which, hidden):
             count = groups // 2
             keep, send = kernel_call(
                 branch_body,
                 [shape(image, middle, dtype=f32), shape(image, middle)],
-                gen_hidden,
+                hidden,
                 *[down[m] for m in masks if m // count == which],
                 name="branch",
                 flops=2 * image * width * units,
             )
-            first, second, third, rest = kernel_call(
+            return kernel_call(
                 core_body,
                 [shape(rows, middle)] * 2 + [shape(rows, middle, dtype=f32)] * 2,
                 keep,
                 hop(send, "tp", core),
                 name="core_sum",
             )
+
+        def branch_sum(first, second, third, rest):
             (third,) = kernel_call(
                 add_body,
                 [shape(rows, middle)],
@@ -473,6 +466,35 @@
                 name="side_sum",
             )
             return rest, hop(second, "tp", side), hop(third, "grp", pair)
+
+        (
+            down[pair | far],
+            down[pair | swap],
+            down[far | swap],
+            gen_hidden,
+            input_blocks,
+        ) = settle(
+            down[pair | far],
+            down[pair | swap],
+            down[far | swap],
+            gen_hidden,
+            input_blocks[None],
+        )
+        down[pair | far | swap] = hop(down[pair | far], "grp", swap)
+        arrived = send_blocks(input_blocks, far)
+        left_terms = branch_core(0, gen_hidden)
+        down[pair | far | swap], gen_hidden, arrived, *left_terms = settle(
+            down[pair | far | swap], gen_hidden, arrived, *left_terms
+        )
+        left_sum = branch_sum(*left_terms)
+        hidden_near, hidden_across = [gen_hidden], [hop(gen_hidden, "grp", swap)]
+        input_blocks = with_arrived(input_blocks, arrived)
+        arrived = send_blocks(input_blocks, pair)
+        right_terms = branch_core(1, gen_hidden)
+        arrived, *right_terms = settle(arrived, *right_terms)
+        right_sum = branch_sum(*right_terms)
+        input_blocks = with_arrived(input_blocks, arrived)
+        arrived = send_blocks(input_blocks, swap)
 
         def latent_body(s, noise_ref, diff_ref, mod_ref, *refs):
             sums, (generated_ref, noised_ref) = refs[:6], refs[6:]
@@ -492,8 +514,6 @@
                     (1.0 - level) * made.astype(f32) + level * diff_ref[0, :, spot].astype(f32)
                 ).astype(bf16)
 
-        left_sum = branch_sum(0)
-        right_sum = branch_sum(1)
         generated, noised = kernel_call(
             latent_body,
             [shape(1, rows, width), shape(rows, width)],
@@ -510,8 +530,6 @@
             noised, hidden_near[0], hidden_across[0], arrived
         )
         hidden_near.append(ring(hidden_near[0]))
-        input_blocks = with_arrived(input_blocks, arrived)
-        arrived = send_blocks(input_blocks, pair)
 
         def score_input_body(s, n0, n1, n2, n3, teacher_ref, critic_ref, t_ref, c_ref):
             for k, part_ref in enumerate((n0, n1, n2, n3)):
@@ -531,11 +549,8 @@
             name="score_input",
         )
 
-        teacher_in, hidden_near[1], arrived = settle(teacher_in, hidden_near[1], arrived)
-        hidden_near.append(ring(hidden_near[1]))
-        hidden_across.append(hop(hidden_near[1], "grp", swap))
-        input_blocks = with_arrived(input_blocks, arrived)
-        arrived = send_blocks(input_blocks, swap)
+        teacher_in, arrived = settle(teacher_in, arrived)
+        input_tokens = gather_tokens(with_arrived(input_blocks, arrived)[:, 0])
 
         tile = 256
 
@@ -550,7 +565,7 @@
             in_specs=[whole, whole] + [pl.BlockSpec((width, tile), lambda j: (0, j))] * 2,
             out_specs=[pl.BlockSpec((image, tile), lambda j: (0, j))] * 2,
             out_shape=[shape(image, score_units)] * 2,
-            compiler_params=pltpu.CompilerParams(vmem_limit_bytes=48 * 1024 * 1024),
+            compiler_params=pltpu.CompilerParams(vmem_limit_bytes=8 * 1024 * 1024),
             cost_estimate=pl.CostEstimate(
                 flops=4 * image * width * score_units,
                 bytes_accessed=4 * width * score_units,
@@ -558,6 +573,12 @@
             ),
             name="score_hidden",
         )(teacher_in, critic_in, teacher_up, critic_up)
+
+        teacher_hidden, hidden_near[1], *input_tokens = settle(
+            teacher_hidden, hidden_near[1], *input_tokens
+        )
+        hidden_near.append(ring(hidden_near[1]))
+        hidden_across.append(hop(hidden_near[1], "grp", swap))
 
         def gap_body(s, t_h, c_h, t_w, c_w, t_mod, c_mod, keep_ref, send_ref):
             values = t_mod[s[2], 2:3] * dot(t_h[...], t_w[...]) - c_mod[s[2], 2:3] * dot(
@@ -575,7 +596,7 @@
             + [pl.BlockSpec((*teacher_mod.shape[:2], tile), lambda j: (0, 0, j))] * 2,
             out_specs=[pl.BlockSpec((image // 2, tile), lambda j: (0, j))] * 2,
             out_shape=[shape(image // 2, width, dtype=f32), shape(image // 2, width)],
-            compiler_params=pltpu.CompilerParams(vmem_limit_bytes=48 * 1024 * 1024),
+            compiler_params=pltpu.CompilerParams(vmem_limit_bytes=8 * 1024 * 1024),
             cost_estimate=pl.CostEstimate(
                 flops=4 * image * width * score_units,
                 bytes_accessed=4 * width * score_units,
@@ -584,12 +605,11 @@
             name="score_gap",
         )(scalars, teacher_hidden, critic_hidden, teacher_down, critic_down, teacher_mod, critic_mod)
 
-        send, hidden_near[2], hidden_across[1], arrived = settle(
-            send, hidden_near[2], hidden_across[1], arrived
+        send, hidden_near[2], hidden_across[1] = settle(
+            send, hidden_near[2], hidden_across[1]
         )
         hidden_near.append(ring(hidden_near[2]))
         hidden_across.append(hop(hidden_near[2], "grp", swap))
-        input_blocks = with_arrived(input_blocks, arrived)
 
         def gap_core_body(keep_ref, got_ref, send_ref, rest_ref):
             send_ref[...] = (keep_ref[rows:, :] + got_ref[rows:, :].astype(f32)).astype(bf16)
@@ -622,25 +642,22 @@
             name="branch_grad",
         )
 
-        branch_grad, hidden_near[3], hidden_across[2], grad_blocks = settle(
-            branch_grad, hidden_near[3], hidden_across[2], grad_blocks[None]
-        )
+        grad_blocks = grad_blocks[None]
         pair_grad = hop(branch_grad, "grp", pair)
         crossed = hop(branch_grad, "tp", side)
         arrived = send_blocks(grad_blocks, far)
-        pair_grad, crossed, arrived = settle(pair_grad, crossed, arrived)
-        grad_blocks = with_arrived(grad_blocks, arrived)
+        pair_grad, crossed, arrived, hidden_near[3], hidden_across[2] = settle(
+            pair_grad, crossed, arrived, hidden_near[3], hidden_across[2]
+        )
+        hidden_across.append(hop(hidden_near[3], "grp", swap))
+        pair_crossed = hop(pair_grad, "tp", side)
         own_tokens = [branch_grad, crossed]
         own_tokens += [hop(values, "tp", core) for values in own_tokens]
-        pair_tokens = gather_tokens(pair_grad)
+        grad_blocks = with_arrived(grad_blocks, arrived)
         arrived = send_blocks(grad_blocks, pair)
-        pair_tokens[-1], arrived = settle(pair_tokens[-1], arrived)
-        grad_blocks = with_arrived(grad_blocks, arrived)
-        arrived = send_blocks(grad_blocks, swap)
-        hidden_last = [
-            hop(hidden_near[-1][:image], "grp", swap),
-            ring(hidden_across[-1][image:]),
-        ]
+        pair_core = hop(pair_grad, "tp", core)
+        pair_crossed, arrived = settle(pair_crossed, arrived)
+        pair_tokens = [pair_grad, pair_crossed, pair_core, hop(pair_crossed, "tp", core)]
 
         def rows_grad_body(*refs):
             tokens, pieces = refs[:8], refs[8 : 8 + groups]
@@ -665,23 +682,26 @@
             in_specs=[pl.BlockSpec(memory_space=pltpu.VMEM) for _ in operands],
             out_specs=pl.BlockSpec(memory_space=pltpu.VMEM),
             scratch_shapes=[pltpu.VMEM((2 * image, units), f32)],
-            compiler_params=pltpu.CompilerParams(vmem_limit_bytes=48 * 1024 * 1024),
+            compiler_params=pltpu.CompilerParams(vmem_limit_bytes=8 * 1024 * 1024),
             cost_estimate=pl.CostEstimate(
                 flops=4 * image * width * units, bytes_accessed=10**7, transcendentals=0
             ),
             name="rows_grad",
         )(*operands)
 
-        rows_grad, arrived, input_blocks, *hidden_last = settle(
-            rows_grad, arrived, input_blocks, *hidden_last
-        )
+        rows_grad, arrived, hidden_across[3] = settle(rows_grad, arrived, hidden_across[3])
+        near, across = [rows_grad, ring(rows_grad)], [hop(rows_grad, "grp", swap)]
         grad_blocks = with_arrived(grad_blocks, arrived)
-        near, across = [rows_grad], []
-        for k in range(groups // 2 - 1):
-            near.append(ring(near[k]))
-            across.append(hop(near[k], "grp", swap))
-        input_columns = own_columns(gather_tokens(input_blocks[:, 0]), scalars)
-        grad_columns = own_columns(gather_tokens(grad_blocks[:, 0]), scalars)
+        arrived = send_blocks(grad_blocks, swap)
+        near[1], across[0], arrived = settle(near[1], across[0], arrived)
+        near.append(ring(near[1]))
+        across.append(hop(near[1], "grp", swap))
+        grad_tokens = gather_tokens(with_arrived(grad_blocks, arrived)[:, 0])
+        near[2], across[1], *grad_tokens = settle(near[2], across[1], *grad_tokens)
+        near.append(ring(near[2]))
+        across.append(hop(near[2], "grp", swap))
+        input_columns = own_columns(input_tokens, scalars)
+        grad_columns = own_columns(grad_tokens, scalars)
 
         def columns_at(table, k, other):
             origin = lax.rem(own + groups - 2 * k, groups) ^ other
@@ -708,7 +728,7 @@
 
         down_sums = [0.0, 0.0]
         for which, columns, piece in in_order(
-            grad_columns, hidden_near, hidden_across, hidden_last
+            grad_columns, hidden_near, hidden_across
         ):
             down_sums[which] += over_tokens(piece, columns)
         near[-1], across[-1], *down_sums = settle(near[-1], across[-1], *down_sums)

time: 408 us -> 361 us (0.88)
  local copies, waits for them, and re-layouts: 44.9 us -> 12.9 us
  waiting for transfers between devices: 203 us -> 235 us
  starting transfers between devices: 70.3 us -> 54.7 us
  matrix products: 25.4 us -> 12.8 us
  Pallas kernels: 52.2 us -> 39.8 us
  other arithmetic: 9.08 us -> 3.6 us
    ppermute x58, waiting for transfers between devices: 159 us -> 191 us  [hop(): return lax.ppermute(values, axis, [(i, i ^ mask) for i in range(size)])]
    unnamed x158 -> x92, local copies, waits for them, and re-layouts: 31.5 us -> 10.3 us
    ppermute x58, starting transfers between devices: 67.6 us -> 52.3 us  [hop(): return lax.ppermute(values, axis, [(i, i ^ mask) for i in range(size)])]
    dot_general x18 -> x17, matrix products: 25.4 us -> 12.8 us  [dot(): lax.dot_general(left, right, (contract, ((), ())), preferred_element_type...]
    concatenate x5 -> x4, other arithmetic: 4.74 us -> 0.13 us  [with_arrived(): return jnp.concatenate([blocks[:, :blocks.shape[1] // 2], arrived], 0)]
    ppermute x8 -> x7, waiting for transfers between devices: 43.7 us -> 43.5 us  [ring(): return lax.ppermute(values, 'grp', ring_pairs)]
  transfers between devices with their start and end apart: 66 -> 65, of which waited for: 29 -> 36; matrix products, arithmetic and copies ran while one was open for 10% -> 4% of each run, Pallas kernels for 12% -> 9%
where the time goes in v3:
time: 361 us
  waiting for transfers between devices  235 us (65%)
  starting transfers between devices  54.7 us (15%)
  Pallas kernels  39.8 us (11%)
  local copies, waits for them, and re-layouts  12.9 us (4%)
  matrix products  12.8 us (4%)
    ppermute x58, waiting for transfers between devices, hop(): return lax.ppermute(values, axis, [(i, i ^ mask) for i in range(size)])  191 us
    ppermute x58, starting transfers between devices, hop(): return lax.ppermute(values, axis, [(i, i ^ mask) for i in range(size)])  52.3 us
    ppermute x7, waiting for transfers between devices, ring(): return lax.ppermute(values, 'grp', ring_pairs)  43.5 us
    pallas_call x14, Pallas kernels, kernel_call(): pl.pallas_call(body, out_shape=tuple(out_shapes), in_specs=specs, out_spe...  17.2 us
    dot_general x17, matrix products, dot(): lax.dot_general(left, right, (contract, ((), ())), preferred_element_type...  12.8 us
    pallas_call x1, Pallas kernels, per_device(): pl.pallas_call(gap_body, grid=(width // tile,), in_specs=[pl.BlockSpec(me...  10.3 us
    unnamed x92, local copies, waits for them, and re-layouts  10.3 us
    pallas_call x1, Pallas kernels, per_device(): pl.pallas_call(hidden_body, grid=(score_units // tile,), in_specs=[whole,...  8.08 us
  transfers between devices with their start and end apart: 65, of which 36 were waited for; matrix products, arithmetic and copies ran while one was open for 4% of the time, Pallas kernels for 9%

profile of v3, /device:TPU:0, one launch (start us, length us, event | category | flops | bytes accessed | tf_op | source)
XLA Modules:
  0.0 360.5 jit_solution(5412107056850387217)
XLA Ops:
  12.8 19.3 %collective-permute-done.refs_0_ = bf16[384,768]{1,0:T(8,128)(2,1)S(1)} collective-permute-done((bf16[384,768]{1,0:T(8,128)(2,1)}, bf16[384,768]{1,0:T(8,128)(2,1)S(1)}, u32[]{:S(2)}, u32[]{:S(2)}) %collective-permute-start) | collective-permute-done | bytes 589856 | tf_op jit(solution)/shard_map/ppermute | solution.py:259
  39.5 20.9 %collective-permute-done.3.refs_0_ = bf16[384,768]{1,0:T(8,128)(2,1)S(1)} collective-permute-done((bf16[384,768]{1,0:T(8,128)(2,1)S(1)}, bf16[384,768]{1,0:T(8,128)(2,1)S(1)}, u32[]{:S(2)}, u32[]{:S(2)}) %collective-permute-start.3) | collective-permute-done | bytes 589856 | tf_op jit(solution)/shard_map/ppermute | solution.py:259
  61.4 8.1 %collective-permute-done.6.refs_3_ = bf16[768,384]{1,0:T(8,128)(2,1)S(1)} collective-permute-done((bf16[768,384]{1,0:T(8,128)(2,1)S(1)}, bf16[768,384]{1,0:T(8,128)(2,1)S(1)}, u32[]{:S(2)}, u32[]{:S(2)}) %collective-permute-start.6) | collective-permute-done | bytes 589856 | tf_op jit(solution)/shard_map/ppermute | solution.py:259
  77.1 6.4 %collective-permute-done.14.p1 = bf16[64,3072]{1,0:T(8,128)(2,1)S(1)} collective-permute-done((bf16[64,3072]{1,0:T(8,128)(2,1)S(1)}, bf16[64,3072]{1,0:T(8,128)(2,1)S(1)}, u32[]{:S(2)}, u32[]{:S(2)}) %collective-permute-start.14) | collective-permute-done | bytes 393248 | tf_op jit(solution)/shard_map/ppermute | solution.py:259
  83.5 14.2 %collective-permute-done.8.refs_2_ = bf16[768,384]{1,0:T(8,128)(2,1)S(1)} collective-permute-done((bf16[768,384]{1,0:T(8,128)(2,1)S(1)}, bf16[768,384]{1,0:T(8,128)(2,1)S(1)}, u32[]{:S(2)}, u32[]{:S(2)}) %collective-permute-start.8) | collective-permute-done | bytes 589856 | tf_op jit(solution)/shard_map/ppermute | solution.py:259
  99.8 4.8 %pre.1 = (f32[512,768]{1,0:T(8,128)S(1)}, bf16[512,768]{1,0:T(8,128)(2,1)S(1)}) custom-call(s32[4]{0:T(128)S(1)} %pad_add_fusion.s, bf16[256,3072]{1,0:T(8,128)(2,1)S(1)} %get-tuple-element.111.rows_ref, bf16[64,3072]{1,0:T(8,128)(2,1)S(1)} %collective-permute-done.13.p0, bf16[64,3072]{1,0:T(8,128)(2,1)S(1)} %collective-permute-done.14.p1, ...), custom_call_target="tpu_custom_call" | custom-call | flops 2415919104 | bytes 10223632 | tf_op jit(solution)/shard_map/pre/pallas_call | solution.py:225
  104.6 10.2 %collective-permute-done.10.refs_0_ = bf16[768,384]{1,0:T(8,128)(2,1)S(1)} collective-permute-done((bf16[768,384]{1,0:T(8,128)(2,1)S(1)}, bf16[768,384]{1,0:T(8,128)(2,1)S(1)}, u32[]{:S(2)}, u32[]{:S(2)}) %collective-permute-start.10) | collective-permute-done | bytes 589856 | tf_op jit(solution)/shard_map/ppermute | solution.py:259
  120.6 9.8 %collective-permute-done.18.refs_2_ = bf16[1,4,64,384]{3,2,1,0:T(8,128)(2,1)S(1)} collective-permute-done((bf16[1,4,64,384]{3,2,1,0:T(8,128)(2,1)S(1)}, bf16[1,4,64,384]{3,2,1,0:T(8,128)(2,1)S(1)}, u32[]{:S(2)}, u32[]{:S(2)}) %collective-permute-start.18) | collective-permute-done | bytes 196640 | tf_op jit(solution)/shard_map/ppermute | solution.py:259
  141.8 4.2 %collective-permute-start.22 = (bf16[64,1536]{1,0:T(8,128)(2,1)S(1)}, bf16[64,1536]{1,0:T(8,128)(2,1)S(1)}, u32[]{:S(2)}, u32[]{:S(2)}) collective-permute-start(bf16[64,1536]{1,0:T(8,128)(2,1)S(1)} %side_sum.2), channel_id=1, source_target_pairs={{0,8},{4,12},{8,0},{12,4},{16,24},{20,28},{24,16},{28,20},{1,9},{5... | collective-permute-start | bytes 589832 | tf_op jit(solution)/shard_map/ppermute | solution.py:259
  148.3 5.8 %collective-permute-done.26.right_ref = bf16[64,1536]{1,0:T(8,128)(2,1)S(1)} collective-permute-done((bf16[64,1536]{1,0:T(8,128)(2,1)S(1)}, bf16[64,1536]{1,0:T(8,128)(2,1)S(1)}, u32[]{:S(2)}, u32[]{:S(2)}) %collective-permute-start.26) | collective-permute-done | bytes 196640 | tf_op jit(solution)/shard_map/ppermute | solution.py:259
  164.0 9.5 %collective-permute-done.30.n1 = bf16[64,3072]{1,0:T(8,128)(2,1)S(1)} collective-permute-done((bf16[64,3072]{1,0:T(8,128)(2,1)S(1)}, bf16[64,3072]{1,0:T(8,128)(2,1)S(1)}, u32[]{:S(2)}, u32[]{:S(2)}) %collective-permute-start.30) | collective-permute-done | bytes 393248 | tf_op jit(solution)/shard_map/ppermute | solution.py:259
  178.9 10.2 %collective-permute-done.34.refs_3_ = bf16[8,64,384]{2,1,0:T(8,128)(2,1)S(1)} collective-permute-done((bf16[8,64,384]{2,1,0:T(8,128)(2,1)S(1)}, bf16[8,64,384]{2,1,0:T(8,128)(2,1)S(1)}, u32[]{:S(2)}, u32[]{:S(2)}) %collective-permute-start.34) | collective-permute-done | bytes 393248 | tf_op jit(solution)/shard_map/ppermute | solution.py:259
  189.2 8.1 %score_hidden.1 = (bf16[256,1536]{1,0:T(8,128)(2,1)S(1)}, bf16[256,1536]{1,0:T(8,128)(2,1)S(1)}) custom-call(bf16[256,3072]{1,0:T(8,128)(2,1)S(1)} %get-tuple-element.153.t_in, bf16[256,3072]{1,0:T(8,128)(2,1)S(1)} %get-tuple-element.154.c_in, bf16[3072,1536]{1,0:T(8,128)(2,1)S(1)} %bitcast.90, bf16[3072,1536]{1,0:T(8,128)(2,1)S(1)} %bitcast.92), custom_call_target="tpu_custom_call" | custom-call | flops 4831838208 | bytes 18874368 | tf_op jit(solution)/shard_map/score_hidden/pallas_call | solution.py:562
  201.5 10.3 %score_gap.1 = (f32[128,3072]{1,0:T(8,128)S(1)}, bf16[128,3072]{1,0:T(8,128)(2,1)S(1)}) custom-call(s32[4]{0:T(128)S(1)} %pad_add_fusion.s, bf16[256,1536]{1,0:T(8,128)(2,1)S(1)} %get-tuple-element.162.t_h, bf16[256,1536]{1,0:T(8,128)(2,1)S(1)} %get-tuple-element.163.c_h, bf16[1536,3072]{1,0:T(8,128)(2,1)S(1)} %bitcast.86, bf16[1536,3072]{1,0:T(8,128)(2,1)S(1)} %bitcast.88, ...), custom_call_target="tpu_custom_call" | custom-call | flops 4831838208 | bytes 18874368 | tf_op jit(solution)/shard_map/score_gap/pallas_call | solution.py:591
  211.9 9.6 %collective-permute-done.37.refs_1_ = bf16[512,768]{1,0:T(8,128)(2,1)S(1)} collective-permute-done((bf16[512,768]{1,0:T(8,128)(2,1)S(1)}, bf16[512,768]{1,0:T(8,128)(2,1)S(1)}, u32[]{:S(2)}, u32[]{:S(2)}) %collective-permute-start.37) | collective-permute-done | bytes 786464 | tf_op jit(solution)/shard_map/ppermute | solution.py:271
  226.6 9.4 %collective-permute-done.40.got_ref = bf16[64,3072]{1,0:T(8,128)(2,1)S(1)} collective-permute-done((bf16[64,3072]{1,0:T(8,128)(2,1)S(1)}, bf16[64,3072]{1,0:T(8,128)(2,1)S(1)}, u32[]{:S(2)}, u32[]{:S(2)}) %collective-permute-start.40) | collective-permute-done | bytes 393248 | tf_op jit(solution)/shard_map/ppermute | solution.py:259
  240.6 8.0 %collective-permute-done.44.refs_3_ = bf16[512,768]{1,0:T(8,128)(2,1)S(1)} collective-permute-done((bf16[512,768]{1,0:T(8,128)(2,1)S(1)}, bf16[512,768]{1,0:T(8,128)(2,1)S(1)}, u32[]{:S(2)}, u32[]{:S(2)}) %collective-permute-start.44) | collective-permute-done | bytes 786464 | tf_op jit(solution)/shard_map/ppermute | solution.py:271
  248.6 7.4 %collective-permute-done.43 = bf16[1,4,64,384]{3,2,0,1:T(8,128)(2,1)S(1)} collective-permute-done((bf16[1,4,64,384]{3,2,0,1:T(8,128)(2,1)S(1)}, bf16[1,4,64,384]{3,2,0,1:T(8,128)(2,1)S(1)}, u32[]{:S(2)}, u32[]{:S(2)}) %collective-permute-start.43) | collective-permute-done | bytes 196640 | tf_op jit(solution)/shard_map/ppermute | solution.py:259
  262.2 5.1 %collective-permute-done.49 = bf16[2,2,64,384]{3,2,0,1:T(8,128)(2,1)S(1)} collective-permute-done((bf16[2,2,64,384]{3,2,0,1:T(8,128)(2,1)S(1)}, bf16[2,2,64,384]{3,2,0,1:T(8,128)(2,1)S(1)}, u32[]{:S(2)}, u32[]{:S(2)}) %collective-permute-start.49) | collective-permute-done | bytes 196640 | tf_op jit(solution)/shard_map/ppermute | solution.py:259
  272.9 4.1 %rows_grad.1.refs_0_ = bf16[512,768]{1,0:T(8,128)(2,1)S(1)} custom-call(bf16[64,3072]{1,0:T(8,128)(2,1)S(1)} %get-tuple-element.170.refs_0_, bf16[64,3072]{1,0:T(8,128)(2,1)S(1)} %get-tuple-element.173.refs_1_, bf16[64,3072]{1,0:T(8,128)(2,1)S(1)} %collective-permute-done.46.refs_2_, bf16[64,3072]{1,0:T(8,128)(2,1)S(1)} %collective-permute-done.47.refs_3_, ...), custom_call_target="tpu_custom_call" | custom-call | flops 2415919104 | bytes 10000000 | tf_op jit(solution)/shard_map/rows_grad/pallas_call | solution.py:679
  283.9 19.7 %collective-permute-done.55 = bf16[4,1,64,384]{3,2,0,1:T(8,128)(2,1)S(1)} collective-permute-done((bf16[4,1,64,384]{3,2,0,1:T(8,128)(2,1)S(1)}, bf16[4,1,64,384]{3,2,0,1:T(8,128)(2,1)S(1)}, u32[]{:S(2)}, u32[]{:S(2)}) %collective-permute-start.55) | collective-permute-done | bytes 196640 | tf_op jit(solution)/shard_map/ppermute | solution.py:259
  314.7 10.0 %collective-permute-done.56.refs_0_ = bf16[512,768]{1,0:T(8,128)(2,1)} collective-permute-done((bf16[512,768]{1,0:T(8,128)(2,1)}, bf16[512,768]{1,0:T(8,128)(2,1)}, u32[]{:S(2)}, u32[]{:S(2)}) %collective-permute-start.56) | collective-permute-done | bytes 786464 | tf_op jit(solution)/shard_map/ppermute | solution.py:271
  333.8 8.5 %collective-permute-done.61.refs_0_ = bf16[512,768]{1,0:T(8,128)(2,1)S(1)} collective-permute-done((bf16[512,768]{1,0:T(8,128)(2,1)}, bf16[512,768]{1,0:T(8,128)(2,1)S(1)}, u32[]{:S(2)}, u32[]{:S(2)}) %collective-permute-start.61) | collective-permute-done | bytes 786464 | tf_op jit(solution)/shard_map/ppermute | solution.py:271
  351.6 5.1 %collective-permute-done.64 = bf16[256,768]{1,0:T(8,128)(2,1)S(1)} collective-permute-done((bf16[256,768]{1,0:T(8,128)(2,1)S(1)}, bf16[256,768]{1,0:T(8,128)(2,1)S(1)}, u32[]{:S(2)}, u32[]{:S(2)}) %collective-permute-start.64) | collective-permute-done | bytes 393248 | tf_op jit(solution)/shard_map/ppermute | solution.py:271
  (273 shorter events, 129.6 us)
Async XLA Ops:
  2.9 29.2 %collective-permute-start = (bf16[384,768]{1,0:T(8,128)(2,1)}, bf16[384,768]{1,0:T(8,128)(2,1)S(1)}, u32[]{:S(2)}, u32[]{:S(2)}) collective-permute-start(bf16[384,768]{1,0:T(8,128)(2,1)} %get-tuple-element.202), channel_id=1, source_target_pairs={{0,8},{4,12},{8,0},{12,4},{16,24},{20,28},{24,16},{28,20},{1,9},{5... | collective-permute-start | bytes 1769480 | tf_op jit(solution)/shard_map/ppermute | solution.py:259
  6.0 26.2 %collective-permute-start.1 = (bf16[384,768]{1,0:T(8,128)(2,1)S(1)}, bf16[384,768]{1,0:T(8,128)(2,1)S(1)}, u32[]{:S(2)}, u32[]{:S(2)}) collective-permute-start(bf16[384,768]{1,0:T(8,128)(2,1)S(1)} %get-tuple-element.201.refs_0_), channel_id=1, source_target_pairs={{0,16},{4,20},{8,24},{12,28},{16,0},{20,4},{24,8},{28,12},{1,17},{... | collective-permute-start | bytes 1769480 | tf_op jit(solution)/shard_map/ppermute | solution.py:259
  8.6 23.6 %collective-permute-start.2 = (bf16[384,768]{1,0:T(8,128)(2,1)S(1)}, bf16[384,768]{1,0:T(8,128)(2,1)}, u32[]{:S(2)}, u32[]{:S(2)}) collective-permute-start(bf16[384,768]{1,0:T(8,128)(2,1)S(1)} %get-tuple-element.201.refs_0_), channel_id=1, source_target_pairs={{0,4},{4,0},{8,12},{12,8},{16,20},{20,16},{24,28},{28,24},{1,5},{5... | collective-permute-start | bytes 1769480 | tf_op jit(solution)/shard_map/ppermute | solution.py:259
  32.2 28.2 %collective-permute-start.3 = (bf16[384,768]{1,0:T(8,128)(2,1)S(1)}, bf16[384,768]{1,0:T(8,128)(2,1)S(1)}, u32[]{:S(2)}, u32[]{:S(2)}) collective-permute-start(bf16[384,768]{1,0:T(8,128)(2,1)S(1)} %get-tuple-element.103.refs_2_), channel_id=1, source_target_pairs={{0,16},{4,20},{8,24},{12,28},{16,0},{20,4},{24,8},{28,12},{1,17},{... | collective-permute-start | bytes 1769480 | tf_op jit(solution)/shard_map/ppermute | solution.py:259
  34.9 25.5 %collective-permute-start.4 = (bf16[384,768]{1,0:T(8,128)(2,1)S(1)}, bf16[384,768]{1,0:T(8,128)(2,1)S(1)}, u32[]{:S(2)}, u32[]{:S(2)}) collective-permute-start(bf16[384,768]{1,0:T(8,128)(2,1)S(1)} %get-tuple-element.103.refs_2_), channel_id=1, source_target_pairs={{0,4},{4,0},{8,12},{12,8},{16,20},{20,16},{24,28},{28,24},{1,5},{5... | collective-permute-start | bytes 1769480 | tf_op jit(solution)/shard_map/ppermute | solution.py:259
  36.4 25.0 %collective-permute-start.5 = (bf16[384,768]{1,0:T(8,128)(2,1)S(1)}, bf16[384,768]{1,0:T(8,128)(2,1)S(1)}, u32[]{:S(2)}, u32[]{:S(2)}) collective-permute-start(bf16[384,768]{1,0:T(8,128)(2,1)S(1)} %get-tuple-element.104.refs_4_), channel_id=1, source_target_pairs={{0,4},{4,0},{8,12},{12,8},{16,20},{20,16},{24,28},{28,24},{1,5},{5... | collective-permute-start | bytes 1769480 | tf_op jit(solution)/shard_map/ppermute | solution.py:259
  36.9 32.6 %collective-permute-start.6 = (bf16[768,384]{1,0:T(8,128)(2,1)S(1)}, bf16[768,384]{1,0:T(8,128)(2,1)S(1)}, u32[]{:S(2)}, u32[]{:S(2)}) collective-permute-start(bf16[768,384]{1,0:T(8,128)(2,1)S(1)} %get-tuple-element.105), channel_id=1, source_target_pairs={{0,8},{4,12},{8,0},{12,4},{16,24},{20,28},{24,16},{28,20},{1,9},{5... | collective-permute-start | bytes 1769480 | tf_op jit(solution)/shard_map/ppermute | solution.py:259
  39.4 36.3 %collective-permute-start.13 = (bf16[64,3072]{1,0:T(8,128)(2,1)S(1)}, bf16[64,3072]{1,0:T(8,128)(2,1)S(1)}, u32[]{:S(2)}, u32[]{:S(2)}) collective-permute-start(bf16[64,3072]{1,0:T(8,128)(2,1)S(1)} %slice.57), channel_id=1, source_target_pairs={{0,8},{4,12},{8,0},{12,4},{16,24},{20,28},{24,16},{28,20},{1,9},{5... | collective-permute-start | bytes 1179656 | tf_op jit(solution)/shard_map/ppermute | solution.py:259
  72.1 25.6 %collective-permute-start.8 = (bf16[768,384]{1,0:T(8,128)(2,1)S(1)}, bf16[768,384]{1,0:T(8,128)(2,1)S(1)}, u32[]{:S(2)}, u32[]{:S(2)}) collective-permute-start(bf16[768,384]{1,0:T(8,128)(2,1)S(1)} %get-tuple-element.108.refs_0_.refs_8_), channel_id=1, source_target_pairs={{0,16},{4,20},{8,24},{12,28},{16,0},{20,4},{24,8},{28,12},{1,17},{... | collective-permute-start | bytes 1769480 | tf_op jit(solution)/shard_map/ppermute | solution.py:259
  72.1 25.6 %collective-permute-start.9 = (bf16[768,384]{1,0:T(8,128)(2,1)S(1)}, bf16[768,384]{1,0:T(8,128)(2,1)S(1)}, u32[]{:S(2)}, u32[]{:S(2)}) collective-permute-start(bf16[768,384]{1,0:T(8,128)(2,1)S(1)} %get-tuple-element.108.refs_0_.refs_8_), channel_id=1, source_target_pairs={{0,4},{4,0},{8,12},{12,8},{16,20},{20,16},{24,28},{28,24},{1,5},{5... | collective-permute-start | bytes 1769480 | tf_op jit(solution)/shard_map/ppermute | solution.py:259
  77.1 22.7 %collective-permute-start.15 = (bf16[64,3072]{1,0:T(8,128)(2,1)S(1)}, bf16[64,3072]{1,0:T(8,128)(2,1)S(1)}, u32[]{:S(2)}, u32[]{:S(2)}) collective-permute-start(bf16[64,3072]{1,0:T(8,128)(2,1)S(1)} %collective-permute-done.13.p0), channel_id=1, source_target_pairs={{0,1},{1,0},{2,3},{3,2},{4,5},{5,4},{6,7},{7,6},{8,9},{9,8},{10,11... | collective-permute-start | bytes 1179656 | tf_op jit(solution)/shard_map/ppermute | solution.py:259
  139.8 21.8 %collective-permute-start.28 = (bf16[512,768]{1,0:T(8,128)(2,1)S(1)}, bf16[512,768]{1,0:T(8,128)(2,1)S(1)}, u32[]{:S(2)}, u32[]{:S(2)}) collective-permute-start(bf16[512,768]{1,0:T(8,128)(2,1)S(1)} %get-tuple-element.134.hidden_ref.refs_1_), channel_id=1, source_target_pairs={{0,4},{4,0},{8,12},{12,8},{16,20},{20,16},{24,28},{28,24},{1,5},{5... | collective-permute-start | bytes 2359304 | tf_op jit(solution)/shard_map/ppermute | solution.py:259
  178.5 21.1 %collective-permute-start.33 = (bf16[512,768]{1,0:T(8,128)(2,1)S(1)}, bf16[512,768]{1,0:T(8,128)(2,1)S(1)}, u32[]{:S(2)}, u32[]{:S(2)}) collective-permute-start(bf16[512,768]{1,0:T(8,128)(2,1)S(1)} %get-tuple-element.156), channel_id=1, source_target_pairs={{0,8},{4,12},{8,16},{12,20},{16,24},{20,28},{24,0},{28,4},{1,9},{5... | collective-permute-start | bytes 2359304 | tf_op jit(solution)/shard_map/ppermute | solution.py:271
  178.9 20.7 %collective-permute-start.35 = (bf16[8,64,384]{2,1,0:T(8,128)(2,1)S(1)}, bf16[8,64,384]{2,1,0:T(8,128)(2,1)S(1)}, u32[]{:S(2)}, u32[]{:S(2)}) collective-permute-start(bf16[8,64,384]{2,1,0:T(8,128)(2,1)S(1)} %maximum_bitcast_fusion.refs_2_), channel_id=1, source_target_pairs={{0,1},{1,0},{2,3},{3,2},{4,5},{5,4},{6,7},{7,6},{8,9},{9,8},{10,11... | collective-permute-start | bytes 1179656 | tf_op jit(solution)/shard_map/ppermute | solution.py:259
  201.2 20.2 %collective-permute-start.37 = (bf16[512,768]{1,0:T(8,128)(2,1)S(1)}, bf16[512,768]{1,0:T(8,128)(2,1)S(1)}, u32[]{:S(2)}, u32[]{:S(2)}) collective-permute-start(bf16[512,768]{1,0:T(8,128)(2,1)S(1)} %get-tuple-element.166), channel_id=1, source_target_pairs={{0,8},{4,12},{8,16},{12,20},{16,24},{20,28},{24,0},{28,4},{1,9},{5... | collective-permute-start | bytes 2359304 | tf_op jit(solution)/shard_map/ppermute | solution.py:271
  201.2 20.2 %collective-permute-start.38 = (bf16[512,768]{1,0:T(8,128)(2,1)S(1)}, bf16[512,768]{1,0:T(8,128)(2,1)S(1)}, u32[]{:S(2)}, u32[]{:S(2)}) collective-permute-start(bf16[512,768]{1,0:T(8,128)(2,1)S(1)} %get-tuple-element.166), channel_id=1, source_target_pairs={{0,4},{4,0},{8,12},{12,8},{16,20},{20,16},{24,28},{28,24},{1,5},{5... | collective-permute-start | bytes 2359304 | tf_op jit(solution)/shard_map/ppermute | solution.py:259
  226.3 22.4 %collective-permute-start.44 = (bf16[512,768]{1,0:T(8,128)(2,1)S(1)}, bf16[512,768]{1,0:T(8,128)(2,1)S(1)}, u32[]{:S(2)}, u32[]{:S(2)}) collective-permute-start(bf16[512,768]{1,0:T(8,128)(2,1)S(1)} %get-tuple-element.172), channel_id=1, source_target_pairs={{0,8},{4,12},{8,16},{12,20},{16,24},{20,28},{24,0},{28,4},{1,9},{5... | collective-permute-start | bytes 2359304 | tf_op jit(solution)/shard_map/ppermute | solution.py:271
  226.3 22.4 %collective-permute-start.45 = (bf16[512,768]{1,0:T(8,128)(2,1)S(1)}, bf16[512,768]{1,0:T(8,128)(2,1)S(1)}, u32[]{:S(2)}, u32[]{:S(2)}) collective-permute-start(bf16[512,768]{1,0:T(8,128)(2,1)S(1)} %get-tuple-element.172), channel_id=1, source_target_pairs={{0,4},{4,0},{8,12},{12,8},{16,20},{20,16},{24,28},{28,24},{1,5},{5... | collective-permute-start | bytes 2359304 | tf_op jit(solution)/shard_map/ppermute | solution.py:259
  236.6 23.4 %collective-permute-start.41 = (bf16[64,3072]{1,0:T(8,128)(2,1)S(1)}, bf16[64,3072]{1,0:T(8,128)(2,1)S(1)}, u32[]{:S(2)}, u32[]{:S(2)}) collective-permute-start(bf16[64,3072]{1,0:T(8,128)(2,1)S(1)} %get-tuple-element.170.refs_0_), channel_id=1, source_target_pairs={{0,8},{4,12},{8,0},{12,4},{16,24},{20,28},{24,16},{28,20},{1,9},{5... | collective-permute-start | bytes 1179656 | tf_op jit(solution)/shard_map/ppermute | solution.py:259
  236.7 23.3 %collective-permute-start.42 = (bf16[64,3072]{1,0:T(8,128)(2,1)S(1)}, bf16[64,3072]{1,0:T(8,128)(2,1)S(1)}, u32[]{:S(2)}, u32[]{:S(2)}) collective-permute-start(bf16[64,3072]{1,0:T(8,128)(2,1)S(1)} %get-tuple-element.170.refs_0_), channel_id=1, source_target_pairs={{0,2},{1,3},{2,0},{3,1},{4,6},{5,7},{6,4},{7,5},{8,10},{9,11},{10,... | collective-permute-start | bytes 1179656 | tf_op jit(solution)/shard_map/ppermute | solution.py:259
  280.0 23.6 %collective-permute-start.53 = (bf16[512,768]{1,0:T(8,128)(2,1)S(1)}, bf16[512,768]{1,0:T(8,128)(2,1)}, u32[]{:S(2)}, u32[]{:S(2)}) collective-permute-start(bf16[512,768]{1,0:T(8,128)(2,1)S(1)} %get-tuple-element.180), channel_id=1, source_target_pairs={{0,8},{4,12},{8,16},{12,20},{16,24},{20,28},{24,0},{28,4},{1,9},{5... | collective-permute-start | bytes 2359304 | tf_op jit(solution)/shard_map/ppermute | solution.py:271
  281.7 21.9 %collective-permute-start.54 = (bf16[512,768]{1,0:T(8,128)(2,1)S(1)}, bf16[512,768]{1,0:T(8,128)(2,1)S(1)}, u32[]{:S(2)}, u32[]{:S(2)}) collective-permute-start(bf16[512,768]{1,0:T(8,128)(2,1)S(1)} %get-tuple-element.180), channel_id=1, source_target_pairs={{0,4},{4,0},{8,12},{12,8},{16,20},{20,16},{24,28},{28,24},{1,5},{5... | collective-permute-start | bytes 2359304 | tf_op jit(solution)/shard_map/ppermute | solution.py:259
  282.1 21.5 %collective-permute-start.55 = (bf16[4,1,64,384]{3,2,0,1:T(8,128)(2,1)S(1)}, bf16[4,1,64,384]{3,2,0,1:T(8,128)(2,1)S(1)}, u32[]{:S(2)}, u32[]{:S(2)}) collective-permute-start(bf16[4,1,64,384]{3,2,0,1:T(8,128)(2,1)S(1)} %get-tuple-element.204), channel_id=1, source_target_pairs={{0,4},{4,0},{8,12},{12,8},{16,20},{20,16},{24,28},{28,24},{1,5},{5... | collective-permute-start | bytes 589832 | tf_op jit(solution)/shard_map/ppermute | solution.py:259
  306.1 18.6 %collective-permute-start.56 = (bf16[512,768]{1,0:T(8,128)(2,1)}, bf16[512,768]{1,0:T(8,128)(2,1)}, u32[]{:S(2)}, u32[]{:S(2)}) collective-permute-start(bf16[512,768]{1,0:T(8,128)(2,1)} %get-tuple-element.182), channel_id=1, source_target_pairs={{0,8},{4,12},{8,16},{12,20},{16,24},{20,28},{24,0},{28,4},{1,9},{5... | collective-permute-start | bytes 2359304 | tf_op jit(solution)/shard_map/ppermute | solution.py:271
  (86 other events, 1017.9 us)

commit v4 on v3

--- a/solution.py
+++ b/solution.py
@@ -487,14 +487,11 @@
             down[pair | far | swap], gen_hidden, arrived, *left_terms
         )
         left_sum = branch_sum(*left_terms)
-        hidden_near, hidden_across = [gen_hidden], [hop(gen_hidden, "grp", swap)]
+        hidden_near = [gen_hidden, ring(gen_hidden)]
+        hidden_across = [hop(gen_hidden, "grp", swap)]
         input_blocks = with_arrived(input_blocks, arrived)
         arrived = send_blocks(input_blocks, pair)
-        right_terms = branch_core(1, gen_hidden)
-        arrived, *right_terms = settle(arrived, *right_terms)
-        right_sum = branch_sum(*right_terms)
-        input_blocks = with_arrived(input_blocks, arrived)
-        arrived = send_blocks(input_blocks, swap)
+        right_sum = branch_sum(*branch_core(1, gen_hidden))
 
         def latent_body(s, noise_ref, diff_ref, mod_ref, *refs):
             sums, (generated_ref, noised_ref) = refs[:6], refs[6:]
@@ -526,10 +523,13 @@
             name="latent",
         )
 
-        noised, hidden_near[0], hidden_across[0], arrived = settle(
-            noised, hidden_near[0], hidden_across[0], arrived
-        )
-        hidden_near.append(ring(hidden_near[0]))
+        noised, hidden_near[1], hidden_across[0], arrived = settle(
+            noised, hidden_near[1], hidden_across[0], arrived
+        )
+        hidden_near.append(ring(hidden_near[1]))
+        hidden_across.append(hop(hidden_near[1], "grp", swap))
+        input_blocks = with_arrived(input_blocks, arrived)
+        arrived = send_blocks(input_blocks, swap)
 
         def score_input_body(s, n0, n1, n2, n3, teacher_ref, critic_ref, t_ref, c_ref):
             for k, part_ref in enumerate((n0, n1, n2, n3)):
@@ -549,8 +549,6 @@
             name="score_input",
         )
 
-        teacher_in, arrived = settle(teacher_in, arrived)
-        input_tokens = gather_tokens(with_arrived(input_blocks, arrived)[:, 0])
 
         tile = 256
 
@@ -574,11 +572,13 @@
             name="score_hidden",
         )(teacher_in, critic_in, teacher_up, critic_up)
 
-        teacher_hidden, hidden_near[1], *input_tokens = settle(
-            teacher_hidden, hidden_near[1], *input_tokens
-        )
-        hidden_near.append(ring(hidden_near[1]))
-        hidden_across.append(hop(hidden_near[1], "grp", swap))
+        teacher_hidden, hidden_near[2], hidden_across[1], arrived = settle(
+            teacher_hidden, hidden_near[2], hidden_across[1], arrived
+        )
+        hidden_near.append(ring(hidden_near[2]))
+        hidden_across.append(hop(hidden_near[2], "grp", swap))
+        input_tokens = [with_arrived(input_blocks, arrived)[:, 0]]
+        input_tokens.append(hop(input_tokens[0], "tp", side))
 
         def gap_body(s, t_h, c_h, t_w, c_w, t_mod, c_mod, keep_ref, send_ref):
             values = t_mod[s[2], 2:3] * dot(t_h[...], t_w[...]) - c_mod[s[2], 2:3] * dot(
@@ -605,11 +605,8 @@
             name="score_gap",
         )(scalars, teacher_hidden, critic_hidden, teacher_down, critic_down, teacher_mod, critic_mod)
 
-        send, hidden_near[2], hidden_across[1] = settle(
-            send, hidden_near[2], hidden_across[1]
-        )
-        hidden_near.append(ring(hidden_near[2]))
-        hidden_across.append(hop(hidden_near[2], "grp", swap))
+        send, *input_tokens = settle(send, *input_tokens)
+        input_tokens += [hop(values, "tp", core) for values in input_tokens]
 
         def gap_core_body(keep_ref, got_ref, send_ref, rest_ref):
             send_ref[...] = (keep_ref[rows:, :] + got_ref[rows:, :].astype(f32)).astype(bf16)
@@ -642,14 +639,14 @@
             name="branch_grad",
         )
 
-        grad_blocks = grad_blocks[None]
+        branch_grad, grad_blocks, hidden_near[3], hidden_across[2] = settle(
+            branch_grad, grad_blocks[None], hidden_near[3], hidden_across[2]
+        )
+        hidden_across.append(hop(hidden_near[3], "grp", swap))
         pair_grad = hop(branch_grad, "grp", pair)
         crossed = hop(branch_grad, "tp", side)
         arrived = send_blocks(grad_blocks, far)
-        pair_grad, crossed, arrived, hidden_near[3], hidden_across[2] = settle(
-            pair_grad, crossed, arrived, hidden_near[3], hidden_across[2]
-        )
-        hidden_across.append(hop(hidden_near[3], "grp", swap))
+        pair_grad, crossed, arrived = settle(pair_grad, crossed, arrived)
         pair_crossed = hop(pair_grad, "tp", side)
         own_tokens = [branch_grad, crossed]
         own_tokens += [hop(values, "tp", core) for values in own_tokens]

time: 361 us -> 344 us (0.953)
  waiting for transfers between devices: 235 us -> 207 us
  starting transfers between devices: 54.7 us -> 68.6 us
  local copies, waits for them, and re-layouts: 12.9 us -> 8.74 us
    ppermute x7, waiting for transfers between devices: 43.5 us -> 26.2 us  [ring(): return lax.ppermute(values, 'grp', ring_pairs)]
    ppermute x58, waiting for transfers between devices: 191 us -> 181 us  [hop(): return lax.ppermute(values, axis, [(i, i ^ mask) for i in range(size)])]
    ppermute x7, starting transfers between devices: 2.43 us -> 9.77 us  [ring(): return lax.ppermute(values, 'grp', ring_pairs)]
    ppermute x58, starting transfers between devices: 52.3 us -> 58.8 us  [hop(): return lax.ppermute(values, axis, [(i, i ^ mask) for i in range(size)])]
    unnamed x92 -> x68, local copies, waits for them, and re-layouts: 10.3 us -> 4.63 us
  transfers between devices with their start and end apart: 65 -> 65, of which waited for: 36 -> 33; matrix products, arithmetic and copies ran while one was open for 4% -> 4% of each run, Pallas kernels for 9% -> 11%
where the time goes in v4:
time: 344 us
  waiting for transfers between devices  207 us (60%)
  starting transfers between devices  68.6 us (20%)
  Pallas kernels  41.1 us (12%)
  matrix products  12.7 us (4%)
  local copies, waits for them, and re-layouts  8.74 us (3%)
  other arithmetic  3.6 us (1%)
    ppermute x58, waiting for transfers between devices, hop(): return lax.ppermute(values, axis, [(i, i ^ mask) for i in range(size)])  181 us
    ppermute x58, starting transfers between devices, hop(): return lax.ppermute(values, axis, [(i, i ^ mask) for i in range(size)])  58.8 us
    ppermute x7, waiting for transfers between devices, ring(): return lax.ppermute(values, 'grp', ring_pairs)  26.2 us
    pallas_call x14, Pallas kernels, kernel_call(): pl.pallas_call(body, out_shape=tuple(out_shapes), in_specs=specs, out_spe...  18.5 us
    dot_general x17, matrix products, dot(): lax.dot_general(left, right, (contract, ((), ())), preferred_element_type...  12.7 us
    pallas_call x1, Pallas kernels, per_device(): pl.pallas_call(gap_body, grid=(width // tile,), in_specs=[pl.BlockSpec(me...  10.3 us
    ppermute x7, starting transfers between devices, ring(): return lax.ppermute(values, 'grp', ring_pairs)  9.77 us
    pallas_call x1, Pallas kernels, per_device(): pl.pallas_call(hidden_body, grid=(score_units // tile,), in_specs=[whole,...  8.23 us
  transfers between devices with their start and end apart: 65, of which 33 were waited for; matrix products, arithmetic and copies ran while one was open for 4% of the time, Pallas kernels for 11%

profile of v4, /device:TPU:0, one launch (start us, length us, event | category | flops | bytes accessed | tf_op | source)
XLA Modules:
  0.0 343.6 jit_solution(10612516115207695152)
XLA Ops:
  14.1 18.2 %collective-permute-done.refs_0_ = bf16[384,768]{1,0:T(8,128)(2,1)} collective-permute-done((bf16[384,768]{1,0:T(8,128)(2,1)}, bf16[384,768]{1,0:T(8,128)(2,1)}, u32[]{:S(2)}, u32[]{:S(2)}) %collective-permute-start) | collective-permute-done | bytes 589856 | tf_op jit(solution)/shard_map/ppermute | solution.py:259
  40.0 20.7 %collective-permute-done.3.refs_0_ = bf16[384,768]{1,0:T(8,128)(2,1)S(1)} collective-permute-done((bf16[384,768]{1,0:T(8,128)(2,1)}, bf16[384,768]{1,0:T(8,128)(2,1)S(1)}, u32[]{:S(2)}, u32[]{:S(2)}) %collective-permute-start.3) | collective-permute-done | bytes 589856 | tf_op jit(solution)/shard_map/ppermute | solution.py:259
  61.9 7.8 %collective-permute-done.6.refs_3_ = bf16[768,384]{1,0:T(8,128)(2,1)S(1)} collective-permute-done((bf16[768,384]{1,0:T(8,128)(2,1)S(1)}, bf16[768,384]{1,0:T(8,128)(2,1)S(1)}, u32[]{:S(2)}, u32[]{:S(2)}) %collective-permute-start.6) | collective-permute-done | bytes 589856 | tf_op jit(solution)/shard_map/ppermute | solution.py:259
  77.2 6.4 %collective-permute-done.14.p1 = bf16[64,3072]{1,0:T(8,128)(2,1)S(1)} collective-permute-done((bf16[64,3072]{1,0:T(8,128)(2,1)S(1)}, bf16[64,3072]{1,0:T(8,128)(2,1)S(1)}, u32[]{:S(2)}, u32[]{:S(2)}) %collective-permute-start.14) | collective-permute-done | bytes 393248 | tf_op jit(solution)/shard_map/ppermute | solution.py:259
  83.6 15.1 %collective-permute-done.8.refs_2_ = bf16[768,384]{1,0:T(8,128)(2,1)S(1)} collective-permute-done((bf16[768,384]{1,0:T(8,128)(2,1)S(1)}, bf16[768,384]{1,0:T(8,128)(2,1)S(1)}, u32[]{:S(2)}, u32[]{:S(2)}) %collective-permute-start.8) | collective-permute-done | bytes 589856 | tf_op jit(solution)/shard_map/ppermute | solution.py:259
  100.8 5.3 %pre.1 = (f32[512,768]{1,0:T(8,128)S(1)}, bf16[512,768]{1,0:T(8,128)(2,1)S(1)}) custom-call(s32[4]{0:T(128)S(1)} %pad_add_fusion.s, bf16[256,3072]{1,0:T(8,128)(2,1)S(1)} %get-tuple-element.104.rows_ref, bf16[64,3072]{1,0:T(8,128)(2,1)S(1)} %collective-permute-done.13.p0, bf16[64,3072]{1,0:T(8,128)(2,1)S(1)} %collective-permute-done.14.p1, ...), custom_call_target="tpu_custom_call" | custom-call | flops 2415919104 | bytes 10223632 | tf_op jit(solution)/shard_map/pre/pallas_call | solution.py:225
  106.1 9.2 %collective-permute-done.10.refs_0_ = bf16[768,384]{1,0:T(8,128)(2,1)S(1)} collective-permute-done((bf16[768,384]{1,0:T(8,128)(2,1)S(1)}, bf16[768,384]{1,0:T(8,128)(2,1)S(1)}, u32[]{:S(2)}, u32[]{:S(2)}) %collective-permute-start.10) | collective-permute-done | bytes 589856 | tf_op jit(solution)/shard_map/ppermute | solution.py:259
  121.6 9.4 %collective-permute-done.18.refs_2_ = bf16[1,4,64,384]{3,2,1,0:T(8,128)(2,1)S(1)} collective-permute-done((bf16[1,4,64,384]{3,2,1,0:T(8,128)(2,1)S(1)}, bf16[1,4,64,384]{3,2,1,0:T(8,128)(2,1)S(1)}, u32[]{:S(2)}, u32[]{:S(2)}) %collective-permute-start.18) | collective-permute-done | bytes 196640 | tf_op jit(solution)/shard_map/ppermute | solution.py:259
  142.2 3.2 collective-permute-done.21.right_ref
  151.9 9.1 %collective-permute-done.29 = bf16[2,2,64,384]{3,2,0,1:T(8,128)(2,1)S(1)} collective-permute-done((bf16[2,2,64,384]{3,2,0,1:T(8,128)(2,1)S(1)}, bf16[2,2,64,384]{3,2,0,1:T(8,128)(2,1)S(1)}, u32[]{:S(2)}, u32[]{:S(2)}) %collective-permute-start.29) | collective-permute-done | bytes 196640 | tf_op jit(solution)/shard_map/ppermute | solution.py:259
  175.2 6.7 %collective-permute-done.30.n1 = bf16[64,3072]{1,0:T(8,128)(2,1)S(1)} collective-permute-done((bf16[64,3072]{1,0:T(8,128)(2,1)S(1)}, bf16[64,3072]{1,0:T(8,128)(2,1)S(1)}, u32[]{:S(2)}, u32[]{:S(2)}) %collective-permute-start.30) | collective-permute-done | bytes 393248 | tf_op jit(solution)/shard_map/ppermute | solution.py:259
  186.3 8.2 %score_hidden.1 = (bf16[256,1536]{1,0:T(8,128)(2,1)S(1)}, bf16[256,1536]{1,0:T(8,128)(2,1)S(1)}) custom-call(bf16[256,3072]{1,0:T(8,128)(2,1)S(1)} %get-tuple-element.139.t_in, bf16[256,3072]{1,0:T(8,128)(2,1)S(1)} %get-tuple-element.140.c_in, bf16[3072,1536]{1,0:T(8,128)(2,1)S(1)} %bitcast.90, bf16[3072,1536]{1,0:T(8,128)(2,1)S(1)} %bitcast.92), custom_call_target="tpu_custom_call" | custom-call | flops 4831838208 | bytes 18874368 | tf_op jit(solution)/shard_map/score_hidden/pallas_call | solution.py:560
  194.6 3.1 collective-permute-done.35
  199.1 10.3 %score_gap.1 = (f32[128,3072]{1,0:T(8,128)S(1)}, bf16[128,3072]{1,0:T(8,128)(2,1)S(1)}) custom-call(s32[4]{0:T(128)S(1)} %pad_add_fusion.s, bf16[256,1536]{1,0:T(8,128)(2,1)S(1)} %get-tuple-element.144.t_h, bf16[256,1536]{1,0:T(8,128)(2,1)S(1)} %get-tuple-element.145.c_h, bf16[1536,3072]{1,0:T(8,128)(2,1)S(1)} %bitcast.86, bf16[1536,3072]{1,0:T(8,128)(2,1)S(1)} %bitcast.88, ...), custom_call_target="tpu_custom_call" | custom-call | flops 4831838208 | bytes 18874368 | tf_op jit(solution)/shard_map/score_gap/pallas_call | solution.py:591
  212.9 10.2 %collective-permute-done.40.got_ref = bf16[64,3072]{1,0:T(8,128)(2,1)S(1)} collective-permute-done((bf16[64,3072]{1,0:T(8,128)(2,1)S(1)}, bf16[64,3072]{1,0:T(8,128)(2,1)S(1)}, u32[]{:S(2)}, u32[]{:S(2)}) %collective-permute-start.40) | collective-permute-done | bytes 393248 | tf_op jit(solution)/shard_map/ppermute | solution.py:259
  223.8 7.4 %collective-permute-done.41.refs_2_ = bf16[512,768]{1,0:T(8,128)(2,1)S(1)} collective-permute-done((bf16[512,768]{1,0:T(8,128)(2,1)S(1)}, bf16[512,768]{1,0:T(8,128)(2,1)S(1)}, u32[]{:S(2)}, u32[]{:S(2)}) %collective-permute-start.41) | collective-permute-done | bytes 786464 | tf_op jit(solution)/shard_map/ppermute | solution.py:271
  234.5 9.5 %collective-permute-done.45.refs_2_ = bf16[1,4,64,384]{3,2,1,0:T(8,128)(2,1)S(1)} collective-permute-done((bf16[1,4,64,384]{3,2,1,0:T(8,128)(2,1)S(1)}, bf16[1,4,64,384]{3,2,1,0:T(8,128)(2,1)S(1)}, u32[]{:S(2)}, u32[]{:S(2)}) %collective-permute-start.45) | collective-permute-done | bytes 196640 | tf_op jit(solution)/shard_map/ppermute | solution.py:259
  252.8 3.2 collective-permute-done.48.refs_0_
  257.7 4.1 %rows_grad.1.refs_0_ = bf16[512,768]{1,0:T(8,128)(2,1)S(1)} custom-call(bf16[64,3072]{1,0:T(8,128)(2,1)S(1)} %get-tuple-element.157.refs_0_, bf16[64,3072]{1,0:T(8,128)(2,1)S(1)} %get-tuple-element.159.refs_1_, bf16[64,3072]{1,0:T(8,128)(2,1)S(1)} %collective-permute-done.46.refs_2_, bf16[64,3072]{1,0:T(8,128)(2,1)S(1)} %collective-permute-done.47.refs_3_, ...), custom_call_target="tpu_custom_call" | custom-call | flops 2415919104 | bytes 10000000 | tf_op jit(solution)/shard_map/rows_grad/pallas_call | solution.py:676
  261.9 4.3 %collective-permute-done.52.refs_2_ = bf16[512,768]{1,0:T(8,128)(2,1)S(1)} collective-permute-done((bf16[512,768]{1,0:T(8,128)(2,1)S(1)}, bf16[512,768]{1,0:T(8,128)(2,1)S(1)}, u32[]{:S(2)}, u32[]{:S(2)}) %collective-permute-start.52) | collective-permute-done | bytes 786464 | tf_op jit(solution)/shard_map/ppermute | solution.py:259
  269.5 18.0 %collective-permute-done.55 = bf16[4,1,64,384]{3,2,0,1:T(8,128)(2,1)S(1)} collective-permute-done((bf16[4,1,64,384]{3,2,0,1:T(8,128)(2,1)S(1)}, bf16[4,1,64,384]{3,2,0,1:T(8,128)(2,1)S(1)}, u32[]{:S(2)}, u32[]{:S(2)}) %collective-permute-start.55) | collective-permute-done | bytes 196640 | tf_op jit(solution)/shard_map/ppermute | solution.py:259
  298.0 9.4 %collective-permute-done.56.refs_0_ = bf16[512,768]{1,0:T(8,128)(2,1)} collective-permute-done((bf16[512,768]{1,0:T(8,128)(2,1)}, bf16[512,768]{1,0:T(8,128)(2,1)}, u32[]{:S(2)}, u32[]{:S(2)}) %collective-permute-start.56) | collective-permute-done | bytes 786464 | tf_op jit(solution)/shard_map/ppermute | solution.py:271
  319.8 4.1 %collective-permute-done.61.refs_0_ = bf16[512,768]{1,0:T(8,128)(2,1)S(1)} collective-permute-done((bf16[512,768]{1,0:T(8,128)(2,1)}, bf16[512,768]{1,0:T(8,128)(2,1)S(1)}, u32[]{:S(2)}, u32[]{:S(2)}) %collective-permute-start.61) | collective-permute-done | bytes 786464 | tf_op jit(solution)/shard_map/ppermute | solution.py:271
  334.7 5.2 %collective-permute-done.64 = bf16[256,768]{1,0:T(8,128)(2,1)S(1)} collective-permute-done((bf16[256,768]{1,0:T(8,128)(2,1)S(1)}, bf16[256,768]{1,0:T(8,128)(2,1)S(1)}, u32[]{:S(2)}, u32[]{:S(2)}) %collective-permute-start.64) | collective-permute-done | bytes 393248 | tf_op jit(solution)/shard_map/ppermute | solution.py:271
  (249 shorter events, 133.4 us)
Async XLA Ops:
  3.1 29.2 %collective-permute-start = (bf16[384,768]{1,0:T(8,128)(2,1)}, bf16[384,768]{1,0:T(8,128)(2,1)}, u32[]{:S(2)}, u32[]{:S(2)}) collective-permute-start(bf16[384,768]{1,0:T(8,128)(2,1)} %get-tuple-element.188), channel_id=1, source_target_pairs={{0,8},{4,12},{8,0},{12,4},{16,24},{20,28},{24,16},{28,20},{1,9},{5... | collective-permute-start | bytes 1769480 | tf_op jit(solution)/shard_map/ppermute | solution.py:259
  6.2 28.7 %collective-permute-start.1 = (bf16[384,768]{1,0:T(8,128)(2,1)}, bf16[384,768]{1,0:T(8,128)(2,1)}, u32[]{:S(2)}, u32[]{:S(2)}) collective-permute-start(bf16[384,768]{1,0:T(8,128)(2,1)} %get-tuple-element.187.refs_0_), channel_id=1, source_target_pairs={{0,16},{4,20},{8,24},{12,28},{16,0},{20,4},{24,8},{28,12},{1,17},{... | collective-permute-start | bytes 1769480 | tf_op jit(solution)/shard_map/ppermute | solution.py:259
  8.8 26.1 %collective-permute-start.2 = (bf16[384,768]{1,0:T(8,128)(2,1)}, bf16[384,768]{1,0:T(8,128)(2,1)}, u32[]{:S(2)}, u32[]{:S(2)}) collective-permute-start(bf16[384,768]{1,0:T(8,128)(2,1)} %get-tuple-element.187.refs_0_), channel_id=1, source_target_pairs={{0,4},{4,0},{8,12},{12,8},{16,20},{20,16},{24,28},{28,24},{1,5},{5... | collective-permute-start | bytes 1769480 | tf_op jit(solution)/shard_map/ppermute | solution.py:259
  34.9 25.9 %collective-permute-start.3 = (bf16[384,768]{1,0:T(8,128)(2,1)}, bf16[384,768]{1,0:T(8,128)(2,1)S(1)}, u32[]{:S(2)}, u32[]{:S(2)}) collective-permute-start(bf16[384,768]{1,0:T(8,128)(2,1)} %get-tuple-element.96.refs_2_), channel_id=1, source_target_pairs={{0,16},{4,20},{8,24},{12,28},{16,0},{20,4},{24,8},{28,12},{1,17},{... | collective-permute-start | bytes 1769480 | tf_op jit(solution)/shard_map/ppermute | solution.py:259
  35.2 25.6 %collective-permute-start.4 = (bf16[384,768]{1,0:T(8,128)(2,1)}, bf16[384,768]{1,0:T(8,128)(2,1)S(1)}, u32[]{:S(2)}, u32[]{:S(2)}) collective-permute-start(bf16[384,768]{1,0:T(8,128)(2,1)} %get-tuple-element.96.refs_2_), channel_id=1, source_target_pairs={{0,4},{4,0},{8,12},{12,8},{16,20},{20,16},{24,28},{28,24},{1,5},{5... | collective-permute-start | bytes 1769480 | tf_op jit(solution)/shard_map/ppermute | solution.py:259
  36.7 25.2 %collective-permute-start.5 = (bf16[384,768]{1,0:T(8,128)(2,1)}, bf16[384,768]{1,0:T(8,128)(2,1)S(1)}, u32[]{:S(2)}, u32[]{:S(2)}) collective-permute-start(bf16[384,768]{1,0:T(8,128)(2,1)} %get-tuple-element.97.refs_4_), channel_id=1, source_target_pairs={{0,4},{4,0},{8,12},{12,8},{16,20},{20,16},{24,28},{28,24},{1,5},{5... | collective-permute-start | bytes 1769480 | tf_op jit(solution)/shard_map/ppermute | solution.py:259
  37.2 32.5 %collective-permute-start.6 = (bf16[768,384]{1,0:T(8,128)(2,1)S(1)}, bf16[768,384]{1,0:T(8,128)(2,1)S(1)}, u32[]{:S(2)}, u32[]{:S(2)}) collective-permute-start(bf16[768,384]{1,0:T(8,128)(2,1)S(1)} %get-tuple-element.98), channel_id=1, source_target_pairs={{0,8},{4,12},{8,0},{12,4},{16,24},{20,28},{24,16},{28,20},{1,9},{5... | collective-permute-start | bytes 1769480 | tf_op jit(solution)/shard_map/ppermute | solution.py:259
  40.0 35.9 %collective-permute-start.13 = (bf16[64,3072]{1,0:T(8,128)(2,1)S(1)}, bf16[64,3072]{1,0:T(8,128)(2,1)S(1)}, u32[]{:S(2)}, u32[]{:S(2)}) collective-permute-start(bf16[64,3072]{1,0:T(8,128)(2,1)S(1)} %slice.57), channel_id=1, source_target_pairs={{0,8},{4,12},{8,0},{12,4},{16,24},{20,28},{24,16},{28,20},{1,9},{5... | collective-permute-start | bytes 1179656 | tf_op jit(solution)/shard_map/ppermute | solution.py:259
  72.4 26.3 %collective-permute-start.8 = (bf16[768,384]{1,0:T(8,128)(2,1)S(1)}, bf16[768,384]{1,0:T(8,128)(2,1)S(1)}, u32[]{:S(2)}, u32[]{:S(2)}) collective-permute-start(bf16[768,384]{1,0:T(8,128)(2,1)S(1)} %get-tuple-element.101.refs_0_.refs_8_), channel_id=1, source_target_pairs={{0,16},{4,20},{8,24},{12,28},{16,0},{20,4},{24,8},{28,12},{1,17},{... | collective-permute-start | bytes 1769480 | tf_op jit(solution)/shard_map/ppermute | solution.py:259
  72.8 25.9 %collective-permute-start.9 = (bf16[768,384]{1,0:T(8,128)(2,1)S(1)}, bf16[768,384]{1,0:T(8,128)(2,1)S(1)}, u32[]{:S(2)}, u32[]{:S(2)}) collective-permute-start(bf16[768,384]{1,0:T(8,128)(2,1)S(1)} %get-tuple-element.101.refs_0_.refs_8_), channel_id=1, source_target_pairs={{0,4},{4,0},{8,12},{12,8},{16,20},{20,16},{24,28},{28,24},{1,5},{5... | collective-permute-start | bytes 1769480 | tf_op jit(solution)/shard_map/ppermute | solution.py:259
  77.2 23.6 %collective-permute-start.15 = (bf16[64,3072]{1,0:T(8,128)(2,1)S(1)}, bf16[64,3072]{1,0:T(8,128)(2,1)S(1)}, u32[]{:S(2)}, u32[]{:S(2)}) collective-permute-start(bf16[64,3072]{1,0:T(8,128)(2,1)S(1)} %collective-permute-done.13.p0), channel_id=1, source_target_pairs={{0,1},{1,0},{2,3},{3,2},{4,5},{5,4},{6,7},{7,6},{8,9},{9,8},{10,11... | collective-permute-start | bytes 1179656 | tf_op jit(solution)/shard_map/ppermute | solution.py:259
  134.9 36.0 %collective-permute-start.27 = (bf16[512,768]{1,0:T(8,128)(2,1)S(1)}, bf16[512,768]{1,0:T(8,128)(2,1)S(1)}, u32[]{:S(2)}, u32[]{:S(2)}) collective-permute-start(bf16[512,768]{1,0:T(8,128)(2,1)S(1)} %get-tuple-element.126.hidden_ref), channel_id=1, source_target_pairs={{0,8},{4,12},{8,16},{12,20},{16,24},{20,28},{24,0},{28,4},{1,9},{5... | collective-permute-start | bytes 2359304 | tf_op jit(solution)/shard_map/ppermute | solution.py:271
  137.1 33.8 %collective-permute-start.28 = (bf16[512,768]{1,0:T(8,128)(2,1)S(1)}, bf16[512,768]{1,0:T(8,128)(2,1)S(1)}, u32[]{:S(2)}, u32[]{:S(2)}) collective-permute-start(bf16[512,768]{1,0:T(8,128)(2,1)S(1)} %get-tuple-element.126.hidden_ref), channel_id=1, source_target_pairs={{0,4},{4,0},{8,12},{12,8},{16,20},{20,16},{24,28},{28,24},{1,5},{5... | collective-permute-start | bytes 2359304 | tf_op jit(solution)/shard_map/ppermute | solution.py:259
  139.8 21.2 %collective-permute-start.29 = (bf16[2,2,64,384]{3,2,0,1:T(8,128)(2,1)S(1)}, bf16[2,2,64,384]{3,2,0,1:T(8,128)(2,1)S(1)}, u32[]{:S(2)}, u32[]{:S(2)}) collective-permute-start(bf16[2,2,64,384]{3,2,0,1:T(8,128)(2,1)S(1)} %fusion.51), channel_id=1, source_target_pairs={{0,8},{4,12},{8,0},{12,4},{16,24},{20,28},{24,16},{28,20},{1,9},{5... | collective-permute-start | bytes 589832 | tf_op jit(solution)/shard_map/ppermute | solution.py:259
  173.5 24.2 %collective-permute-start.33 = (bf16[512,768]{1,0:T(8,128)(2,1)S(1)}, bf16[512,768]{1,0:T(8,128)(2,1)S(1)}, u32[]{:S(2)}, u32[]{:S(2)}) collective-permute-start(bf16[512,768]{1,0:T(8,128)(2,1)S(1)} %get-tuple-element.142), channel_id=1, source_target_pairs={{0,8},{4,12},{8,16},{12,20},{16,24},{20,28},{24,0},{28,4},{1,9},{5... | collective-permute-start | bytes 2359304 | tf_op jit(solution)/shard_map/ppermute | solution.py:271
  173.7 24.0 %collective-permute-start.34 = (bf16[512,768]{1,0:T(8,128)(2,1)S(1)}, bf16[512,768]{1,0:T(8,128)(2,1)S(1)}, u32[]{:S(2)}, u32[]{:S(2)}) collective-permute-start(bf16[512,768]{1,0:T(8,128)(2,1)S(1)} %get-tuple-element.142), channel_id=1, source_target_pairs={{0,4},{4,0},{8,12},{12,8},{16,20},{20,16},{24,28},{28,24},{1,5},{5... | collective-permute-start | bytes 2359304 | tf_op jit(solution)/shard_map/ppermute | solution.py:259
  209.5 21.7 %collective-permute-start.41 = (bf16[512,768]{1,0:T(8,128)(2,1)S(1)}, bf16[512,768]{1,0:T(8,128)(2,1)S(1)}, u32[]{:S(2)}, u32[]{:S(2)}) collective-permute-start(bf16[512,768]{1,0:T(8,128)(2,1)S(1)} %get-tuple-element.156), channel_id=1, source_target_pairs={{0,8},{4,12},{8,16},{12,20},{16,24},{20,28},{24,0},{28,4},{1,9},{5... | collective-permute-start | bytes 2359304 | tf_op jit(solution)/shard_map/ppermute | solution.py:271
  210.4 20.8 %collective-permute-start.42 = (bf16[512,768]{1,0:T(8,128)(2,1)S(1)}, bf16[512,768]{1,0:T(8,128)(2,1)S(1)}, u32[]{:S(2)}, u32[]{:S(2)}) collective-permute-start(bf16[512,768]{1,0:T(8,128)(2,1)S(1)} %get-tuple-element.156), channel_id=1, source_target_pairs={{0,4},{4,0},{8,12},{12,8},{16,20},{20,16},{24,28},{28,24},{1,5},{5... | collective-permute-start | bytes 2359304 | tf_op jit(solution)/shard_map/ppermute | solution.py:259
  266.1 21.3 %collective-permute-start.53 = (bf16[512,768]{1,0:T(8,128)(2,1)S(1)}, bf16[512,768]{1,0:T(8,128)(2,1)}, u32[]{:S(2)}, u32[]{:S(2)}) collective-permute-start(bf16[512,768]{1,0:T(8,128)(2,1)S(1)} %get-tuple-element.166), channel_id=1, source_target_pairs={{0,8},{4,12},{8,16},{12,20},{16,24},{20,28},{24,0},{28,4},{1,9},{5... | collective-permute-start | bytes 2359304 | tf_op jit(solution)/shard_map/ppermute | solution.py:271
  266.8 20.7 %collective-permute-start.54 = (bf16[512,768]{1,0:T(8,128)(2,1)S(1)}, bf16[512,768]{1,0:T(8,128)(2,1)S(1)}, u32[]{:S(2)}, u32[]{:S(2)}) collective-permute-start(bf16[512,768]{1,0:T(8,128)(2,1)S(1)} %get-tuple-element.166), channel_id=1, source_target_pairs={{0,4},{4,0},{8,12},{12,8},{16,20},{20,16},{24,28},{28,24},{1,5},{5... | collective-permute-start | bytes 2359304 | tf_op jit(solution)/shard_map/ppermute | solution.py:259
  268.4 19.0 %collective-permute-start.55 = (bf16[4,1,64,384]{3,2,0,1:T(8,128)(2,1)S(1)}, bf16[4,1,64,384]{3,2,0,1:T(8,128)(2,1)S(1)}, u32[]{:S(2)}, u32[]{:S(2)}) collective-permute-start(bf16[4,1,64,384]{3,2,0,1:T(8,128)(2,1)S(1)} %get-tuple-element.190), channel_id=1, source_target_pairs={{0,4},{4,0},{8,12},{12,8},{16,20},{20,16},{24,28},{28,24},{1,5},{5... | collective-permute-start | bytes 589832 | tf_op jit(solution)/shard_map/ppermute | solution.py:259
  269.0 23.1 %collective-permute-start.37 = (bf16[8,64,384]{2,1,0:T(8,128)(2,1)S(1)}, bf16[8,64,384]{2,1,0:T(8,128)(2,1)}, u32[]{:S(2)}, u32[]{:S(2)}) collective-permute-start(bf16[8,64,384]{2,1,0:T(8,128)(2,1)S(1)} %get-tuple-element.148.refs_0_), channel_id=1, source_target_pairs={{0,1},{1,0},{2,3},{3,2},{4,5},{5,4},{6,7},{7,6},{8,9},{9,8},{10,11... | collective-permute-start | bytes 1179656 | tf_op jit(solution)/shard_map/ppermute | solution.py:259
  269.0 23.1 %collective-permute-start.38 = (bf16[8,64,384]{2,1,0:T(8,128)(2,1)}, bf16[8,64,384]{2,1,0:T(8,128)(2,1)}, u32[]{:S(2)}, u32[]{:S(2)}) collective-permute-start(bf16[8,64,384]{2,1,0:T(8,128)(2,1)} %get-tuple-element.149.refs_1_), channel_id=1, source_target_pairs={{0,1},{1,0},{2,3},{3,2},{4,5},{5,4},{6,7},{7,6},{8,9},{9,8},{10,11... | collective-permute-start | bytes 1179656 | tf_op jit(solution)/shard_map/ppermute | solution.py:259
  289.7 17.7 %collective-permute-start.56 = (bf16[512,768]{1,0:T(8,128)(2,1)}, bf16[512,768]{1,0:T(8,128)(2,1)}, u32[]{:S(2)}, u32[]{:S(2)}) collective-permute-start(bf16[512,768]{1,0:T(8,128)(2,1)} %get-tuple-element.168), channel_id=1, source_target_pairs={{0,8},{4,12},{8,16},{12,20},{16,24},{20,28},{24,0},{28,4},{1,9},{5... | collective-permute-start | bytes 2359304 | tf_op jit(solution)/shard_map/ppermute | solution.py:271
  (74 other events, 906.2 us)

commit v5 on v4

--- a/solution.py
+++ b/solution.py
@@ -276,14 +276,14 @@
     def with_arrived(blocks, arrived):
         return jnp.concatenate([blocks[:, : blocks.shape[1] // 2], arrived], 0)
 
-    def own_columns(tokens, scalars):
+    def own_columns(tokens, scalars, sent):
         _, rows, depth = tokens[0].shape
 
         def body(s, *refs):
             for g in masks:
                 for at, image_index in enumerate((g, g ^ pair)):
                     m = s[0] ^ image_index
-                    spot = (m & pair) + (m & 1) * 4 + (m // 4)
+                    spot = sum(((m // bit) & 1) << place for place, bit in enumerate(sent))
                     for k, ref in enumerate(refs[:-1]):
                         start = (at * parts + k) * rows
                         refs[-1][g, start : start + rows, :] = ref[spot]
@@ -347,7 +347,8 @@
                 values = normalize(values) * (1.0 + mod_ref[1:2]) + mod_ref[0:1]
                 rows_ref[k * rows : (k + 1) * rows, :] = values.astype(bf16)
             for m in masks:
-                blocks_ref[m] = rows_ref[:rows, block(s[0], m)]
+                place = (m & pair) * 2 + (m & far) // 2 + (m & swap)
+                blocks_ref[place] = rows_ref[:rows, block(s[0], m)]
 
         up[pair] = hop(up_send, "grp", pair)
         up[far] = hop(up[0], "grp", far)
@@ -383,9 +384,10 @@
         up[pair | far | swap] = hop(up[pair | far], "grp", swap)
         down[far] = hop(down[0], "grp", far)
         down[swap] = hop(down[0], "grp", swap)
-        up[pair | far | swap], down[pair], down[far], down[swap] = settle(
-            up[pair | far | swap], down[pair], down[far], down[swap]
-        )
+        up[pair | far | swap], down[pair], down[far], down[swap], input_blocks = settle(
+            up[pair | far | swap], down[pair], down[far], down[swap], input_blocks[None]
+        )
+        arrived = send_blocks(input_blocks, pair)
         down[pair | far] = hop(down[pair], "grp", far)
         down[pair | swap] = hop(down[pair], "grp", swap)
         down[far | swap] = hop(down[far], "grp", swap)
@@ -472,14 +474,15 @@
             down[pair | swap],
             down[far | swap],
             gen_hidden,
-            input_blocks,
+            arrived,
         ) = settle(
             down[pair | far],
             down[pair | swap],
             down[far | swap],
             gen_hidden,
-            input_blocks[None],
-        )
+            arrived,
+        )
+        input_blocks = with_arrived(input_blocks, arrived)
         down[pair | far | swap] = hop(down[pair | far], "grp", swap)
         arrived = send_blocks(input_blocks, far)
         left_terms = branch_core(0, gen_hidden)
@@ -489,8 +492,6 @@
         left_sum = branch_sum(*left_terms)
         hidden_near = [gen_hidden, ring(gen_hidden)]
         hidden_across = [hop(gen_hidden, "grp", swap)]
-        input_blocks = with_arrived(input_blocks, arrived)
-        arrived = send_blocks(input_blocks, pair)
         right_sum = branch_sum(*branch_core(1, gen_hidden))
 
         def latent_body(s, noise_ref, diff_ref, mod_ref, *refs):
@@ -653,7 +654,9 @@
         grad_blocks = with_arrived(grad_blocks, arrived)
         arrived = send_blocks(grad_blocks, pair)
         pair_core = hop(pair_grad, "tp", core)
-        pair_crossed, arrived = settle(pair_crossed, arrived)
+        pair_crossed, arrived, hidden_across[3] = settle(
+            pair_crossed, arrived, hidden_across[3]
+        )
         pair_tokens = [pair_grad, pair_crossed, pair_core, hop(pair_crossed, "tp", core)]
 
         def rows_grad_body(*refs):
@@ -686,7 +689,7 @@
             name="rows_grad",
         )(*operands)
 
-        rows_grad, arrived, hidden_across[3] = settle(rows_grad, arrived, hidden_across[3])
+        rows_grad, arrived = settle(rows_grad, arrived)
         near, across = [rows_grad, ring(rows_grad)], [hop(rows_grad, "grp", swap)]
         grad_blocks = with_arrived(grad_blocks, arrived)
         arrived = send_blocks(grad_blocks, swap)
@@ -697,8 +700,8 @@
         near[2], across[1], *grad_tokens = settle(near[2], across[1], *grad_tokens)
         near.append(ring(near[2]))
         across.append(hop(near[2], "grp", swap))
-        input_columns = own_columns(input_tokens, scalars)
-        grad_columns = own_columns(grad_tokens, scalars)
+        input_columns = own_columns(input_tokens, scalars, (pair, far, swap))
+        grad_columns = own_columns(grad_tokens, scalars, (far, pair, swap))
 
         def columns_at(table, k, other):
             origin = lax.rem(own + groups - 2 * k, groups) ^ other

time: 344 us -> 344 us (level)
    ppermute x7, waiting for transfers between devices: 26.2 us -> 31.3 us  [ring(): return lax.ppermute(values, 'grp', ring_pairs)]
    ppermute x58, waiting for transfers between devices: 181 us -> 176 us  [hop(): return lax.ppermute(values, axis, [(i, i ^ mask) for i in range(size)])]
    ppermute x7, starting transfers between devices: 9.77 us -> 5.76 us  [ring(): return lax.ppermute(values, 'grp', ring_pairs)]
  transfers between devices with their start and end apart: 65 -> 65, of which waited for: 33 -> 32; matrix products, arithmetic and copies ran while one was open for 4% -> 4% of each run, Pallas kernels for 11% -> 10%
where the time goes in v5:
time: 344 us; the launch traced here: 343 us
  waiting for transfers between devices  207 us (60%)
  starting transfers between devices  67.5 us (20%)
  Pallas kernels  41.3 us (12%)
  matrix products  12.8 us (4%)
  local copies, waits for them, and re-layouts  8.36 us (2%)
  other arithmetic  3.6 us (1%)
    ppermute x58, waiting for transfers between devices, hop(): return lax.ppermute(values, axis, [(i, i ^ mask) for i in range(size)])  176 us
    ppermute x58, starting transfers between devices, hop(): return lax.ppermute(values, axis, [(i, i ^ mask) for i in range(size)])  61.7 us
    ppermute x7, waiting for transfers between devices, ring(): return lax.ppermute(values, 'grp', ring_pairs)  31.3 us
    pallas_call x14, Pallas kernels, kernel_call(): pl.pallas_call(body, out_shape=tuple(out_shapes), in_specs=specs, out_spe...  18.7 us
    dot_general x17, matrix products, dot(): lax.dot_general(left, right, (contract, ((), ())), preferred_element_type...  12.8 us
    pallas_call x1, Pallas kernels, per_device(): pl.pallas_call(gap_body, grid=(width // tile,), in_specs=[pl.BlockSpec(me...  10.3 us
    pallas_call x1, Pallas kernels, per_device(): pl.pallas_call(hidden_body, grid=(score_units // tile,), in_specs=[whole,...  8.19 us
  transfers between devices with their start and end apart: 65, of which 32 were waited for; matrix products, arithmetic and copies ran while one was open for 4% of the time, Pallas kernels for 10%

profile of v5, /device:TPU:0, one launch (start us, length us, event | category | flops | bytes accessed | tf_op | source)
XLA Modules:
  0.0 342.9 jit_solution(13746116904440556294)
XLA Ops:
  14.1 18.2 %collective-permute-done.refs_0_ = bf16[384,768]{1,0:T(8,128)(2,1)} collective-permute-done((bf16[384,768]{1,0:T(8,128)(2,1)}, bf16[384,768]{1,0:T(8,128)(2,1)}, u32[]{:S(2)}, u32[]{:S(2)}) %collective-permute-start) | collective-permute-done | bytes 589856 | tf_op jit(solution)/shard_map/ppermute | solution.py:259
  40.0 20.7 %collective-permute-done.3.refs_0_ = bf16[384,768]{1,0:T(8,128)(2,1)S(1)} collective-permute-done((bf16[384,768]{1,0:T(8,128)(2,1)}, bf16[384,768]{1,0:T(8,128)(2,1)S(1)}, u32[]{:S(2)}, u32[]{:S(2)}) %collective-permute-start.3) | collective-permute-done | bytes 589856 | tf_op jit(solution)/shard_map/ppermute | solution.py:259
  61.9 7.8 %collective-permute-done.6.refs_3_ = bf16[768,384]{1,0:T(8,128)(2,1)S(1)} collective-permute-done((bf16[768,384]{1,0:T(8,128)(2,1)S(1)}, bf16[768,384]{1,0:T(8,128)(2,1)S(1)}, u32[]{:S(2)}, u32[]{:S(2)}) %collective-permute-start.6) | collective-permute-done | bytes 589856 | tf_op jit(solution)/shard_map/ppermute | solution.py:259
  77.2 6.4 %collective-permute-done.14.p1 = bf16[64,3072]{1,0:T(8,128)(2,1)S(1)} collective-permute-done((bf16[64,3072]{1,0:T(8,128)(2,1)S(1)}, bf16[64,3072]{1,0:T(8,128)(2,1)S(1)}, u32[]{:S(2)}, u32[]{:S(2)}) %collective-permute-start.14) | collective-permute-done | bytes 393248 | tf_op jit(solution)/shard_map/ppermute | solution.py:259
  83.6 15.1 %collective-permute-done.8.refs_2_ = bf16[768,384]{1,0:T(8,128)(2,1)S(1)} collective-permute-done((bf16[768,384]{1,0:T(8,128)(2,1)S(1)}, bf16[768,384]{1,0:T(8,128)(2,1)S(1)}, u32[]{:S(2)}, u32[]{:S(2)}) %collective-permute-start.8) | collective-permute-done | bytes 589856 | tf_op jit(solution)/shard_map/ppermute | solution.py:259
  103.3 5.3 %pre.1 = (f32[512,768]{1,0:T(8,128)S(1)}, bf16[512,768]{1,0:T(8,128)(2,1)S(1)}) custom-call(s32[4]{0:T(128)S(1)} %pad_add_fusion.s, bf16[256,3072]{1,0:T(8,128)(2,1)S(1)} %get-tuple-element.106.rows_ref, bf16[64,3072]{1,0:T(8,128)(2,1)S(1)} %collective-permute-done.13.p0, bf16[64,3072]{1,0:T(8,128)(2,1)S(1)} %collective-permute-done.14.p1, ...), custom_call_target="tpu_custom_call" | custom-call | flops 2415919104 | bytes 10223632 | tf_op jit(solution)/shard_map/pre/pallas_call | solution.py:225
  108.6 6.7 %collective-permute-done.10.refs_0_ = bf16[768,384]{1,0:T(8,128)(2,1)S(1)} collective-permute-done((bf16[768,384]{1,0:T(8,128)(2,1)S(1)}, bf16[768,384]{1,0:T(8,128)(2,1)S(1)}, u32[]{:S(2)}, u32[]{:S(2)}) %collective-permute-start.10) | collective-permute-done | bytes 589856 | tf_op jit(solution)/shard_map/ppermute | solution.py:259
  121.5 9.8 %collective-permute-done.19 = bf16[2,2,64,384]{3,2,0,1:T(8,128)(2,1)S(1)} collective-permute-done((bf16[2,2,64,384]{3,2,0,1:T(8,128)(2,1)S(1)}, bf16[2,2,64,384]{3,2,0,1:T(8,128)(2,1)S(1)}, u32[]{:S(2)}, u32[]{:S(2)}) %collective-permute-start.19) | collective-permute-done | bytes 196640 | tf_op jit(solution)/shard_map/ppermute | solution.py:259
  141.3 4.0 %collective-permute-done.22.right_ref = bf16[64,1536]{1,0:T(8,128)(2,1)S(1)} collective-permute-done((bf16[64,1536]{1,0:T(8,128)(2,1)S(1)}, bf16[64,1536]{1,0:T(8,128)(2,1)S(1)}, u32[]{:S(2)}, u32[]{:S(2)}) %collective-permute-start.22) | collective-permute-done | bytes 196640 | tf_op jit(solution)/shard_map/ppermute | solution.py:259
  156.0 5.0 %collective-permute-done.23.refs_2_ = bf16[64,1536]{1,0:T(8,128)(2,1)S(1)} collective-permute-done((bf16[64,1536]{1,0:T(8,128)(2,1)S(1)}, bf16[64,1536]{1,0:T(8,128)(2,1)S(1)}, u32[]{:S(2)}, u32[]{:S(2)}) %collective-permute-start.23) | collective-permute-done | bytes 196640 | tf_op jit(solution)/shard_map/ppermute | solution.py:259
  161.0 4.1 %collective-permute-done.27.refs_5_ = bf16[64,1536]{1,0:T(8,128)(2,1)S(1)} collective-permute-done((bf16[64,1536]{1,0:T(8,128)(2,1)S(1)}, bf16[64,1536]{1,0:T(8,128)(2,1)S(1)}, u32[]{:S(2)}, u32[]{:S(2)}) %collective-permute-start.27) | collective-permute-done | bytes 196640 | tf_op jit(solution)/shard_map/ppermute | solution.py:259
  171.2 6.7 %collective-permute-done.30.n1 = bf16[64,3072]{1,0:T(8,128)(2,1)S(1)} collective-permute-done((bf16[64,3072]{1,0:T(8,128)(2,1)S(1)}, bf16[64,3072]{1,0:T(8,128)(2,1)S(1)}, u32[]{:S(2)}, u32[]{:S(2)}) %collective-permute-start.30) | collective-permute-done | bytes 393248 | tf_op jit(solution)/shard_map/ppermute | solution.py:259
  182.6 8.2 %score_hidden.1 = (bf16[256,1536]{1,0:T(8,128)(2,1)S(1)}, bf16[256,1536]{1,0:T(8,128)(2,1)S(1)}) custom-call(bf16[256,3072]{1,0:T(8,128)(2,1)S(1)} %get-tuple-element.141.t_in, bf16[256,3072]{1,0:T(8,128)(2,1)S(1)} %get-tuple-element.142.c_in, bf16[3072,1536]{1,0:T(8,128)(2,1)S(1)} %bitcast.90, bf16[3072,1536]{1,0:T(8,128)(2,1)S(1)} %bitcast.92), custom_call_target="tpu_custom_call" | custom-call | flops 4831838208 | bytes 18874368 | tf_op jit(solution)/shard_map/score_hidden/pallas_call | solution.py:561
  194.9 10.3 %score_gap.1 = (f32[128,3072]{1,0:T(8,128)S(1)}, bf16[128,3072]{1,0:T(8,128)(2,1)S(1)}) custom-call(s32[4]{0:T(128)S(1)} %pad_add_fusion.s, bf16[256,1536]{1,0:T(8,128)(2,1)S(1)} %get-tuple-element.146.t_h, bf16[256,1536]{1,0:T(8,128)(2,1)S(1)} %get-tuple-element.147.c_h, bf16[1536,3072]{1,0:T(8,128)(2,1)S(1)} %bitcast.86, bf16[1536,3072]{1,0:T(8,128)(2,1)S(1)} %bitcast.88, ...), custom_call_target="tpu_custom_call" | custom-call | flops 4831838208 | bytes 18874368 | tf_op jit(solution)/shard_map/score_gap/pallas_call | solution.py:592
  209.0 10.1 %collective-permute-done.40.got_ref = bf16[64,3072]{1,0:T(8,128)(2,1)S(1)} collective-permute-done((bf16[64,3072]{1,0:T(8,128)(2,1)S(1)}, bf16[64,3072]{1,0:T(8,128)(2,1)S(1)}, u32[]{:S(2)}, u32[]{:S(2)}) %collective-permute-start.40) | collective-permute-done | bytes 393248 | tf_op jit(solution)/shard_map/ppermute | solution.py:259
  219.8 7.3 %collective-permute-done.41.refs_2_ = bf16[512,768]{1,0:T(8,128)(2,1)S(1)} collective-permute-done((bf16[512,768]{1,0:T(8,128)(2,1)S(1)}, bf16[512,768]{1,0:T(8,128)(2,1)S(1)}, u32[]{:S(2)}, u32[]{:S(2)}) %collective-permute-start.41) | collective-permute-done | bytes 786464 | tf_op jit(solution)/shard_map/ppermute | solution.py:271
  232.1 7.8 %collective-permute-done.45.refs_2_ = bf16[1,4,64,384]{3,2,1,0:T(8,128)(2,1)S(1)} collective-permute-done((bf16[1,4,64,384]{3,2,1,0:T(8,128)(2,1)S(1)}, bf16[1,4,64,384]{3,2,1,0:T(8,128)(2,1)S(1)}, u32[]{:S(2)}, u32[]{:S(2)}) %collective-permute-start.45) | collective-permute-done | bytes 196640 | tf_op jit(solution)/shard_map/ppermute | solution.py:259
  245.2 3.5 %collective-permute-done.49 = bf16[2,2,64,384]{3,2,0,1:T(8,128)(2,1)S(1)} collective-permute-done((bf16[2,2,64,384]{3,2,0,1:T(8,128)(2,1)S(1)}, bf16[2,2,64,384]{3,2,0,1:T(8,128)(2,1)S(1)}, u32[]{:S(2)}, u32[]{:S(2)}) %collective-permute-start.49) | collective-permute-done | bytes 196640 | tf_op jit(solution)/shard_map/ppermute | solution.py:259
  253.6 4.1 %rows_grad.1.refs_0_ = bf16[512,768]{1,0:T(8,128)(2,1)S(1)} custom-call(bf16[64,3072]{1,0:T(8,128)(2,1)S(1)} %get-tuple-element.159.refs_0_, bf16[64,3072]{1,0:T(8,128)(2,1)S(1)} %get-tuple-element.161.refs_1_, bf16[64,3072]{1,0:T(8,128)(2,1)S(1)} %collective-permute-done.46.refs_2_, bf16[64,3072]{1,0:T(8,128)(2,1)S(1)} %collective-permute-done.47.refs_3_, ...), custom_call_target="tpu_custom_call" | custom-call | flops 2415919104 | bytes 10000000 | tf_op jit(solution)/shard_map/rows_grad/pallas_call | solution.py:679
  262.0 20.8 %collective-permute-done.55 = bf16[4,1,64,384]{3,2,0,1:T(8,128)(2,1)S(1)} collective-permute-done((bf16[4,1,64,384]{3,2,0,1:T(8,128)(2,1)S(1)}, bf16[4,1,64,384]{3,2,0,1:T(8,128)(2,1)S(1)}, u32[]{:S(2)}, u32[]{:S(2)}) %collective-permute-start.55) | collective-permute-done | bytes 196640 | tf_op jit(solution)/shard_map/ppermute | solution.py:259
  288.0 5.0 %collective-permute-done.58.refs_3_ = bf16[8,64,384]{2,1,0:T(8,128)(2,1)S(1)} collective-permute-done((bf16[8,64,384]{2,1,0:T(8,128)(2,1)S(1)}, bf16[8,64,384]{2,1,0:T(8,128)(2,1)S(1)}, u32[]{:S(2)}, u32[]{:S(2)}) %collective-permute-start.58) | collective-permute-done | bytes 393248 | tf_op jit(solution)/shard_map/ppermute | solution.py:259
  294.7 9.3 %collective-permute-done.56.refs_0_ = bf16[512,768]{1,0:T(8,128)(2,1)} collective-permute-done((bf16[512,768]{1,0:T(8,128)(2,1)}, bf16[512,768]{1,0:T(8,128)(2,1)}, u32[]{:S(2)}, u32[]{:S(2)}) %collective-permute-start.56) | collective-permute-done | bytes 786464 | tf_op jit(solution)/shard_map/ppermute | solution.py:271
  315.1 8.2 %collective-permute-done.61.refs_0_ = bf16[512,768]{1,0:T(8,128)(2,1)S(1)} collective-permute-done((bf16[512,768]{1,0:T(8,128)(2,1)}, bf16[512,768]{1,0:T(8,128)(2,1)S(1)}, u32[]{:S(2)}, u32[]{:S(2)}) %collective-permute-start.61) | collective-permute-done | bytes 786464 | tf_op jit(solution)/shard_map/ppermute | solution.py:271
  332.7 6.4 %collective-permute-done.64 = bf16[256,768]{1,0:T(8,128)(2,1)S(1)} collective-permute-done((bf16[256,768]{1,0:T(8,128)(2,1)S(1)}, bf16[256,768]{1,0:T(8,128)(2,1)S(1)}, u32[]{:S(2)}, u32[]{:S(2)}) %collective-permute-start.64) | collective-permute-done | bytes 393248 | tf_op jit(solution)/shard_map/ppermute | solution.py:271
  (249 shorter events, 129.9 us)
Async XLA Ops:
  3.1 29.2 %collective-permute-start = (bf16[384,768]{1,0:T(8,128)(2,1)}, bf16[384,768]{1,0:T(8,128)(2,1)}, u32[]{:S(2)}, u32[]{:S(2)}) collective-permute-start(bf16[384,768]{1,0:T(8,128)(2,1)} %get-tuple-element.190), channel_id=1, source_target_pairs={{0,8},{4,12},{8,0},{12,4},{16,24},{20,28},{24,16},{28,20},{1,9},{5... | collective-permute-start | bytes 1769480 | tf_op jit(solution)/shard_map/ppermute | solution.py:259
  6.2 28.7 %collective-permute-start.1 = (bf16[384,768]{1,0:T(8,128)(2,1)}, bf16[384,768]{1,0:T(8,128)(2,1)}, u32[]{:S(2)}, u32[]{:S(2)}) collective-permute-start(bf16[384,768]{1,0:T(8,128)(2,1)} %get-tuple-element.189.refs_0_), channel_id=1, source_target_pairs={{0,16},{4,20},{8,24},{12,28},{16,0},{20,4},{24,8},{28,12},{1,17},{... | collective-permute-start | bytes 1769480 | tf_op jit(solution)/shard_map/ppermute | solution.py:259
  8.8 26.1 %collective-permute-start.2 = (bf16[384,768]{1,0:T(8,128)(2,1)}, bf16[384,768]{1,0:T(8,128)(2,1)}, u32[]{:S(2)}, u32[]{:S(2)}) collective-permute-start(bf16[384,768]{1,0:T(8,128)(2,1)} %get-tuple-element.189.refs_0_), channel_id=1, source_target_pairs={{0,4},{4,0},{8,12},{12,8},{16,20},{20,16},{24,28},{28,24},{1,5},{5... | collective-permute-start | bytes 1769480 | tf_op jit(solution)/shard_map/ppermute | solution.py:259
  34.9 25.9 %collective-permute-start.3 = (bf16[384,768]{1,0:T(8,128)(2,1)}, bf16[384,768]{1,0:T(8,128)(2,1)S(1)}, u32[]{:S(2)}, u32[]{:S(2)}) collective-permute-start(bf16[384,768]{1,0:T(8,128)(2,1)} %get-tuple-element.97.refs_2_), channel_id=1, source_target_pairs={{0,16},{4,20},{8,24},{12,28},{16,0},{20,4},{24,8},{28,12},{1,17},{... | collective-permute-start | bytes 1769480 | tf_op jit(solution)/shard_map/ppermute | solution.py:259
  35.2 25.6 %collective-permute-start.4 = (bf16[384,768]{1,0:T(8,128)(2,1)}, bf16[384,768]{1,0:T(8,128)(2,1)S(1)}, u32[]{:S(2)}, u32[]{:S(2)}) collective-permute-start(bf16[384,768]{1,0:T(8,128)(2,1)} %get-tuple-element.97.refs_2_), channel_id=1, source_target_pairs={{0,4},{4,0},{8,12},{12,8},{16,20},{20,16},{24,28},{28,24},{1,5},{5... | collective-permute-start | bytes 1769480 | tf_op jit(solution)/shard_map/ppermute | solution.py:259
  36.7 25.2 %collective-permute-start.5 = (bf16[384,768]{1,0:T(8,128)(2,1)}, bf16[384,768]{1,0:T(8,128)(2,1)S(1)}, u32[]{:S(2)}, u32[]{:S(2)}) collective-permute-start(bf16[384,768]{1,0:T(8,128)(2,1)} %get-tuple-element.98.refs_4_), channel_id=1, source_target_pairs={{0,4},{4,0},{8,12},{12,8},{16,20},{20,16},{24,28},{28,24},{1,5},{5... | collective-permute-start | bytes 1769480 | tf_op jit(solution)/shard_map/ppermute | solution.py:259
  37.2 32.5 %collective-permute-start.6 = (bf16[768,384]{1,0:T(8,128)(2,1)S(1)}, bf16[768,384]{1,0:T(8,128)(2,1)S(1)}, u32[]{:S(2)}, u32[]{:S(2)}) collective-permute-start(bf16[768,384]{1,0:T(8,128)(2,1)S(1)} %get-tuple-element.99), channel_id=1, source_target_pairs={{0,8},{4,12},{8,0},{12,4},{16,24},{20,28},{24,16},{28,20},{1,9},{5... | collective-permute-start | bytes 1769480 | tf_op jit(solution)/shard_map/ppermute | solution.py:259
  40.0 35.9 %collective-permute-start.13 = (bf16[64,3072]{1,0:T(8,128)(2,1)S(1)}, bf16[64,3072]{1,0:T(8,128)(2,1)S(1)}, u32[]{:S(2)}, u32[]{:S(2)}) collective-permute-start(bf16[64,3072]{1,0:T(8,128)(2,1)S(1)} %slice.57), channel_id=1, source_target_pairs={{0,8},{4,12},{8,0},{12,4},{16,24},{20,28},{24,16},{28,20},{1,9},{5... | collective-permute-start | bytes 1179656 | tf_op jit(solution)/shard_map/ppermute | solution.py:259
  72.4 26.3 %collective-permute-start.8 = (bf16[768,384]{1,0:T(8,128)(2,1)S(1)}, bf16[768,384]{1,0:T(8,128)(2,1)S(1)}, u32[]{:S(2)}, u32[]{:S(2)}) collective-permute-start(bf16[768,384]{1,0:T(8,128)(2,1)S(1)} %get-tuple-element.102.refs_0_.refs_8_), channel_id=1, source_target_pairs={{0,16},{4,20},{8,24},{12,28},{16,0},{20,4},{24,8},{28,12},{1,17},{... | collective-permute-start | bytes 1769480 | tf_op jit(solution)/shard_map/ppermute | solution.py:259
  72.8 25.9 %collective-permute-start.9 = (bf16[768,384]{1,0:T(8,128)(2,1)S(1)}, bf16[768,384]{1,0:T(8,128)(2,1)S(1)}, u32[]{:S(2)}, u32[]{:S(2)}) collective-permute-start(bf16[768,384]{1,0:T(8,128)(2,1)S(1)} %get-tuple-element.102.refs_0_.refs_8_), channel_id=1, source_target_pairs={{0,4},{4,0},{8,12},{12,8},{16,20},{20,16},{24,28},{28,24},{1,5},{5... | collective-permute-start | bytes 1769480 | tf_op jit(solution)/shard_map/ppermute | solution.py:259
  77.2 23.6 %collective-permute-start.15 = (bf16[64,3072]{1,0:T(8,128)(2,1)S(1)}, bf16[64,3072]{1,0:T(8,128)(2,1)S(1)}, u32[]{:S(2)}, u32[]{:S(2)}) collective-permute-start(bf16[64,3072]{1,0:T(8,128)(2,1)S(1)} %collective-permute-done.13.p0), channel_id=1, source_target_pairs={{0,1},{1,0},{2,3},{3,2},{4,5},{5,4},{6,7},{7,6},{8,9},{9,8},{10,11... | collective-permute-start | bytes 1179656 | tf_op jit(solution)/shard_map/ppermute | solution.py:259
  134.9 31.8 %collective-permute-start.28 = (bf16[512,768]{1,0:T(8,128)(2,1)S(1)}, bf16[512,768]{1,0:T(8,128)(2,1)S(1)}, u32[]{:S(2)}, u32[]{:S(2)}) collective-permute-start(bf16[512,768]{1,0:T(8,128)(2,1)S(1)} %get-tuple-element.128.hidden_ref), channel_id=1, source_target_pairs={{0,8},{4,12},{8,16},{12,20},{16,24},{20,28},{24,0},{28,4},{1,9},{5... | collective-permute-start | bytes 2359304 | tf_op jit(solution)/shard_map/ppermute | solution.py:271
  137.1 29.7 %collective-permute-start.29 = (bf16[512,768]{1,0:T(8,128)(2,1)S(1)}, bf16[512,768]{1,0:T(8,128)(2,1)S(1)}, u32[]{:S(2)}, u32[]{:S(2)}) collective-permute-start(bf16[512,768]{1,0:T(8,128)(2,1)S(1)} %get-tuple-element.128.hidden_ref), channel_id=1, source_target_pairs={{0,4},{4,0},{8,12},{12,8},{16,20},{20,16},{24,28},{28,24},{1,5},{5... | collective-permute-start | bytes 2359304 | tf_op jit(solution)/shard_map/ppermute | solution.py:259
  169.3 24.2 %collective-permute-start.33 = (bf16[512,768]{1,0:T(8,128)(2,1)S(1)}, bf16[512,768]{1,0:T(8,128)(2,1)S(1)}, u32[]{:S(2)}, u32[]{:S(2)}) collective-permute-start(bf16[512,768]{1,0:T(8,128)(2,1)S(1)} %get-tuple-element.144), channel_id=1, source_target_pairs={{0,8},{4,12},{8,16},{12,20},{16,24},{20,28},{24,0},{28,4},{1,9},{5... | collective-permute-start | bytes 2359304 | tf_op jit(solution)/shard_map/ppermute | solution.py:271
  169.5 24.0 %collective-permute-start.34 = (bf16[512,768]{1,0:T(8,128)(2,1)S(1)}, bf16[512,768]{1,0:T(8,128)(2,1)S(1)}, u32[]{:S(2)}, u32[]{:S(2)}) collective-permute-start(bf16[512,768]{1,0:T(8,128)(2,1)S(1)} %get-tuple-element.144), channel_id=1, source_target_pairs={{0,4},{4,0},{8,12},{12,8},{16,20},{20,16},{24,28},{28,24},{1,5},{5... | collective-permute-start | bytes 2359304 | tf_op jit(solution)/shard_map/ppermute | solution.py:259
  205.3 21.7 %collective-permute-start.41 = (bf16[512,768]{1,0:T(8,128)(2,1)S(1)}, bf16[512,768]{1,0:T(8,128)(2,1)S(1)}, u32[]{:S(2)}, u32[]{:S(2)}) collective-permute-start(bf16[512,768]{1,0:T(8,128)(2,1)S(1)} %get-tuple-element.158), channel_id=1, source_target_pairs={{0,8},{4,12},{8,16},{12,20},{16,24},{20,28},{24,0},{28,4},{1,9},{5... | collective-permute-start | bytes 2359304 | tf_op jit(solution)/shard_map/ppermute | solution.py:271
  206.2 20.8 %collective-permute-start.42 = (bf16[512,768]{1,0:T(8,128)(2,1)S(1)}, bf16[512,768]{1,0:T(8,128)(2,1)S(1)}, u32[]{:S(2)}, u32[]{:S(2)}) collective-permute-start(bf16[512,768]{1,0:T(8,128)(2,1)S(1)} %get-tuple-element.158), channel_id=1, source_target_pairs={{0,4},{4,0},{8,12},{12,8},{16,20},{20,16},{24,28},{28,24},{1,5},{5... | collective-permute-start | bytes 2359304 | tf_op jit(solution)/shard_map/ppermute | solution.py:259
  228.0 23.8 %collective-permute-start.50 = (bf16[512,768]{1,0:T(8,128)(2,1)S(1)}, bf16[512,768]{1,0:T(8,128)(2,1)S(1)}, u32[]{:S(2)}, u32[]{:S(2)}) collective-permute-start(bf16[512,768]{1,0:T(8,128)(2,1)S(1)} %get-tuple-element.164), channel_id=1, source_target_pairs={{0,4},{4,0},{8,12},{12,8},{16,20},{20,16},{24,28},{28,24},{1,5},{5... | collective-permute-start | bytes 2359304 | tf_op jit(solution)/shard_map/ppermute | solution.py:259
  257.7 25.1 %collective-permute-start.53 = (bf16[512,768]{1,0:T(8,128)(2,1)S(1)}, bf16[512,768]{1,0:T(8,128)(2,1)}, u32[]{:S(2)}, u32[]{:S(2)}) collective-permute-start(bf16[512,768]{1,0:T(8,128)(2,1)S(1)} %get-tuple-element.168), channel_id=1, source_target_pairs={{0,8},{4,12},{8,16},{12,20},{16,24},{20,28},{24,0},{28,4},{1,9},{5... | collective-permute-start | bytes 2359304 | tf_op jit(solution)/shard_map/ppermute | solution.py:271
  259.3 23.5 %collective-permute-start.54 = (bf16[512,768]{1,0:T(8,128)(2,1)S(1)}, bf16[512,768]{1,0:T(8,128)(2,1)S(1)}, u32[]{:S(2)}, u32[]{:S(2)}) collective-permute-start(bf16[512,768]{1,0:T(8,128)(2,1)S(1)} %get-tuple-element.168), channel_id=1, source_target_pairs={{0,4},{4,0},{8,12},{12,8},{16,20},{20,16},{24,28},{28,24},{1,5},{5... | collective-permute-start | bytes 2359304 | tf_op jit(solution)/shard_map/ppermute | solution.py:259
  261.2 21.7 %collective-permute-start.55 = (bf16[4,1,64,384]{3,2,0,1:T(8,128)(2,1)S(1)}, bf16[4,1,64,384]{3,2,0,1:T(8,128)(2,1)S(1)}, u32[]{:S(2)}, u32[]{:S(2)}) collective-permute-start(bf16[4,1,64,384]{3,2,0,1:T(8,128)(2,1)S(1)} %get-tuple-element.192), channel_id=1, source_target_pairs={{0,4},{4,0},{8,12},{12,8},{16,20},{20,16},{24,28},{28,24},{1,5},{5... | collective-permute-start | bytes 589832 | tf_op jit(solution)/shard_map/ppermute | solution.py:259
  261.5 24.8 %collective-permute-start.37 = (bf16[8,64,384]{2,1,0:T(8,128)(2,1)S(1)}, bf16[8,64,384]{2,1,0:T(8,128)(2,1)}, u32[]{:S(2)}, u32[]{:S(2)}) collective-permute-start(bf16[8,64,384]{2,1,0:T(8,128)(2,1)S(1)} %get-tuple-element.150.refs_0_), channel_id=1, source_target_pairs={{0,1},{1,0},{2,3},{3,2},{4,5},{5,4},{6,7},{7,6},{8,9},{9,8},{10,11... | collective-permute-start | bytes 1179656 | tf_op jit(solution)/shard_map/ppermute | solution.py:259
  261.5 24.8 %collective-permute-start.38 = (bf16[8,64,384]{2,1,0:T(8,128)(2,1)}, bf16[8,64,384]{2,1,0:T(8,128)(2,1)}, u32[]{:S(2)}, u32[]{:S(2)}) collective-permute-start(bf16[8,64,384]{2,1,0:T(8,128)(2,1)} %get-tuple-element.151.refs_1_), channel_id=1, source_target_pairs={{0,1},{1,0},{2,3},{3,2},{4,5},{5,4},{6,7},{7,6},{8,9},{9,8},{10,11... | collective-permute-start | bytes 1179656 | tf_op jit(solution)/shard_map/ppermute | solution.py:259
  283.8 20.3 %collective-permute-start.56 = (bf16[512,768]{1,0:T(8,128)(2,1)}, bf16[512,768]{1,0:T(8,128)(2,1)}, u32[]{:S(2)}, u32[]{:S(2)}) collective-permute-start(bf16[512,768]{1,0:T(8,128)(2,1)} %get-tuple-element.170), channel_id=1, source_target_pairs={{0,8},{4,12},{8,16},{12,20},{16,24},{20,28},{24,0},{28,4},{1,9},{5... | collective-permute-start | bytes 2359304 | tf_op jit(solution)/shard_map/ppermute | solution.py:271
  (74 other events, 891.4 us)

commit v6 on v5

--- a/solution.py
+++ b/solution.py
@@ -658,6 +658,8 @@
             pair_crossed, arrived, hidden_across[3]
         )
         pair_tokens = [pair_grad, pair_crossed, pair_core, hop(pair_crossed, "tp", core)]
+        grad_blocks = with_arrived(grad_blocks, arrived)
+        arrived = send_blocks(grad_blocks, swap)
 
         def rows_grad_body(*refs):
             tokens, pieces = refs[:8], refs[8 : 8 + groups]
@@ -691,8 +693,6 @@
 
         rows_grad, arrived = settle(rows_grad, arrived)
         near, across = [rows_grad, ring(rows_grad)], [hop(rows_grad, "grp", swap)]
-        grad_blocks = with_arrived(grad_blocks, arrived)
-        arrived = send_blocks(grad_blocks, swap)
         near[1], across[0], arrived = settle(near[1], across[0], arrived)
         near.append(ring(near[1]))
         across.append(hop(near[1], "grp", swap))

time: 344 us -> 341 us (level)
    ppermute x58, waiting for transfers between devices: 176 us -> 155 us  [hop(): return lax.ppermute(values, axis, [(i, i ^ mask) for i in range(size)])]
    ppermute x7, waiting for transfers between devices: 31.3 us -> 48.7 us  [ring(): return lax.ppermute(values, 'grp', ring_pairs)]
  transfers between devices with their start and end apart: 65 -> 65, of which waited for: 32 -> 32; matrix products, arithmetic and copies ran while one was open for 4% -> 4% of each run, Pallas kernels for 10% -> 11%
where the time goes in v6:
time: 341 us; the launch traced here: 340 us
  waiting for transfers between devices  204 us (60%)
  starting transfers between devices  67.9 us (20%)
  Pallas kernels  41.3 us (12%)
  matrix products  12.7 us (4%)
  local copies, waits for them, and re-layouts  8.35 us (2%)
  other arithmetic  3.6 us (1%)
    ppermute x58, waiting for transfers between devices, hop(): return lax.ppermute(values, axis, [(i, i ^ mask) for i in range(size)])  155 us
    ppermute x58, starting transfers between devices, hop(): return lax.ppermute(values, axis, [(i, i ^ mask) for i in range(size)])  63.3 us
    ppermute x7, waiting for transfers between devices, ring(): return lax.ppermute(values, 'grp', ring_pairs)  48.7 us
    pallas_call x14, Pallas kernels, kernel_call(): pl.pallas_call(body, out_shape=tuple(out_shapes), in_specs=specs, out_spe...  18.7 us
    dot_general x17, matrix products, dot(): lax.dot_general(left, right, (contract, ((), ())), preferred_element_type...  12.7 us
    pallas_call x1, Pallas kernels, per_device(): pl.pallas_call(gap_body, grid=(width // tile,), in_specs=[pl.BlockSpec(me...  10.3 us
    pallas_call x1, Pallas kernels, per_device(): pl.pallas_call(hidden_body, grid=(score_units // tile,), in_specs=[whole,...  8.19 us
  transfers between devices with their start and end apart: 65, of which 32 were waited for; matrix products, arithmetic and copies ran while one was open for 4% of the time, Pallas kernels for 11%

profile of v6, /device:TPU:0, one launch (start us, length us, event | category | flops | bytes accessed | tf_op | source)
XLA Modules:
  0.0 340.2 jit_solution(10737233488159768076)
XLA Ops:
  14.1 18.2 %collective-permute-done.refs_0_ = bf16[384,768]{1,0:T(8,128)(2,1)} collective-permute-done((bf16[384,768]{1,0:T(8,128)(2,1)}, bf16[384,768]{1,0:T(8,128)(2,1)}, u32[]{:S(2)}, u32[]{:S(2)}) %collective-permute-start) | collective-permute-done | bytes 589856 | tf_op jit(solution)/shard_map/ppermute | solution.py:259
  40.0 20.7 %collective-permute-done.3.refs_0_ = bf16[384,768]{1,0:T(8,128)(2,1)S(1)} collective-permute-done((bf16[384,768]{1,0:T(8,128)(2,1)}, bf16[384,768]{1,0:T(8,128)(2,1)S(1)}, u32[]{:S(2)}, u32[]{:S(2)}) %collective-permute-start.3) | collective-permute-done | bytes 589856 | tf_op jit(solution)/shard_map/ppermute | solution.py:259
  61.9 7.8 %collective-permute-done.6.refs_3_ = bf16[768,384]{1,0:T(8,128)(2,1)S(1)} collective-permute-done((bf16[768,384]{1,0:T(8,128)(2,1)S(1)}, bf16[768,384]{1,0:T(8,128)(2,1)S(1)}, u32[]{:S(2)}, u32[]{:S(2)}) %collective-permute-start.6) | collective-permute-done | bytes 589856 | tf_op jit(solution)/shard_map/ppermute | solution.py:259
  77.2 6.4 %collective-permute-done.14.p1 = bf16[64,3072]{1,0:T(8,128)(2,1)S(1)} collective-permute-done((bf16[64,3072]{1,0:T(8,128)(2,1)S(1)}, bf16[64,3072]{1,0:T(8,128)(2,1)S(1)}, u32[]{:S(2)}, u32[]{:S(2)}) %collective-permute-start.14) | collective-permute-done | bytes 393248 | tf_op jit(solution)/shard_map/ppermute | solution.py:259
  83.6 15.1 %collective-permute-done.8.refs_2_ = bf16[768,384]{1,0:T(8,128)(2,1)S(1)} collective-permute-done((bf16[768,384]{1,0:T(8,128)(2,1)S(1)}, bf16[768,384]{1,0:T(8,128)(2,1)S(1)}, u32[]{:S(2)}, u32[]{:S(2)}) %collective-permute-start.8) | collective-permute-done | bytes 589856 | tf_op jit(solution)/shard_map/ppermute | solution.py:259
  103.3 5.3 %pre.1 = (f32[512,768]{1,0:T(8,128)S(1)}, bf16[512,768]{1,0:T(8,128)(2,1)S(1)}) custom-call(s32[4]{0:T(128)S(1)} %pad_add_fusion.s, bf16[256,3072]{1,0:T(8,128)(2,1)S(1)} %get-tuple-element.106.rows_ref, bf16[64,3072]{1,0:T(8,128)(2,1)S(1)} %collective-permute-done.13.p0, bf16[64,3072]{1,0:T(8,128)(2,1)S(1)} %collective-permute-done.14.p1, ...), custom_call_target="tpu_custom_call" | custom-call | flops 2415919104 | bytes 10223632 | tf_op jit(solution)/shard_map/pre/pallas_call | solution.py:225
  108.6 6.7 %collective-permute-done.10.refs_0_ = bf16[768,384]{1,0:T(8,128)(2,1)S(1)} collective-permute-done((bf16[768,384]{1,0:T(8,128)(2,1)S(1)}, bf16[768,384]{1,0:T(8,128)(2,1)S(1)}, u32[]{:S(2)}, u32[]{:S(2)}) %collective-permute-start.10) | collective-permute-done | bytes 589856 | tf_op jit(solution)/shard_map/ppermute | solution.py:259
  121.5 9.8 %collective-permute-done.19 = bf16[2,2,64,384]{3,2,0,1:T(8,128)(2,1)S(1)} collective-permute-done((bf16[2,2,64,384]{3,2,0,1:T(8,128)(2,1)S(1)}, bf16[2,2,64,384]{3,2,0,1:T(8,128)(2,1)S(1)}, u32[]{:S(2)}, u32[]{:S(2)}) %collective-permute-start.19) | collective-permute-done | bytes 196640 | tf_op jit(solution)/shard_map/ppermute | solution.py:259
  141.3 4.0 %collective-permute-done.22.right_ref = bf16[64,1536]{1,0:T(8,128)(2,1)S(1)} collective-permute-done((bf16[64,1536]{1,0:T(8,128)(2,1)S(1)}, bf16[64,1536]{1,0:T(8,128)(2,1)S(1)}, u32[]{:S(2)}, u32[]{:S(2)}) %collective-permute-start.22) | collective-permute-done | bytes 196640 | tf_op jit(solution)/shard_map/ppermute | solution.py:259
  156.0 5.0 %collective-permute-done.23.refs_2_ = bf16[64,1536]{1,0:T(8,128)(2,1)S(1)} collective-permute-done((bf16[64,1536]{1,0:T(8,128)(2,1)S(1)}, bf16[64,1536]{1,0:T(8,128)(2,1)S(1)}, u32[]{:S(2)}, u32[]{:S(2)}) %collective-permute-start.23) | collective-permute-done | bytes 196640 | tf_op jit(solution)/shard_map/ppermute | solution.py:259
  161.0 4.1 %collective-permute-done.27.refs_5_ = bf16[64,1536]{1,0:T(8,128)(2,1)S(1)} collective-permute-done((bf16[64,1536]{1,0:T(8,128)(2,1)S(1)}, bf16[64,1536]{1,0:T(8,128)(2,1)S(1)}, u32[]{:S(2)}, u32[]{:S(2)}) %collective-permute-start.27) | collective-permute-done | bytes 196640 | tf_op jit(solution)/shard_map/ppermute | solution.py:259
  171.2 6.7 %collective-permute-done.30.n1 = bf16[64,3072]{1,0:T(8,128)(2,1)S(1)} collective-permute-done((bf16[64,3072]{1,0:T(8,128)(2,1)S(1)}, bf16[64,3072]{1,0:T(8,128)(2,1)S(1)}, u32[]{:S(2)}, u32[]{:S(2)}) %collective-permute-start.30) | collective-permute-done | bytes 393248 | tf_op jit(solution)/shard_map/ppermute | solution.py:259
  182.6 8.2 %score_hidden.1 = (bf16[256,1536]{1,0:T(8,128)(2,1)S(1)}, bf16[256,1536]{1,0:T(8,128)(2,1)S(1)}) custom-call(bf16[256,3072]{1,0:T(8,128)(2,1)S(1)} %get-tuple-element.141.t_in, bf16[256,3072]{1,0:T(8,128)(2,1)S(1)} %get-tuple-element.142.c_in, bf16[3072,1536]{1,0:T(8,128)(2,1)S(1)} %bitcast.90, bf16[3072,1536]{1,0:T(8,128)(2,1)S(1)} %bitcast.92), custom_call_target="tpu_custom_call" | custom-call | flops 4831838208 | bytes 18874368 | tf_op jit(solution)/shard_map/score_hidden/pallas_call | solution.py:561
  194.9 10.3 %score_gap.1 = (f32[128,3072]{1,0:T(8,128)S(1)}, bf16[128,3072]{1,0:T(8,128)(2,1)S(1)}) custom-call(s32[4]{0:T(128)S(1)} %pad_add_fusion.s, bf16[256,1536]{1,0:T(8,128)(2,1)S(1)} %get-tuple-element.146.t_h, bf16[256,1536]{1,0:T(8,128)(2,1)S(1)} %get-tuple-element.147.c_h, bf16[1536,3072]{1,0:T(8,128)(2,1)S(1)} %bitcast.86, bf16[1536,3072]{1,0:T(8,128)(2,1)S(1)} %bitcast.88, ...), custom_call_target="tpu_custom_call" | custom-call | flops 4831838208 | bytes 18874368 | tf_op jit(solution)/shard_map/score_gap/pallas_call | solution.py:592
  209.0 10.1 %collective-permute-done.40.got_ref = bf16[64,3072]{1,0:T(8,128)(2,1)S(1)} collective-permute-done((bf16[64,3072]{1,0:T(8,128)(2,1)S(1)}, bf16[64,3072]{1,0:T(8,128)(2,1)S(1)}, u32[]{:S(2)}, u32[]{:S(2)}) %collective-permute-start.40) | collective-permute-done | bytes 393248 | tf_op jit(solution)/shard_map/ppermute | solution.py:259
  219.8 7.3 %collective-permute-done.41.refs_2_ = bf16[512,768]{1,0:T(8,128)(2,1)S(1)} collective-permute-done((bf16[512,768]{1,0:T(8,128)(2,1)S(1)}, bf16[512,768]{1,0:T(8,128)(2,1)S(1)}, u32[]{:S(2)}, u32[]{:S(2)}) %collective-permute-start.41) | collective-permute-done | bytes 786464 | tf_op jit(solution)/shard_map/ppermute | solution.py:271
  232.1 7.8 %collective-permute-done.45.refs_2_ = bf16[1,4,64,384]{3,2,1,0:T(8,128)(2,1)S(1)} collective-permute-done((bf16[1,4,64,384]{3,2,1,0:T(8,128)(2,1)S(1)}, bf16[1,4,64,384]{3,2,1,0:T(8,128)(2,1)S(1)}, u32[]{:S(2)}, u32[]{:S(2)}) %collective-permute-start.45) | collective-permute-done | bytes 196640 | tf_op jit(solution)/shard_map/ppermute | solution.py:259
  245.2 3.5 %collective-permute-done.49 = bf16[2,2,64,384]{3,2,0,1:T(8,128)(2,1)S(1)} collective-permute-done((bf16[2,2,64,384]{3,2,0,1:T(8,128)(2,1)S(1)}, bf16[2,2,64,384]{3,2,0,1:T(8,128)(2,1)S(1)}, u32[]{:S(2)}, u32[]{:S(2)}) %collective-permute-start.49) | collective-permute-done | bytes 196640 | tf_op jit(solution)/shard_map/ppermute | solution.py:259
  253.9 4.1 %rows_grad.1.refs_0_ = bf16[512,768]{1,0:T(8,128)(2,1)S(1)} custom-call(bf16[64,3072]{1,0:T(8,128)(2,1)S(1)} %get-tuple-element.159.refs_0_, bf16[64,3072]{1,0:T(8,128)(2,1)S(1)} %get-tuple-element.161.refs_1_, bf16[64,3072]{1,0:T(8,128)(2,1)S(1)} %collective-permute-done.46.refs_2_, bf16[64,3072]{1,0:T(8,128)(2,1)S(1)} %collective-permute-done.47.refs_3_, ...), custom_call_target="tpu_custom_call" | custom-call | flops 2415919104 | bytes 10000000 | tf_op jit(solution)/shard_map/rows_grad/pallas_call | solution.py:681
  263.0 17.5 %collective-permute-done.54.refs_0_ = bf16[512,768]{1,0:T(8,128)(2,1)} collective-permute-done((bf16[512,768]{1,0:T(8,128)(2,1)S(1)}, bf16[512,768]{1,0:T(8,128)(2,1)}, u32[]{:S(2)}, u32[]{:S(2)}) %collective-permute-start.54) | collective-permute-done | bytes 786464 | tf_op jit(solution)/shard_map/ppermute | solution.py:271
  284.8 5.6 %collective-permute-done.58.refs_3_ = bf16[8,64,384]{2,1,0:T(8,128)(2,1)S(1)} collective-permute-done((bf16[8,64,384]{2,1,0:T(8,128)(2,1)S(1)}, bf16[8,64,384]{2,1,0:T(8,128)(2,1)S(1)}, u32[]{:S(2)}, u32[]{:S(2)}) %collective-permute-start.58) | collective-permute-done | bytes 393248 | tf_op jit(solution)/shard_map/ppermute | solution.py:259
  292.1 9.3 %collective-permute-done.56.refs_0_ = bf16[512,768]{1,0:T(8,128)(2,1)} collective-permute-done((bf16[512,768]{1,0:T(8,128)(2,1)}, bf16[512,768]{1,0:T(8,128)(2,1)}, u32[]{:S(2)}, u32[]{:S(2)}) %collective-permute-start.56) | collective-permute-done | bytes 786464 | tf_op jit(solution)/shard_map/ppermute | solution.py:271
  312.5 8.1 %collective-permute-done.61.refs_0_ = bf16[512,768]{1,0:T(8,128)(2,1)S(1)} collective-permute-done((bf16[512,768]{1,0:T(8,128)(2,1)}, bf16[512,768]{1,0:T(8,128)(2,1)S(1)}, u32[]{:S(2)}, u32[]{:S(2)}) %collective-permute-start.61) | collective-permute-done | bytes 786464 | tf_op jit(solution)/shard_map/ppermute | solution.py:271
  329.8 6.6 %collective-permute-done.64 = bf16[256,768]{1,0:T(8,128)(2,1)S(1)} collective-permute-done((bf16[256,768]{1,0:T(8,128)(2,1)S(1)}, bf16[256,768]{1,0:T(8,128)(2,1)S(1)}, u32[]{:S(2)}, u32[]{:S(2)}) %collective-permute-start.64) | collective-permute-done | bytes 393248 | tf_op jit(solution)/shard_map/ppermute | solution.py:271
  (249 shorter events, 129.9 us)
Async XLA Ops:
  3.1 29.2 %collective-permute-start = (bf16[384,768]{1,0:T(8,128)(2,1)}, bf16[384,768]{1,0:T(8,128)(2,1)}, u32[]{:S(2)}, u32[]{:S(2)}) collective-permute-start(bf16[384,768]{1,0:T(8,128)(2,1)} %get-tuple-element.190), channel_id=1, source_target_pairs={{0,8},{4,12},{8,0},{12,4},{16,24},{20,28},{24,16},{28,20},{1,9},{5... | collective-permute-start | bytes 1769480 | tf_op jit(solution)/shard_map/ppermute | solution.py:259
  6.2 28.7 %collective-permute-start.1 = (bf16[384,768]{1,0:T(8,128)(2,1)}, bf16[384,768]{1,0:T(8,128)(2,1)}, u32[]{:S(2)}, u32[]{:S(2)}) collective-permute-start(bf16[384,768]{1,0:T(8,128)(2,1)} %get-tuple-element.189.refs_0_), channel_id=1, source_target_pairs={{0,16},{4,20},{8,24},{12,28},{16,0},{20,4},{24,8},{28,12},{1,17},{... | collective-permute-start | bytes 1769480 | tf_op jit(solution)/shard_map/ppermute | solution.py:259
  8.8 26.1 %collective-permute-start.2 = (bf16[384,768]{1,0:T(8,128)(2,1)}, bf16[384,768]{1,0:T(8,128)(2,1)}, u32[]{:S(2)}, u32[]{:S(2)}) collective-permute-start(bf16[384,768]{1,0:T(8,128)(2,1)} %get-tuple-element.189.refs_0_), channel_id=1, source_target_pairs={{0,4},{4,0},{8,12},{12,8},{16,20},{20,16},{24,28},{28,24},{1,5},{5... | collective-permute-start | bytes 1769480 | tf_op jit(solution)/shard_map/ppermute | solution.py:259
  34.9 25.9 %collective-permute-start.3 = (bf16[384,768]{1,0:T(8,128)(2,1)}, bf16[384,768]{1,0:T(8,128)(2,1)S(1)}, u32[]{:S(2)}, u32[]{:S(2)}) collective-permute-start(bf16[384,768]{1,0:T(8,128)(2,1)} %get-tuple-element.97.refs_2_), channel_id=1, source_target_pairs={{0,16},{4,20},{8,24},{12,28},{16,0},{20,4},{24,8},{28,12},{1,17},{... | collective-permute-start | bytes 1769480 | tf_op jit(solution)/shard_map/ppermute | solution.py:259
  35.2 25.6 %collective-permute-start.4 = (bf16[384,768]{1,0:T(8,128)(2,1)}, bf16[384,768]{1,0:T(8,128)(2,1)S(1)}, u32[]{:S(2)}, u32[]{:S(2)}) collective-permute-start(bf16[384,768]{1,0:T(8,128)(2,1)} %get-tuple-element.97.refs_2_), channel_id=1, source_target_pairs={{0,4},{4,0},{8,12},{12,8},{16,20},{20,16},{24,28},{28,24},{1,5},{5... | collective-permute-start | bytes 1769480 | tf_op jit(solution)/shard_map/ppermute | solution.py:259
  36.7 25.2 %collective-permute-start.5 = (bf16[384,768]{1,0:T(8,128)(2,1)}, bf16[384,768]{1,0:T(8,128)(2,1)S(1)}, u32[]{:S(2)}, u32[]{:S(2)}) collective-permute-start(bf16[384,768]{1,0:T(8,128)(2,1)} %get-tuple-element.98.refs_4_), channel_id=1, source_target_pairs={{0,4},{4,0},{8,12},{12,8},{16,20},{20,16},{24,28},{28,24},{1,5},{5... | collective-permute-start | bytes 1769480 | tf_op jit(solution)/shard_map/ppermute | solution.py:259
  37.2 32.5 %collective-permute-start.6 = (bf16[768,384]{1,0:T(8,128)(2,1)S(1)}, bf16[768,384]{1,0:T(8,128)(2,1)S(1)}, u32[]{:S(2)}, u32[]{:S(2)}) collective-permute-start(bf16[768,384]{1,0:T(8,128)(2,1)S(1)} %get-tuple-element.99), channel_id=1, source_target_pairs={{0,8},{4,12},{8,0},{12,4},{16,24},{20,28},{24,16},{28,20},{1,9},{5... | collective-permute-start | bytes 1769480 | tf_op jit(solution)/shard_map/ppermute | solution.py:259
  40.0 35.9 %collective-permute-start.13 = (bf16[64,3072]{1,0:T(8,128)(2,1)S(1)}, bf16[64,3072]{1,0:T(8,128)(2,1)S(1)}, u32[]{:S(2)}, u32[]{:S(2)}) collective-permute-start(bf16[64,3072]{1,0:T(8,128)(2,1)S(1)} %slice.57), channel_id=1, source_target_pairs={{0,8},{4,12},{8,0},{12,4},{16,24},{20,28},{24,16},{28,20},{1,9},{5... | collective-permute-start | bytes 1179656 | tf_op jit(solution)/shard_map/ppermute | solution.py:259
  72.4 26.3 %collective-permute-start.8 = (bf16[768,384]{1,0:T(8,128)(2,1)S(1)}, bf16[768,384]{1,0:T(8,128)(2,1)S(1)}, u32[]{:S(2)}, u32[]{:S(2)}) collective-permute-start(bf16[768,384]{1,0:T(8,128)(2,1)S(1)} %get-tuple-element.102.refs_0_.refs_8_), channel_id=1, source_target_pairs={{0,16},{4,20},{8,24},{12,28},{16,0},{20,4},{24,8},{28,12},{1,17},{... | collective-permute-start | bytes 1769480 | tf_op jit(solution)/shard_map/ppermute | solution.py:259
  72.8 25.9 %collective-permute-start.9 = (bf16[768,384]{1,0:T(8,128)(2,1)S(1)}, bf16[768,384]{1,0:T(8,128)(2,1)S(1)}, u32[]{:S(2)}, u32[]{:S(2)}) collective-permute-start(bf16[768,384]{1,0:T(8,128)(2,1)S(1)} %get-tuple-element.102.refs_0_.refs_8_), channel_id=1, source_target_pairs={{0,4},{4,0},{8,12},{12,8},{16,20},{20,16},{24,28},{28,24},{1,5},{5... | collective-permute-start | bytes 1769480 | tf_op jit(solution)/shard_map/ppermute | solution.py:259
  77.2 23.6 %collective-permute-start.15 = (bf16[64,3072]{1,0:T(8,128)(2,1)S(1)}, bf16[64,3072]{1,0:T(8,128)(2,1)S(1)}, u32[]{:S(2)}, u32[]{:S(2)}) collective-permute-start(bf16[64,3072]{1,0:T(8,128)(2,1)S(1)} %collective-permute-done.13.p0), channel_id=1, source_target_pairs={{0,1},{1,0},{2,3},{3,2},{4,5},{5,4},{6,7},{7,6},{8,9},{9,8},{10,11... | collective-permute-start | bytes 1179656 | tf_op jit(solution)/shard_map/ppermute | solution.py:259
  134.9 31.8 %collective-permute-start.28 = (bf16[512,768]{1,0:T(8,128)(2,1)S(1)}, bf16[512,768]{1,0:T(8,128)(2,1)S(1)}, u32[]{:S(2)}, u32[]{:S(2)}) collective-permute-start(bf16[512,768]{1,0:T(8,128)(2,1)S(1)} %get-tuple-element.128.hidden_ref), channel_id=1, source_target_pairs={{0,8},{4,12},{8,16},{12,20},{16,24},{20,28},{24,0},{28,4},{1,9},{5... | collective-permute-start | bytes 2359304 | tf_op jit(solution)/shard_map/ppermute | solution.py:271
  137.1 29.7 %collective-permute-start.29 = (bf16[512,768]{1,0:T(8,128)(2,1)S(1)}, bf16[512,768]{1,0:T(8,128)(2,1)S(1)}, u32[]{:S(2)}, u32[]{:S(2)}) collective-permute-start(bf16[512,768]{1,0:T(8,128)(2,1)S(1)} %get-tuple-element.128.hidden_ref), channel_id=1, source_target_pairs={{0,4},{4,0},{8,12},{12,8},{16,20},{20,16},{24,28},{28,24},{1,5},{5... | collective-permute-start | bytes 2359304 | tf_op jit(solution)/shard_map/ppermute | solution.py:259
  169.3 24.2 %collective-permute-start.33 = (bf16[512,768]{1,0:T(8,128)(2,1)S(1)}, bf16[512,768]{1,0:T(8,128)(2,1)S(1)}, u32[]{:S(2)}, u32[]{:S(2)}) collective-permute-start(bf16[512,768]{1,0:T(8,128)(2,1)S(1)} %get-tuple-element.144), channel_id=1, source_target_pairs={{0,8},{4,12},{8,16},{12,20},{16,24},{20,28},{24,0},{28,4},{1,9},{5... | collective-permute-start | bytes 2359304 | tf_op jit(solution)/shard_map/ppermute | solution.py:271
  169.5 24.0 %collective-permute-start.34 = (bf16[512,768]{1,0:T(8,128)(2,1)S(1)}, bf16[512,768]{1,0:T(8,128)(2,1)S(1)}, u32[]{:S(2)}, u32[]{:S(2)}) collective-permute-start(bf16[512,768]{1,0:T(8,128)(2,1)S(1)} %get-tuple-element.144), channel_id=1, source_target_pairs={{0,4},{4,0},{8,12},{12,8},{16,20},{20,16},{24,28},{28,24},{1,5},{5... | collective-permute-start | bytes 2359304 | tf_op jit(solution)/shard_map/ppermute | solution.py:259
  205.3 21.7 %collective-permute-start.41 = (bf16[512,768]{1,0:T(8,128)(2,1)S(1)}, bf16[512,768]{1,0:T(8,128)(2,1)S(1)}, u32[]{:S(2)}, u32[]{:S(2)}) collective-permute-start(bf16[512,768]{1,0:T(8,128)(2,1)S(1)} %get-tuple-element.158), channel_id=1, source_target_pairs={{0,8},{4,12},{8,16},{12,20},{16,24},{20,28},{24,0},{28,4},{1,9},{5... | collective-permute-start | bytes 2359304 | tf_op jit(solution)/shard_map/ppermute | solution.py:271
  206.2 20.8 %collective-permute-start.42 = (bf16[512,768]{1,0:T(8,128)(2,1)S(1)}, bf16[512,768]{1,0:T(8,128)(2,1)S(1)}, u32[]{:S(2)}, u32[]{:S(2)}) collective-permute-start(bf16[512,768]{1,0:T(8,128)(2,1)S(1)} %get-tuple-element.158), channel_id=1, source_target_pairs={{0,4},{4,0},{8,12},{12,8},{16,20},{20,16},{24,28},{28,24},{1,5},{5... | collective-permute-start | bytes 2359304 | tf_op jit(solution)/shard_map/ppermute | solution.py:259
  228.0 23.8 %collective-permute-start.50 = (bf16[512,768]{1,0:T(8,128)(2,1)S(1)}, bf16[512,768]{1,0:T(8,128)(2,1)S(1)}, u32[]{:S(2)}, u32[]{:S(2)}) collective-permute-start(bf16[512,768]{1,0:T(8,128)(2,1)S(1)} %get-tuple-element.164), channel_id=1, source_target_pairs={{0,4},{4,0},{8,12},{12,8},{16,20},{20,16},{24,28},{28,24},{1,5},{5... | collective-permute-start | bytes 2359304 | tf_op jit(solution)/shard_map/ppermute | solution.py:259
  259.4 21.1 %collective-permute-start.54 = (bf16[512,768]{1,0:T(8,128)(2,1)S(1)}, bf16[512,768]{1,0:T(8,128)(2,1)}, u32[]{:S(2)}, u32[]{:S(2)}) collective-permute-start(bf16[512,768]{1,0:T(8,128)(2,1)S(1)} %get-tuple-element.168), channel_id=1, source_target_pairs={{0,8},{4,12},{8,16},{12,20},{16,24},{20,28},{24,0},{28,4},{1,9},{5... | collective-permute-start | bytes 2359304 | tf_op jit(solution)/shard_map/ppermute | solution.py:271
  260.7 19.7 %collective-permute-start.55 = (bf16[512,768]{1,0:T(8,128)(2,1)S(1)}, bf16[512,768]{1,0:T(8,128)(2,1)S(1)}, u32[]{:S(2)}, u32[]{:S(2)}) collective-permute-start(bf16[512,768]{1,0:T(8,128)(2,1)S(1)} %get-tuple-element.168), channel_id=1, source_target_pairs={{0,4},{4,0},{8,12},{12,8},{16,20},{20,16},{24,28},{28,24},{1,5},{5... | collective-permute-start | bytes 2359304 | tf_op jit(solution)/shard_map/ppermute | solution.py:259
  262.5 20.6 %collective-permute-start.37 = (bf16[8,64,384]{2,1,0:T(8,128)(2,1)S(1)}, bf16[8,64,384]{2,1,0:T(8,128)(2,1)}, u32[]{:S(2)}, u32[]{:S(2)}) collective-permute-start(bf16[8,64,384]{2,1,0:T(8,128)(2,1)S(1)} %get-tuple-element.150.refs_0_), channel_id=1, source_target_pairs={{0,1},{1,0},{2,3},{3,2},{4,5},{5,4},{6,7},{7,6},{8,9},{9,8},{10,11... | collective-permute-start | bytes 1179656 | tf_op jit(solution)/shard_map/ppermute | solution.py:259
  262.5 20.6 %collective-permute-start.38 = (bf16[8,64,384]{2,1,0:T(8,128)(2,1)}, bf16[8,64,384]{2,1,0:T(8,128)(2,1)}, u32[]{:S(2)}, u32[]{:S(2)}) collective-permute-start(bf16[8,64,384]{2,1,0:T(8,128)(2,1)} %get-tuple-element.151.refs_1_), channel_id=1, source_target_pairs={{0,1},{1,0},{2,3},{3,2},{4,5},{5,4},{6,7},{7,6},{8,9},{9,8},{10,11... | collective-permute-start | bytes 1179656 | tf_op jit(solution)/shard_map/ppermute | solution.py:259
  281.4 20.1 %collective-permute-start.56 = (bf16[512,768]{1,0:T(8,128)(2,1)}, bf16[512,768]{1,0:T(8,128)(2,1)}, u32[]{:S(2)}, u32[]{:S(2)}) collective-permute-start(bf16[512,768]{1,0:T(8,128)(2,1)} %get-tuple-element.170), channel_id=1, source_target_pairs={{0,8},{4,12},{8,16},{12,20},{16,24},{20,28},{24,0},{28,4},{1,9},{5... | collective-permute-start | bytes 2359304 | tf_op jit(solution)/shard_map/ppermute | solution.py:271
  281.4 20.1 %collective-permute-start.57 = (bf16[512,768]{1,0:T(8,128)(2,1)}, bf16[512,768]{1,0:T(8,128)(2,1)}, u32[]{:S(2)}, u32[]{:S(2)}) collective-permute-start(bf16[512,768]{1,0:T(8,128)(2,1)} %get-tuple-element.170), channel_id=1, source_target_pairs={{0,4},{4,0},{8,12},{12,8},{16,20},{20,16},{24,28},{28,24},{1,5},{5... | collective-permute-start | bytes 2359304 | tf_op jit(solution)/shard_map/ppermute | solution.py:259
  (74 other events, 877.1 us)
